TPU v7x, 32 devices: a whole 2x2x4 slice. The times are simulated.
32 devices in a mesh: seq: 8 (over z, y), head: 4 (over x, core).
Axes of the slice: x: 2, y: 2, z: 4, core: 2. Of those that a mesh axis runs over, the one named last changes fastest.
Arguments:
- tokens: bfloat16 [8, 4096, 1024], P(None, 'seq'), may hold values from -6 to 6
- doc_ids: int32 [8, 4096], replicated, may hold values from 0 to 8, as said below
- norm_gain: float32 [1024], replicated, may hold values from 0.5 to 1.5
- head_input_weight: bfloat16 [1024, 2, 2048], P(None, None, 'head'), may hold values from -0.1875 to 0.1875
- state_input_weight: bfloat16 [1024, 256], replicated, may hold values from -0.1875 to 0.1875
- timestep_input_weight: bfloat16 [1024, 32], P(None, 'head'), may hold values from -0.1875 to 0.1875
- conv_x: float32 [5, 2048], P(None, 'head'), may hold values from -3 to 3
- conv_state: float32 [5, 256], replicated, may hold values from -3 to 3
- head_params: float32 [3, 32], P(None, 'head'), as said below
- gated_gain: float32 [2048], P('head'), may hold values from 0.5 to 1.5
- output_weight: bfloat16 [2048, 1024], P('head'), may hold values from -0.125 to 0.125
- cotangent: bfloat16 [8, 4096, 1024], P(None, 'seq'), may hold values from -6 to 6
Outputs:
- output: bfloat16 [8, 4096, 1024], P(None, 'seq')
- input_grad: bfloat16 [8, 4096, 1024], P(None, 'seq')
- norm_gain_grad: float32 [1024], replicated
- in_heads_grad: float32 [1024, 2, 2048], P('seq', None, 'head')
- in_state_grad: float32 [1024, 256], P('seq')
- in_dt_grad: float32 [1024, 32], P(None, 'head')
- conv_x_grad: float32 [5, 2048], P(None, 'head')
- conv_state_grad: float32 [5, 256], replicated
- head_params_grad: float32 [3, 32], P(None, 'head')
- gated_gain_grad: float32 [2048], P('head')
- out_proj_grad: float32 [2048, 1024], P('head', 'seq')
Inputs may be any that keep to these rules, and one draw needn't show every extreme that they name: `doc_ids`: never falls along a sequence and starts at 0 in every sequence; one sequence, chosen by the draw, is a single document. `head_params`: row 0 is the time-step bias, row 1 the logarithm of the decay rate, row 2 the skip coefficient.
All inputs are finite; a program needn't handle non-finite values.
Results may differ from a plain program's by a relative error of at most 0.012.
The roundings to bfloat16 on the way count: a program that leaves them out, or rounds other values in their place, can miss the bound.
Values may be sent and summed in bfloat16 or wider, within the bound.
No kernel may reach another device: no remote copies, remote signals or barrier semaphores. Data moves between devices by JAX's collectives and lax.ppermute only.
A program may use at most 640 MiB of HBM per device.

v0:
```python
import jax
import jax.numpy as jnp
from jax import lax
from jax.sharding import PartitionSpec as P

BLOCK = 256


epsilon = 1e-05
accurate = lax.Precision.HIGH


def shifted(value, axis, steps):
    count = lax.axis_size(axis)
    leading, last = (max(0, -steps), min(count, count - steps))
    return lax.ppermute(value, axis, [(source, source + steps) for source in range(leading, last)])


def rounded(value):
    return lax.optimization_barrier(value.astype(jnp.bfloat16)).astype(jnp.float32)


def causal_conv(padded, padded_ids, weights):
    width = weights.shape[0] - 1
    length = padded.shape[1] - width + 1
    current = padded_ids[:, width - 1 :]
    total = jnp.zeros((padded.shape[0], length, padded.shape[2]), jnp.float32) + weights[width]
    for offset in range(width):
        same_doc = (padded_ids[:, offset : offset + length] == current).astype(jnp.float32)
        total = total + weights[offset] * padded[:, offset : offset + length] * same_doc[:, :, None]
    return jax.nn.silu(total)


def block_pass(carry, block):
    state, prev_ids = carry
    x_heads, b_proj, c_proj, step_sizes, log_decay, block_ids = block
    length = x_heads.shape[1]
    cumulated = jnp.cumsum(log_decay, axis=1)
    later = lax.broadcasted_iota(jnp.int32, (length, length), 0) >= lax.broadcasted_iota(
        jnp.int32, (length, length), 1
    )
    same_doc = (block_ids[:, :, None] == block_ids[:, None, :]) & later[None]
    by_head = jnp.transpose(cumulated, (0, 2, 1))
    spread = jnp.minimum(by_head[:, :, :, None] - by_head[:, :, None, :], 0.0)
    decays = jnp.where(same_doc[:, None], jnp.exp(spread), 0.0)
    scores = jnp.einsum("sin,sjn->sij", c_proj, b_proj, precision=accurate)
    mixing = scores[:, None] * decays * jnp.transpose(step_sizes, (0, 2, 1))[:, :, None, :]
    inside = jnp.einsum("shij,sjhp->sihp", mixing, x_heads, precision=accurate)
    carried = (block_ids == prev_ids[:, None]).astype(jnp.float32)[:, :, None] * jnp.exp(cumulated)
    outside = jnp.einsum("sin,shnp->sihp", c_proj, state, precision=accurate) * carried[..., None]
    last_doc = (block_ids == block_ids[:, -1:]).astype(jnp.float32)
    tail = jnp.exp(cumulated[:, -1:, :] - cumulated) * last_doc[:, :, None]
    survive = (
        jnp.exp(cumulated[:, -1, :]) * (block_ids[:, -1] == prev_ids).astype(jnp.float32)[:, None]
    )
    fresh = jnp.einsum(
        "sjn,sjhp->shnp", b_proj, x_heads * (tail * step_sizes)[..., None], precision=accurate
    )
    new_state = state * survive[:, :, None, None] + fresh
    return ((new_state, block_ids[:, -1]), inside + outside)


def ssd_scan(x_heads, b_proj, c_proj, step_sizes, log_decay, seq_ids, prev_ids, state):
    count, total = seq_ids.shape
    blocks_n = total // BLOCK

    def split(value):
        return jnp.moveaxis(value.reshape((count, blocks_n, BLOCK) + value.shape[2:]), 1, 0)

    pieces = tuple(
        (split(value) for value in (x_heads, b_proj, c_proj, step_sizes, log_decay, seq_ids))
    )
    (state, prev_ids), outs = lax.scan(block_pass, (state, prev_ids), pieces)
    return (jnp.moveaxis(outs, 0, 1).reshape(x_heads.shape), state)


def range_state(x_heads, b_proj, step_sizes, log_decay, seq_ids, prev_ids):
    cumulated = jnp.cumsum(log_decay, axis=1)
    last_doc = (seq_ids == seq_ids[:, -1:]).astype(jnp.float32)
    tail = jnp.exp(cumulated[:, -1:, :] - cumulated) * last_doc[:, :, None]
    own_state = jnp.einsum(
        "sjn,sjhp->shnp", b_proj, x_heads * (tail * step_sizes)[..., None], precision=accurate
    )
    survive = (
        jnp.exp(cumulated[:, -1, :]) * (seq_ids[:, -1] == prev_ids).astype(jnp.float32)[:, None]
    )
    return (own_state, survive)


def shards(
    tokens,
    doc_ids,
    norm_gain,
    head_input_weight,
    state_input_weight,
    timestep_input_weight,
    conv_x,
    conv_state,
    head_params,
    gated_gain,
    output_weight,
    cotangent,
):
    seqs, length, width = tokens.shape
    heads = head_params.shape[1]
    inner = gated_gain.shape[0]
    head_size = inner // heads
    state_size = state_input_weight.shape[1] // 2
    taps = conv_x.shape[0] - 1
    inner_total = inner * lax.axis_size("head")
    start = lax.axis_index("seq") * length
    seq_ids = lax.dynamic_slice_in_dim(doc_ids, start, length, 1)
    lead_ids = jnp.concatenate([jnp.full((seqs, taps - 1), -1, jnp.int32), doc_ids], axis=1)
    before_ids = lax.dynamic_slice_in_dim(lead_ids, start, taps - 1, 1)
    padded_ids = jnp.concatenate([before_ids, seq_ids], axis=1)
    prev_ids = before_ids[:, -1]
    tok_float = tokens.astype(jnp.float32)
    scale = lax.rsqrt(jnp.mean(tok_float * tok_float, axis=-1, keepdims=True) + epsilon)
    normalized_rows = (tok_float * scale * norm_gain).astype(jnp.bfloat16)
    projected_rows = jnp.einsum(
        "ipr,rzm->ipzm", normalized_rows, head_input_weight, preferred_element_type=jnp.float32
    ).astype(jnp.bfloat16)
    incoming_state = jnp.einsum(
        "tfa,aw->tfw", normalized_rows, state_input_weight, preferred_element_type=jnp.float32
    ).astype(jnp.bfloat16)
    unprocessed_steps = jnp.einsum(
        "coz,zx->cox", normalized_rows, timestep_input_weight, preferred_element_type=jnp.float32
    )
    rows = jnp.concatenate([projected_rows[:, :, 1], incoming_state], axis=2)
    edge = shifted(rows[:, length - (taps - 1) :], "seq", 1)
    padded = jnp.concatenate([edge, rows], axis=1).astype(jnp.float32)
    conv_weights = jnp.concatenate([conv_x, conv_state], axis=1)
    acted, conv_pull = jax.vjp(
        lambda values, taps_w: causal_conv(values, padded_ids, taps_w), padded, conv_weights
    )
    acted = rounded(acted)
    x_heads = acted[:, :, :inner].reshape(seqs, length, heads, head_size)
    b_proj = acted[:, :, inner : inner + state_size]
    c_proj = acted[:, :, inner + state_size :]
    step_in = unprocessed_steps + head_params[0]
    step_sizes = jax.nn.softplus(step_in)
    log_decay = -step_sizes * jnp.exp(head_params[1])
    (own_state, survive), state_pull = jax.vjp(
        lambda a, b, c, d: range_state(a, b, c, d, seq_ids, prev_ids),
        x_heads,
        b_proj,
        step_sizes,
        log_decay,
    )

    def relay(turn, carried):
        return shifted(survive[:, :, None, None] * carried + own_state, "seq", 1)

    incoming = lax.fori_loop(0, lax.axis_size("seq") - 1, relay, jnp.zeros_like(own_state))

    def output_part(a, b, c, d, e, entering):
        return ssd_scan(a, b, c, d, e, seq_ids, prev_ids, entering)[0]

    mixed_ssd, ssd_pull = jax.vjp(
        output_part, x_heads, b_proj, c_proj, step_sizes, log_decay, incoming
    )
    summed = (mixed_ssd + head_params[2][:, None] * x_heads).reshape(seqs, length, inner)
    gate = projected_rows[:, :, 0].astype(jnp.float32)
    gated = summed * jax.nn.silu(gate)
    squares = lax.psum(jnp.sum(gated * gated, axis=-1, keepdims=True), "head")
    rescale = lax.rsqrt(squares / inner_total + epsilon)
    normalized_output = (gated * rescale * gated_gain).astype(jnp.bfloat16)
    partial_value = jnp.einsum(
        "tqe,ez->tqz", normalized_output, output_weight, preferred_element_type=jnp.float32
    )
    branch_path = lax.psum(partial_value, "head")
    output = (tok_float + branch_path).astype(jnp.bfloat16)
    d_normed_out = jnp.einsum(
        "zqn,an->zqa", cotangent, output_weight, preferred_element_type=jnp.float32
    )
    output_gradient = jnp.einsum(
        "gnu,gnx->ux", normalized_output, cotangent, preferred_element_type=jnp.float32
    )
    gated_gain_grad = jnp.sum(d_normed_out * gated * rescale, axis=(0, 1))
    d_scaled = d_normed_out * gated_gain
    cross = lax.psum(jnp.sum(d_scaled * gated, axis=-1, keepdims=True), "head")
    d_gated = rescale * d_scaled - gated * rescale**3 * cross / inner_total
    sigma = jax.nn.sigmoid(gate)
    d_summed = d_gated * jax.nn.silu(gate)
    d_gate = d_gated * summed * sigma * (1.0 + gate * (1.0 - sigma))
    d_heads = d_summed.reshape(seqs, length, heads, head_size)
    skip_grad = jnp.sum(d_heads * x_heads, axis=(0, 1, 3))
    y_dx, y_db, y_dc, y_ds, y_dl, pulled = ssd_pull(d_heads)

    def relay_back(turn, carried):
        return shifted(survive[:, :, None, None] * carried + pulled, "seq", -1)

    leaving = lax.fori_loop(0, lax.axis_size("seq") - 1, relay_back, jnp.zeros_like(pulled))
    d_survive = jnp.sum(leaving * incoming, axis=(2, 3))
    s_dx, s_db, s_ds, s_dl = state_pull((leaving, d_survive))
    d_x = y_dx + s_dx + head_params[2][:, None] * d_heads
    d_log = y_dl + s_dl
    decay_grad = jnp.sum(d_log * log_decay, axis=(0, 1))
    d_step = y_ds + s_ds - d_log * jnp.exp(head_params[1])
    d_raw_float = d_step * jax.nn.sigmoid(step_in)
    bias_grad = jnp.sum(d_raw_float, axis=(0, 1))
    unprocessed_gradient = d_raw_float.astype(jnp.bfloat16)
    d_bc = lax.psum(jnp.concatenate([y_db + s_db, y_dc], axis=2), "head")
    d_acted = jnp.concatenate([d_x.reshape(seqs, length, inner), d_bc], axis=2)
    d_padded, conv_grad = conv_pull(d_acted)
    returned = shifted(d_padded[:, : taps - 1].astype(jnp.bfloat16), "seq", -1).astype(jnp.float32)
    filler = jnp.zeros((seqs, length - (taps - 1), d_padded.shape[2]), jnp.float32)
    d_rows = d_padded[:, taps - 1 :] + jnp.concatenate([filler, returned], axis=1)
    projection_gradient = jnp.stack([d_gate, d_rows[:, :, :inner]], axis=2).astype(jnp.bfloat16)
    state_delta_gradient = d_rows[:, :, inner:].astype(jnp.bfloat16)
    head_rows_gradient = jnp.einsum(
        "vyr,vyph->rph", normalized_rows, projection_gradient, preferred_element_type=jnp.float32
    )
    state_gradient_rows = jnp.einsum(
        "few,fea->wa", normalized_rows, state_delta_gradient, preferred_element_type=jnp.float32
    )
    timestep_gradient = jnp.einsum(
        "uar,uav->rv", normalized_rows, unprocessed_gradient, preferred_element_type=jnp.float32
    )
    partial_gradient = jnp.einsum(
        "iafv,wfv->iaw", projection_gradient, head_input_weight, preferred_element_type=jnp.float32
    )
    partial_gradient = partial_gradient + jnp.einsum(
        "qvi,fi->qvf",
        unprocessed_gradient,
        timestep_input_weight,
        preferred_element_type=jnp.float32,
    )
    d_normed = lax.psum(partial_gradient, "head")
    d_normed = d_normed + jnp.einsum(
        "kmw,qw->kmq", state_delta_gradient, state_input_weight, preferred_element_type=jnp.float32
    )
    gain_grad = jnp.sum(d_normed * tok_float * scale, axis=(0, 1))
    d_unit = d_normed * norm_gain
    d_tokens = scale * d_unit - tok_float * scale**3 * jnp.mean(
        d_unit * tok_float, axis=-1, keepdims=True
    )
    input_grad = (cotangent.astype(jnp.float32) + d_tokens).astype(jnp.bfloat16)
    heads_total, state_total, out_total = (
        lax.psum_scatter(head_rows_gradient, "seq", scatter_dimension=0, tiled=True),
        lax.psum_scatter(state_gradient_rows, "seq", scatter_dimension=0, tiled=True),
        lax.psum_scatter(output_gradient, "seq", scatter_dimension=1, tiled=True),
    )
    params_grad = jnp.stack([bias_grad, decay_grad, skip_grad])
    small = (
        gain_grad,
        timestep_gradient,
        conv_grad[:, :inner],
        conv_grad[:, inner:],
        params_grad,
        gated_gain_grad,
    )
    gain_total, dt_total, conv_x_total, conv_state_total, params_total, gated_total = lax.psum(
        (small[0], small[1], small[2], small[3], small[4], small[5]), "seq"
    )
    return (
        output,
        input_grad,
        gain_total,
        heads_total,
        state_total,
        dt_total,
        conv_x_total,
        conv_state_total,
        params_total,
        gated_total,
        out_total,
    )


def solution(mesh):
    return jax.shard_map(
        shards,
        mesh=mesh,
        in_specs=(
            P(None, "seq", None),
            P(),
            P(),
            P(None, None, "head"),
            P(),
            P(None, "head"),
            P(None, "head"),
            P(),
            P(None, "head"),
            P("head"),
            P("head", None),
            P(None, "seq", None),
        ),
        out_specs=(
            P(None, "seq", None),
            P(None, "seq", None),
            P(),
            P("seq", None, "head"),
            P("seq", None),
            P(None, "head"),
            P(None, "head"),
            P(),
            P(None, "head"),
            P("head"),
            P("head", "seq"),
        ),
        check_vma=False,
    )
```

profile of v0, /device:TPU:0, one launch (start us, length us, event | category | flops | bytes accessed | tf_op | source)
XLA Modules:
  0.0 2522.2 jit_solution(11990556011425087448)
XLA Ops:
  17.7 12.2 fusion.156
  104.0 26.0 %multiply_convert_fusion = (bf16[8,512,768]{1,2,0:T(8,128)(2,1)S(1)}, f32[8,512,768]{1,2,0:T(8,128)}) fusion(f32[8,515,768]{1,2,0:T(8,128)} %maximum_convert_fusion, f32[768]{0:T(1024)S(1)} %copy-done.57, f32[8,512]{1,0:T(8,128)S(1)} %copy-done.45, f32[768]{0:T(1024)S(1)} %copy-done.59, f32[8,512]{1,0:T(8,128)S(1)} %copy-done.43, f32[768]{0:T(1024)S(1)} %copy-done.61, ...), kind=kLoop, calls=%fused_computation.225 | loop fusion | flops 50331648 | bytes 69270528 | tf_op jit(solution)/shard_map/convert_element_type | solution.py:20
  162.1 349.7 %while.103 = (s32[]{:T(128)}, f32[8,8,128,64]{2,3,1,0:T(8,128)S(1)}, f32[8,8]{1,0:T(8,128)S(1)}, f32[8,8,128,64]{2,3,1,0:T(8,128)}, s32[]{:T(128)}) while((s32[]{:T(128)}, f32[8,8,128,64]{2,3,1,0:T(8,128)S(1)}, f32[8,8]{1,0:T(8,128)S(1)}, f32[8,8,128,64]{2,3,1,0:T(8,128)}, s32[]{:T(128)}) %tuple.239), condition=%wide.region_4.5_spmd, body=%wide.region_3.4_spmd.sunk | while | flops 1048578 | bytes 14680421 | solution.py:154
  168.3 44.8 %collective-permute-done = f32[8,8,128,64]{2,3,1,0:T(8,128)S(1)} collective-permute-done((f32[8,8,128,64]{2,3,1,0:T(8,128)}, f32[8,8,128,64]{2,3,1,0:T(8,128)S(1)}, u32[]{:S(2)}, u32[]{:S(2)}) %collective-permute-start) | collective-permute-done | bytes 2097184 | tf_op jit(solution)/shard_map/while/body/eval_jaxpr/ppermute | solution.py:16
  220.7 43.9 %collective-permute-done = f32[8,8,128,64]{2,3,1,0:T(8,128)S(1)} collective-permute-done((f32[8,8,128,64]{2,3,1,0:T(8,128)}, f32[8,8,128,64]{2,3,1,0:T(8,128)S(1)}, u32[]{:S(2)}, u32[]{:S(2)}) %collective-permute-start) | collective-permute-done | bytes 2097184 | tf_op jit(solution)/shard_map/while/body/eval_jaxpr/ppermute | solution.py:16
  272.2 42.9 %collective-permute-done = f32[8,8,128,64]{2,3,1,0:T(8,128)S(1)} collective-permute-done((f32[8,8,128,64]{2,3,1,0:T(8,128)}, f32[8,8,128,64]{2,3,1,0:T(8,128)S(1)}, u32[]{:S(2)}, u32[]{:S(2)}) %collective-permute-start) | collective-permute-done | bytes 2097184 | tf_op jit(solution)/shard_map/while/body/eval_jaxpr/ppermute | solution.py:16
  323.7 42.0 %collective-permute-done = f32[8,8,128,64]{2,3,1,0:T(8,128)S(1)} collective-permute-done((f32[8,8,128,64]{2,3,1,0:T(8,128)}, f32[8,8,128,64]{2,3,1,0:T(8,128)S(1)}, u32[]{:S(2)}, u32[]{:S(2)}) %collective-permute-start) | collective-permute-done | bytes 2097184 | tf_op jit(solution)/shard_map/while/body/eval_jaxpr/ppermute | solution.py:16
  374.2 41.1 %collective-permute-done = f32[8,8,128,64]{2,3,1,0:T(8,128)S(1)} collective-permute-done((f32[8,8,128,64]{2,3,1,0:T(8,128)}, f32[8,8,128,64]{2,3,1,0:T(8,128)S(1)}, u32[]{:S(2)}, u32[]{:S(2)}) %collective-permute-start) | collective-permute-done | bytes 2097184 | tf_op jit(solution)/shard_map/while/body/eval_jaxpr/ppermute | solution.py:16
  423.8 40.2 %collective-permute-done = f32[8,8,128,64]{2,3,1,0:T(8,128)S(1)} collective-permute-done((f32[8,8,128,64]{2,3,1,0:T(8,128)}, f32[8,8,128,64]{2,3,1,0:T(8,128)S(1)}, u32[]{:S(2)}, u32[]{:S(2)}) %collective-permute-start) | collective-permute-done | bytes 2097184 | tf_op jit(solution)/shard_map/while/body/eval_jaxpr/ppermute | solution.py:16
  472.5 39.3 %collective-permute-done = f32[8,8,128,64]{2,3,1,0:T(8,128)S(1)} collective-permute-done((f32[8,8,128,64]{2,3,1,0:T(8,128)}, f32[8,8,128,64]{2,3,1,0:T(8,128)S(1)}, u32[]{:S(2)}, u32[]{:S(2)}) %collective-permute-start) | collective-permute-done | bytes 2097184 | tf_op jit(solution)/shard_map/while/body/eval_jaxpr/ppermute | solution.py:16
  546.0 155.9 %while.105 = (s32[]{:T(128)}, f32[8,8,128,64]{2,3,1,0:T(8,128)}, s32[8]{0:T(128)S(1)}, f32[2,8,256,8,64]{2,4,3,1,0:T(8,128)}, f32[2,8,8,256,256]{4,3,2,1,0:T(8,1...) while((s32[]{:T(128)}, f32[8,8,128,64]{2,3,1,0:T(8,128)}, ...), condition=%wide.region_8.9_spmd.clone, body=%wide.region_5.8_spmd.clone.sunk | while | flops 3691184384 | bytes 242420592 | solution.py:73
  557.8 29.0 %fusion.287 = (f32[2,8,8,256,256]{4,3,2,1,0:T(8,128)}, f32[2,8,8,256,256]{4,3,2,1,0:T(8,128)}, f32[2,8,8,256,256]{4,3,2,1,0:T(8,128)}, f32[2,8,8,256,256]{4,3,2,1,0:T(8,128)}, f32[2,8,8,256,256]{4,3,2,1,0:T(8,128)}) fusion(f32[2,8,8,256,256]{4,3,2,1,0:T(8,128)} %get-tuple-element.2554, s32[]{:T(128)} %get-tuple-element.2543, ...), kind=kLoop, calls=%fused_computation.114.clone.1 | loop fusion | flops 37748736 | bytes 86704640 | tf_op jit(solution)/shard_map/jvp()/while/body/jit(dynamic_update_index_in_dim)/dynamic_update_slice | solution.py:73
  596.9 13.1 bitcast_dynamic-update-slice_fusion.24
  635.6 29.0 %fusion.287 = (f32[2,8,8,256,256]{4,3,2,1,0:T(8,128)}, f32[2,8,8,256,256]{4,3,2,1,0:T(8,128)}, f32[2,8,8,256,256]{4,3,2,1,0:T(8,128)}, f32[2,8,8,256,256]{4,3,2,1,0:T(8,128)}, f32[2,8,8,256,256]{4,3,2,1,0:T(8,128)}) fusion(f32[2,8,8,256,256]{4,3,2,1,0:T(8,128)} %get-tuple-element.2554, s32[]{:T(128)} %get-tuple-element.2543, ...), kind=kLoop, calls=%fused_computation.114.clone.1 | loop fusion | flops 37748736 | bytes 86704640 | tf_op jit(solution)/shard_map/jvp()/while/body/jit(dynamic_update_index_in_dim)/dynamic_update_slice | solution.py:73
  674.8 13.1 bitcast_dynamic-update-slice_fusion.24
  701.9 15.4 copy.437
  750.1 13.4 multiply_reduce_fusion.4
  774.0 20.1 multiply_reduce_fusion.5
  821.6 295.1 %while.106 = (s32[]{:T(128)}, f32[8,8,128,64]{2,3,1,0:T(8,128)S(1)}, f32[2,8,256,8,64]{2,4,3,1,0:T(8,128)}, f32[2,8,256,128]{3,2,1,0:T(8,128)}, f32[2,8,256,128]...) while((s32[]{:T(128)}, f32[8,8,128,64]{2,3,1,0:T(8,128)S(1)}, ...), condition=%wide.region_25.26_spmd.clone, body=%wide.region_14.25_spmd.clone.sunk | while | flops 7308738560 | bytes 238504784 | solution.py:73
  839.8 35.7 %fusion.302 = (f32[8,8,256]{2,1,0:T(8,128)S(1)}, f32[8,256,256]{2,1,0:T(8,128)}, f32[8,8,256,256]{3,2,1,0:T(8,128)}) fusion(f32[2,8,8,256,256]{4,3,2,1,0:T(8,128)} %get-tuple-element.2701, s32[]{:T(128)S(6)} %sub.243, f32[2,8,8,256,256]{4,3,2,1,0:T(8,128)} %get-tuple-element.2698, f32[8,8,256]{2,1,0:T(8,128)S(1)} %dynamic-slice_bitcast_fusion.16, ...), kind=kOutput, calls=%fused_computation.6.clone.1 | convolution fusion | flops 1647820800 | bytes 100795904 | tf_op jit(solution)/shard_map/transpose(jvp())/while/body/eval_jaxpr/shij,sjhp->sihp/dot_general | solution.py:48
  902.4 19.8 reduce-window.75
  943.9 16.0 bitcast_dynamic-update-slice_fusion.28
  983.3 35.7 %fusion.302 = (f32[8,8,256]{2,1,0:T(8,128)S(1)}, f32[8,256,256]{2,1,0:T(8,128)}, f32[8,8,256,256]{3,2,1,0:T(8,128)}) fusion(f32[2,8,8,256,256]{4,3,2,1,0:T(8,128)} %get-tuple-element.2701, s32[]{:T(128)S(6)} %sub.243, f32[2,8,8,256,256]{4,3,2,1,0:T(8,128)} %get-tuple-element.2698, f32[8,8,256]{2,1,0:T(8,128)S(1)} %dynamic-slice_bitcast_fusion.16, ...), kind=kOutput, calls=%fused_computation.6.clone.1 | convolution fusion | flops 1647820800 | bytes 100795904 | tf_op jit(solution)/shard_map/transpose(jvp())/while/body/eval_jaxpr/shij,sjhp->sihp/dot_general | solution.py:48
  1045.9 19.8 reduce-window.75
  1087.3 16.1 bitcast_dynamic-update-slice_fusion.28
  1134.4 358.4 %while.104 = (s32[]{:T(128)}, f32[8,8,128,64]{2,3,1,0:T(8,128)}, f32[8,8]{1,0:T(8,128)S(1)}, f32[8,8,128,64]{2,3,1,0:T(8,128)S(1)}, s32[]{:T(128)}) while((s32[]{:T(128)}, f32[8,8,128,64]{2,3,1,0:T(8,128)}, f32[8,8]{1,0:T(8,128)S(1)}, f32[8,8,128,64]{2,3,1,0:T(8,128)S(1)}, s32[]{:T(128)}) %tuple.240), condition=%wide.region_27.28_spmd, body=%wide.region_26.27_spmd.sunk | while | flops 1048578 | bytes 14680421 | solution.py:193
  1139.1 49.5 %collective-permute-done.1 = f32[8,8,128,64]{2,3,1,0:T(8,128)} collective-permute-done((f32[8,8,128,64]{2,3,1,0:T(8,128)}, f32[8,8,128,64]{2,3,1,0:T(8,128)}, u32[]{:S(2)}, u32[]{:S(2)}) %collective-permute-start.1) | collective-permute-done | bytes 2097184 | tf_op jit(solution)/shard_map/while/body/eval_jaxpr/ppermute | solution.py:16
  1193.3 48.9 %collective-permute-done.1 = f32[8,8,128,64]{2,3,1,0:T(8,128)} collective-permute-done((f32[8,8,128,64]{2,3,1,0:T(8,128)}, f32[8,8,128,64]{2,3,1,0:T(8,128)}, u32[]{:S(2)}, u32[]{:S(2)}) %collective-permute-start.1) | collective-permute-done | bytes 2097184 | tf_op jit(solution)/shard_map/while/body/eval_jaxpr/ppermute | solution.py:16
  1246.8 47.3 %collective-permute-done.1 = f32[8,8,128,64]{2,3,1,0:T(8,128)} collective-permute-done((f32[8,8,128,64]{2,3,1,0:T(8,128)}, f32[8,8,128,64]{2,3,1,0:T(8,128)}, u32[]{:S(2)}, u32[]{:S(2)}) %collective-permute-start.1) | collective-permute-done | bytes 2097184 | tf_op jit(solution)/shard_map/while/body/eval_jaxpr/ppermute | solution.py:16
  1298.8 46.4 %collective-permute-done.1 = f32[8,8,128,64]{2,3,1,0:T(8,128)} collective-permute-done((f32[8,8,128,64]{2,3,1,0:T(8,128)}, f32[8,8,128,64]{2,3,1,0:T(8,128)}, u32[]{:S(2)}, u32[]{:S(2)}) %collective-permute-start.1) | collective-permute-done | bytes 2097184 | tf_op jit(solution)/shard_map/while/body/eval_jaxpr/ppermute | solution.py:16
  1349.9 45.5 %collective-permute-done.1 = f32[8,8,128,64]{2,3,1,0:T(8,128)} collective-permute-done((f32[8,8,128,64]{2,3,1,0:T(8,128)}, f32[8,8,128,64]{2,3,1,0:T(8,128)}, u32[]{:S(2)}, u32[]{:S(2)}) %collective-permute-start.1) | collective-permute-done | bytes 2097184 | tf_op jit(solution)/shard_map/while/body/eval_jaxpr/ppermute | solution.py:16
  1400.0 44.6 %collective-permute-done.1 = f32[8,8,128,64]{2,3,1,0:T(8,128)} collective-permute-done((f32[8,8,128,64]{2,3,1,0:T(8,128)}, f32[8,8,128,64]{2,3,1,0:T(8,128)}, u32[]{:S(2)}, u32[]{:S(2)}) %collective-permute-start.1) | collective-permute-done | bytes 2097184 | tf_op jit(solution)/shard_map/while/body/eval_jaxpr/ppermute | solution.py:16
  1449.2 43.7 %collective-permute-done.1 = f32[8,8,128,64]{2,3,1,0:T(8,128)} collective-permute-done((f32[8,8,128,64]{2,3,1,0:T(8,128)}, f32[8,8,128,64]{2,3,1,0:T(8,128)}, u32[]{:S(2)}, u32[]{:S(2)}) %collective-permute-start.1) | collective-permute-done | bytes 2097184 | tf_op jit(solution)/shard_map/while/body/eval_jaxpr/ppermute | solution.py:16
  1507.5 14.8 multiply_reduce_fusion.6
  1522.3 66.7 %all-reduce.20.cloned.1.call-done = f32[8,512,256]{1,2,0:T(8,128)} async-done(((f32[8,512,256]{1,2,0:T(8,128)}), f32[8,512,256]{1,2,0:T(8,128)}) %all-reduce.20.cloned.1.call-update) | async-done | bytes 4194320 | tf_op jit(solution)/shard_map/psum | solution.py:203
  1589.1 35.8 %multiply_reduce_fusion.3 = (f32[768]{0:T(1024)}, f32[768]{0:T(1024)}, f32[768]{0:T(1024)}, f32[768]{0:T(1024)}, f32[768]{0:T(1024)}, /*index=5*/f32[8,512,768]{1,2,0:T(8,128)}) fusion(f32[8,515,768]{1,2,0:T(8,128)} %maximum_convert_fusion, f32[8,512]{1,0:T(8,128)S(1)} %copy-done.46, f32[8,512]{1,0:T(8,128)S(1)} %copy-done.44, f32[8,512]{1,0:T(8,128)S(1)} %copy-done.42, ...), kind=kLoop, calls=%fused_computation.224 | loop fusion | flops 69202176 | bytes 88144896 | tf_op jit(solution)/shard_map/transpose(jvp())/reduce_sum | solution.py:30
  1624.8 21.6 broadcast_multiply_fusion.1
  1646.4 19.3 pad_add_fusion
  1695.2 16.5 fusion.165
  1723.9 40.2 %reduce-window.58 = f32[8,8,4,128]{3,1,2,0:T(8,128)S(1)} reduce-window(f32[8,8,4,128]{3,1,2,0:T(8,128)} %copy.456, f32[]{:T(128)} %constant.214.clone.1), window={size=1x1x1x128 pad=0_0x0_0x0_0x0_127}, to_apply=%region_32.33 | reduce-window | flops 4161536 | bytes 262148 | tf_op jit(solution)/shard_map/reduce-window.6
  1783.3 12.0 fusion.196
  1795.3 12.4 fusion.159
  1815.9 11.6 convolution_bitcast_fusion
  1843.8 531.7 %all-reduce.22.cloned.1.call-done = (f32[8,512,1024]{2,1,0:T(8,128)}, f32[8,512,1024]{2,1,0:T(8,128)}) async-done(((f32[8,512,1024]{2,1,0:T(8,128)}, f32[8,512,1024]{2,1,0:T(8,128)}), (f32[8,512,1024]{2,1,0:T(8,128)}, f32[8,512,1024]{2,1,0:T(8,128)})) %all-reduce.22.cloned.1.call-update) | async-done | bytes 33554448 | tf_op jit(solution)/shard_map/psum | solution.py:171
  2375.6 15.4 fusion.138
  2390.9 38.3 %all-reduce.15 = (f32[1024]{0:T(1024)}, f32[1024,8]{0,1:T(8,128)}, f32[5,512]{1,0:T(8,128)}, f32[5,256]{1,0:T(8,128)}, f32[3,8]{1,0:T(4,128)}, /*index=5*/f32[512]{0:T(512)}) all-reduce(f32[1024]{0:T(1024)S(1)} %get-tuple-element.1747, f32[1024,8]{0,1:T(8,128)S(1)} %convolution_bitcast_fusion.1, ...), channel_id=1, replica_groups=mesh['seq'=8,'head'=4] {'seq'}, use_global_device_ids=true, to_apply=%region_37.38 | all-reduce | flops 13592 | bytes 108736 | tf_op jit(solution)/shard_map/psum | solution.py:253
  2429.2 24.1 fusion.135
  2453.3 61.9 %reduce-scatter.6.cloned.1.call-done = f32[128,256]{1,0:T(8,128)} async-done(((f32[1024,256]{1,0:T(8,128)}), f32[128,256]{1,0:T(8,128)}) %reduce-scatter.6.cloned.1.call-update) | async-done | bytes 131088 | tf_op jit(solution)/shard_map/reduce_scatter | solution.py:241
  (530 shorter events, 641.0 us)
Async XLA Ops:
  7.2 742.9 %copy-start = (bf16[512,1024]{1,0:T(8,128)(2,1)S(1)}, bf16[512,1024]{1,0:T(8,128)(2,1)}, u32[]{:S(2)}) copy-start(bf16[512,1024]{1,0:T(8,128)(2,1)} %param.30) | copy-start | bytes 3145732
  7.2 1581.8 %all-reduce.20.cloned.1.call-start = ((), (), s32[]{:S(2)}) async-start(), calls=%async_computation.3 | async-start | bytes 8388608 | tf_op jit(solution)/shard_map/psum | solution.py:203
  13.1 36.7 %copy-start.48 = (f32[8,512]{1,0:T(8,128)}, f32[8,512]{1,0:T(8,128)S(1)}, u32[]{:S(2)}) copy-start(f32[8,512]{1,0:T(8,128)S(1)} %get-tuple-element.1972) | copy-start | bytes 49156
  44.1 48.0 %collective-permute-start.2 = (bf16[8,3,768]{2,0,1:T(8,128)(2,1)}, bf16[8,3,768]{2,0,1:T(8,128)(2,1)}, u32[]{:S(2)}, u32[]{:S(2)}) collective-permute-start(bf16[8,3,768]{2,0,1:T(8,128)(2,1)} %copy.427), channel_id=1, source_target_pairs={{0,4},{4,8},{8,12},{12,16},{16,20},{20,24},{24,28},{1,5},{5,9},{9,... | collective-permute-start | bytes 110600 | tf_op jit(solution)/shard_map/ppermute | solution.py:16
  63.5 24.4 copy-start.12
  64.1 21.0 copy-start.85
  87.3 67.2 %copy-start.25 = (f32[8,512,8]{1,2,0:T(8,128)}, f32[8,512,8]{1,2,0:T(8,128)S(1)}, u32[]{:S(2)}) copy-start(f32[8,512,8]{1,2,0:T(8,128)S(1)} %copy.430) | copy-start | bytes 393220
  165.3 47.7 %collective-permute-start = (f32[8,8,128,64]{2,3,1,0:T(8,128)}, f32[8,8,128,64]{2,3,1,0:T(8,128)S(1)}, u32[]{:S(2)}, u32[]{:S(2)}) collective-permute-start(f32[8,8,128,64]{2,3,1,0:T(8,128)} %multiply_add_fusion.8), channel_id=1, source_target_pairs={{0,4},{4,8},{8,12},{12,16},{16,20},{20,24},{24,28},{1,5},{5,9},{9,... | collective-permute-start | bytes 6291464 | tf_op jit(solution)/shard_map/while/body/eval_jaxpr/ppermute | solution.py:16
  216.3 48.3 %collective-permute-start = (f32[8,8,128,64]{2,3,1,0:T(8,128)}, f32[8,8,128,64]{2,3,1,0:T(8,128)S(1)}, u32[]{:S(2)}, u32[]{:S(2)}) collective-permute-start(f32[8,8,128,64]{2,3,1,0:T(8,128)} %multiply_add_fusion.8), channel_id=1, source_target_pairs={{0,4},{4,8},{8,12},{12,16},{16,20},{20,24},{24,28},{1,5},{5,9},{9,... | collective-permute-start | bytes 6291464 | tf_op jit(solution)/shard_map/while/body/eval_jaxpr/ppermute | solution.py:16
  267.8 47.4 %collective-permute-start = (f32[8,8,128,64]{2,3,1,0:T(8,128)}, f32[8,8,128,64]{2,3,1,0:T(8,128)S(1)}, u32[]{:S(2)}, u32[]{:S(2)}) collective-permute-start(f32[8,8,128,64]{2,3,1,0:T(8,128)} %multiply_add_fusion.8), channel_id=1, source_target_pairs={{0,4},{4,8},{8,12},{12,16},{16,20},{20,24},{24,28},{1,5},{5,9},{9,... | collective-permute-start | bytes 6291464 | tf_op jit(solution)/shard_map/while/body/eval_jaxpr/ppermute | solution.py:16
  318.4 47.3 %collective-permute-start = (f32[8,8,128,64]{2,3,1,0:T(8,128)}, f32[8,8,128,64]{2,3,1,0:T(8,128)S(1)}, u32[]{:S(2)}, u32[]{:S(2)}) collective-permute-start(f32[8,8,128,64]{2,3,1,0:T(8,128)} %multiply_add_fusion.8), channel_id=1, source_target_pairs={{0,4},{4,8},{8,12},{12,16},{16,20},{20,24},{24,28},{1,5},{5,9},{9,... | collective-permute-start | bytes 6291464 | tf_op jit(solution)/shard_map/while/body/eval_jaxpr/ppermute | solution.py:16
  368.9 46.4 %collective-permute-start = (f32[8,8,128,64]{2,3,1,0:T(8,128)}, f32[8,8,128,64]{2,3,1,0:T(8,128)S(1)}, u32[]{:S(2)}, u32[]{:S(2)}) collective-permute-start(f32[8,8,128,64]{2,3,1,0:T(8,128)} %multiply_add_fusion.8), channel_id=1, source_target_pairs={{0,4},{4,8},{8,12},{12,16},{16,20},{20,24},{24,28},{1,5},{5,9},{9,... | collective-permute-start | bytes 6291464 | tf_op jit(solution)/shard_map/while/body/eval_jaxpr/ppermute | solution.py:16
  418.5 45.5 %collective-permute-start = (f32[8,8,128,64]{2,3,1,0:T(8,128)}, f32[8,8,128,64]{2,3,1,0:T(8,128)S(1)}, u32[]{:S(2)}, u32[]{:S(2)}) collective-permute-start(f32[8,8,128,64]{2,3,1,0:T(8,128)} %multiply_add_fusion.8), channel_id=1, source_target_pairs={{0,4},{4,8},{8,12},{12,16},{16,20},{20,24},{24,28},{1,5},{5,9},{9,... | collective-permute-start | bytes 6291464 | tf_op jit(solution)/shard_map/while/body/eval_jaxpr/ppermute | solution.py:16
  467.2 44.6 %collective-permute-start = (f32[8,8,128,64]{2,3,1,0:T(8,128)}, f32[8,8,128,64]{2,3,1,0:T(8,128)S(1)}, u32[]{:S(2)}, u32[]{:S(2)}) collective-permute-start(f32[8,8,128,64]{2,3,1,0:T(8,128)} %multiply_add_fusion.8), channel_id=1, source_target_pairs={{0,4},{4,8},{8,12},{12,16},{16,20},{20,24},{24,28},{1,5},{5,9},{9,... | collective-permute-start | bytes 6291464 | tf_op jit(solution)/shard_map/while/body/eval_jaxpr/ppermute | solution.py:16
  557.8 34.7 %slice-start = ((s8[8388608]{0:T(1024)(128)(4,1)}), s8[4194304]{0:T(1024)(128)(4,1)S(1)}, s32[]{:S(2)}) async-start(s8[8388608]{0:T(1024)(128)(4,1)} %bitcast.645), calls=%async_computation.8 | async-start | bytes 8388608 | tf_op jit(solution)/shard_map/jvp()/while
  557.8 34.7 %slice-start.1 = ((s8[8388608]{0:T(1024)(128)(4,1)}), s8[4194304]{0:T(1024)(128)(4,1)S(1)}, s32[]{:S(2)}) async-start(s8[8388608]{0:T(1024)(128)(4,1)} %bitcast.645), calls=%async_computation.9 | async-start | bytes 8388608 | tf_op jit(solution)/shard_map/jvp()/while
  635.6 34.7 %slice-start = ((s8[8388608]{0:T(1024)(128)(4,1)}), s8[4194304]{0:T(1024)(128)(4,1)S(1)}, s32[]{:S(2)}) async-start(s8[8388608]{0:T(1024)(128)(4,1)} %bitcast.645), calls=%async_computation.8 | async-start | bytes 8388608 | tf_op jit(solution)/shard_map/jvp()/while
  635.6 34.7 %slice-start.1 = ((s8[8388608]{0:T(1024)(128)(4,1)}), s8[4194304]{0:T(1024)(128)(4,1)S(1)}, s32[]{:S(2)}) async-start(s8[8388608]{0:T(1024)(128)(4,1)} %bitcast.645), calls=%async_computation.9 | async-start | bytes 8388608 | tf_op jit(solution)/shard_map/jvp()/while
  728.8 21.4 copy-start.65
  750.1 24.0 copy-start.35
  924.1 15.4 copy-start.19
  943.9 16.0 copy-start.56
  1087.3 16.1 copy-start.56
  1134.4 358.4 %copy-start.26 = (f32[8,512,8]{1,2,0:T(8,128)S(1)}, f32[8,512,8]{1,2,0:T(8,128)}, u32[]{:S(2)}) copy-start(f32[8,512,8]{1,2,0:T(8,128)} %copy-done.25) | copy-start | bytes 393220
  1137.8 50.8 %collective-permute-start.1 = (f32[8,8,128,64]{2,3,1,0:T(8,128)}, f32[8,8,128,64]{2,3,1,0:T(8,128)}, u32[]{:S(2)}, u32[]{:S(2)}) collective-permute-start(f32[8,8,128,64]{2,3,1,0:T(8,128)} %multiply_add_fusion.9), channel_id=1, source_target_pairs={{4,0},{8,4},{12,8},{16,12},{20,16},{24,20},{28,24},{5,1},{9,5},{13... | collective-permute-start | bytes 6291464 | tf_op jit(solution)/shard_map/while/body/eval_jaxpr/ppermute | solution.py:16
  1192.0 50.2 %collective-permute-start.1 = (f32[8,8,128,64]{2,3,1,0:T(8,128)}, f32[8,8,128,64]{2,3,1,0:T(8,128)}, u32[]{:S(2)}, u32[]{:S(2)}) collective-permute-start(f32[8,8,128,64]{2,3,1,0:T(8,128)} %multiply_add_fusion.9), channel_id=1, source_target_pairs={{4,0},{8,4},{12,8},{16,12},{20,16},{24,20},{28,24},{5,1},{9,5},{13... | collective-permute-start | bytes 6291464 | tf_op jit(solution)/shard_map/while/body/eval_jaxpr/ppermute | solution.py:16
  1245.5 48.6 %collective-permute-start.1 = (f32[8,8,128,64]{2,3,1,0:T(8,128)}, f32[8,8,128,64]{2,3,1,0:T(8,128)}, u32[]{:S(2)}, u32[]{:S(2)}) collective-permute-start(f32[8,8,128,64]{2,3,1,0:T(8,128)} %multiply_add_fusion.9), channel_id=1, source_target_pairs={{4,0},{8,4},{12,8},{16,12},{20,16},{24,20},{28,24},{5,1},{9,5},{13... | collective-permute-start | bytes 6291464 | tf_op jit(solution)/shard_map/while/body/eval_jaxpr/ppermute | solution.py:16
  1297.5 47.7 %collective-permute-start.1 = (f32[8,8,128,64]{2,3,1,0:T(8,128)}, f32[8,8,128,64]{2,3,1,0:T(8,128)}, u32[]{:S(2)}, u32[]{:S(2)}) collective-permute-start(f32[8,8,128,64]{2,3,1,0:T(8,128)} %multiply_add_fusion.9), channel_id=1, source_target_pairs={{4,0},{8,4},{12,8},{16,12},{20,16},{24,20},{28,24},{5,1},{9,5},{13... | collective-permute-start | bytes 6291464 | tf_op jit(solution)/shard_map/while/body/eval_jaxpr/ppermute | solution.py:16
  1348.6 46.8 %collective-permute-start.1 = (f32[8,8,128,64]{2,3,1,0:T(8,128)}, f32[8,8,128,64]{2,3,1,0:T(8,128)}, u32[]{:S(2)}, u32[]{:S(2)}) collective-permute-start(f32[8,8,128,64]{2,3,1,0:T(8,128)} %multiply_add_fusion.9), channel_id=1, source_target_pairs={{4,0},{8,4},{12,8},{16,12},{20,16},{24,20},{28,24},{5,1},{9,5},{13... | collective-permute-start | bytes 6291464 | tf_op jit(solution)/shard_map/while/body/eval_jaxpr/ppermute | solution.py:16
  1398.7 45.9 %collective-permute-start.1 = (f32[8,8,128,64]{2,3,1,0:T(8,128)}, f32[8,8,128,64]{2,3,1,0:T(8,128)}, u32[]{:S(2)}, u32[]{:S(2)}) collective-permute-start(f32[8,8,128,64]{2,3,1,0:T(8,128)} %multiply_add_fusion.9), channel_id=1, source_target_pairs={{4,0},{8,4},{12,8},{16,12},{20,16},{24,20},{28,24},{5,1},{9,5},{13... | collective-permute-start | bytes 6291464 | tf_op jit(solution)/shard_map/while/body/eval_jaxpr/ppermute | solution.py:16
  1447.9 44.9 %collective-permute-start.1 = (f32[8,8,128,64]{2,3,1,0:T(8,128)}, f32[8,8,128,64]{2,3,1,0:T(8,128)}, u32[]{:S(2)}, u32[]{:S(2)}) collective-permute-start(f32[8,8,128,64]{2,3,1,0:T(8,128)} %multiply_add_fusion.9), channel_id=1, source_target_pairs={{4,0},{8,4},{12,8},{16,12},{20,16},{24,20},{28,24},{5,1},{9,5},{13... | collective-permute-start | bytes 6291464 | tf_op jit(solution)/shard_map/while/body/eval_jaxpr/ppermute | solution.py:16
  1502.9 338.7 %reduce-scatter.4.cloned.1.call-start = ((), (), s32[]{:S(2)}) async-start(), calls=%async_computation.4 | async-start | bytes 4718592 | tf_op jit(solution)/shard_map/reduce_scatter | solution.py:240
  1507.5 81.6 %copy-start.42 = (f32[8,512]{1,0:T(8,128)S(1)}, f32[8,512]{1,0:T(8,128)}, u32[]{:S(2)}) copy-start(f32[8,512]{1,0:T(8,128)} %get-tuple-element.1968) | copy-start | bytes 49156
  1507.5 81.6 %copy-start.44 = (f32[8,512]{1,0:T(8,128)S(1)}, f32[8,512]{1,0:T(8,128)}, u32[]{:S(2)}) copy-start(f32[8,512]{1,0:T(8,128)} %get-tuple-element.1969) | copy-start | bytes 49156
  1507.5 81.6 %copy-start.46 = (f32[8,512]{1,0:T(8,128)S(1)}, f32[8,512]{1,0:T(8,128)}, u32[]{:S(2)}) copy-start(f32[8,512]{1,0:T(8,128)} %get-tuple-element.1970) | copy-start | bytes 49156
  1589.0 35.8 %copy-start.58 = (f32[768]{0:T(1024)S(1)}, f32[768]{0:T(1024)}, u32[]{:S(2)}) copy-start(f32[768]{0:T(1024)} %get-tuple-element.1753) | copy-start | bytes 9220
  1589.0 35.8 %copy-start.60 = (f32[768]{0:T(1024)S(1)}, f32[768]{0:T(1024)}, u32[]{:S(2)}) copy-start(f32[768]{0:T(1024)} %get-tuple-element.1754) | copy-start | bytes 9220
  1589.0 35.8 %copy-start.62 = (f32[768]{0:T(1024)S(1)}, f32[768]{0:T(1024)}, u32[]{:S(2)}) copy-start(f32[768]{0:T(1024)} %get-tuple-element.1755) | copy-start | bytes 9220
  1589.0 35.8 %copy-start.64 = (f32[768]{0:T(1024)S(1)}, f32[768]{0:T(1024)}, u32[]{:S(2)}) copy-start(f32[768]{0:T(1024)} %get-tuple-element.1756) | copy-start | bytes 9220
  1672.2 5.9 collective-permute-start.3
  1695.2 18.5 copy-start.7
  1711.7 663.8 %all-reduce.22.cloned.1.call-start = ((), (), s32[]{:S(2)}) async-start(), calls=%async_computation.7 | async-start | bytes 67108864 | tf_op jit(solution)/shard_map/psum | solution.py:171
  1719.5 55.5 %copy-start.15 = (f32[8,8,4,128]{1,0,3,2:T(8,128)S(1)}, f32[8,8,4,128]{1,0,3,2:T(8,128)}, u32[]{:S(2)}) copy-start(f32[8,8,4,128]{1,0,3,2:T(8,128)} %copy.423) | copy-start | bytes 393220
  1815.8 637.5 %reduce-scatter.8.cloned.1.call-start = ((), (), s32[]{:S(2)}) async-start(), calls=%async_computation.6 | async-start | bytes 2359296 | tf_op jit(solution)/shard_map/reduce_scatter | solution.py:242
  1827.6 687.6 %reduce-scatter.6.cloned.1.call-start = ((), (), s32[]{:S(2)}) async-start(), calls=%async_computation.5 | async-start | bytes 1179648 | tf_op jit(solution)/shard_map/reduce_scatter | solution.py:241
  1833.1 542.5 %copy-start.38 = (bf16[1024,256]{1,0:T(8,128)(2,1)S(1)}, bf16[1024,256]{1,0:T(8,128)(2,1)}, u32[]{:S(2)}) copy-start(bf16[1024,256]{1,0:T(8,128)(2,1)} %param.24) | copy-start | bytes 1572868
  2375.5 15.4 copy-start.86
  2375.6 53.7 %copy-start.54 = (f32[8,512]{1,0:T(8,128)S(1)}, f32[8,512]{1,0:T(8,128)}, u32[]{:S(2)}) copy-start(f32[8,512]{1,0:T(8,128)} %get-tuple-element.1971) | copy-start | bytes 49156
  (83 other events, 652.1 us)
Sparse Core Ops, SparseCore 0:
  1503.0 85.9 all-reduce.19
  1711.8 88.2 reduce-scatter.3
  1815.9 559.5 all-reduce.21
  2379.9 68.5 reduce-scatter.7
  2452.7 62.4 reduce-scatter.5
where the time goes:
time: 2530 us; the launch traced here: 2520 us
  waiting for transfers between devices  1290 us (51%)
  other arithmetic  488 us (19%)
  matrix products  376 us (15%)
  local copies, waits for them, and re-layouts  241 us (10%)
  blocking collectives  59 us (2%)
  starting transfers between devices  49.1 us (2%)
    ppermute x16, waiting for transfers between devices, shifted(): lax.ppermute(value, axis, [(source, source + steps) for source in range(l...  625 us
    psum x1, waiting for transfers between devices, shards(): branch_path = lax.psum(partial_value, 'head')  532 us
    dot_general x6, matrix products, block_pass(): inside = jnp.einsum('shij,sjhp->sihp', mixing, x_heads, precision=accurate)  130 us
    another operation x27, other arithmetic  111 us
    dynamic_update_slice x18, other arithmetic, ssd_scan(): (state, prev_ids), outs = lax.scan(block_pass, (state, prev_ids), pieces)  75 us
    psum x1, waiting for transfers between devices, shards(): d_bc = lax.psum(jnp.concatenate([y_db + s_db, y_dc], axis=2), 'head')  66.7 us
    reduce_scatter x1, waiting for transfers between devices, shards(): lax.psum_scatter(state_gradient_rows, 'seq', scatter_dimension=0, tiled=T...  61.9 us
  transfers between devices with their start and end apart: 21, of which 18 were waited for; matrix products, arithmetic and copies ran while one was open for 9% of the time, Pallas kernels for 0%

commit v1 on v0

v1 whole, which is shorter than its diff:
```python
import functools

import jax
import jax.numpy as jnp
from jax import lax
from jax.experimental import pallas as pl
from jax.experimental.pallas import tpu as pltpu
from jax.sharding import PartitionSpec as P

F32 = jnp.float32
BF16 = jnp.bfloat16
EPS = 1e-5
CHUNK = 128
PAD = 16
LANES = 128
HEAD_DIM = 64
VMEM = 60 * 1024 * 1024


def dot(a, b):
    return lax.dot_general(a, b, (((1,), (0,)), ((), ())), preferred_element_type=F32)


def dot_nt(a, b):
    return lax.dot_general(a, b, (((1,), (1,)), ((), ())), preferred_element_type=F32)


def dot_tn(a, b):
    return lax.dot_general(a, b, (((0,), (0,)), ((), ())), preferred_element_type=F32)


def split(value):
    high = value.astype(BF16)
    return high, (value - high.astype(F32)).astype(BF16)


def head_map(width):
    lane = lax.broadcasted_iota(jnp.int32, (LANES, width), 1)
    row = lax.broadcasted_iota(jnp.int32, (LANES, width), 0)
    return (lax.shift_right_logical(lane, 6) == row).astype(F32).astype(BF16)


def expand(value, heads):
    high, low = split(value)
    return dot(high, heads) + dot(low, heads)


def by_head(value, heads):
    high, low = split(value)
    return dot_nt(high, heads) + dot_nt(low, heads)


def widen(value, width):
    return jnp.concatenate([value] * (width // LANES), axis=1)


def fold8(value):
    return value[0:8] + value[8:16]


def sigmoid(value):
    return 1.0 / (1.0 + jnp.exp(-value))


def triangle(lower):
    row = lax.broadcasted_iota(jnp.int32, (CHUNK, CHUNK), 0)
    column = lax.broadcasted_iota(jnp.int32, (CHUNK, CHUNK), 1)
    return (row >= column if lower else row <= column)


def exact_dot(ones, value):
    return jnp.dot(ones, value, precision=lax.Precision.HIGHEST, preferred_element_type=F32)


def rows_at(start, count):
    return pl.ds(pl.multiple_of(start, 16), count)


def conv_slab(rows, ids, taps, start):
    values = rows(start - PAD, 32).astype(F32)
    marks = ids(start - PAD, 32)
    current = marks[16:32]
    total = taps[4:5]
    entering = []
    for k in range(4):
        moved = values[13 + k : 29 + k]
        if k < 3:
            same = (marks[13 + k : 29 + k] == current).astype(F32)
            moved = moved * widen(same, values.shape[1])
        entering.append(moved)
        total = total + taps[k : k + 1] * moved
    return total, entering


def conv_forward(rows, ids, taps, store, length):
    def step(i, carry):
        total, _ = conv_slab(rows, ids, taps, PAD + i * 16)
        store(i * 16, (total * sigmoid(total)).astype(BF16))
        return carry

    lax.fori_loop(0, length // 16, step, 0)


def conv_backward(rows, ids, taps, d_acted, d_pre, d_rows, length):
    width = d_pre.shape[1]
    zero = jnp.zeros((16, width), F32)
    d_pre[0:16, :] = zero
    d_pre[length + PAD : length + PAD + 16, :] = zero

    def first(i, sums):
        start = PAD + i * 16
        total, entering = conv_slab(rows, ids, taps, start)
        sigma = sigmoid(total)
        grad = d_acted(i * 16) * (sigma * (1.0 + total * (1.0 - sigma)))
        d_pre[rows_at(start, 16), :] = grad
        return tuple(s + fold8(grad * e) for s, e in zip(sums, entering + [1.0]))

    sums = lax.fori_loop(0, length // 16, first, tuple(jnp.zeros((8, width), F32) for _ in range(5)))

    def second(i, carry):
        start = i * 16
        values = d_pre[rows_at(start, 32), :]
        marks = ids(start, 32)
        current = marks[0:16]
        total = taps[3:4] * values[0:16]
        for k in range(3):
            same = (marks[3 - k : 19 - k] == current).astype(F32)
            total = total + taps[k : k + 1] * (values[3 - k : 19 - k] * widen(same, width))
        d_rows(start, total.astype(BF16))
        return carry

    lax.fori_loop(0, (length + PAD) // 16, second, 0)
    return sums


def project_kernel(blocks, normed, state_w, *refs):
    weights, refs = refs[:blocks], refs[blocks:]
    steps, refs = refs[:blocks], refs[blocks:]
    gate, rows, raw, state_rows = refs
    width = gate.shape[3]
    values = normed[0]
    state_rows[0] = dot(values, state_w[...]).astype(BF16)
    for r in range(blocks):
        gate[r, 0] = dot(values[PAD:], weights[r][:, :width]).astype(BF16)
        rows[r, 0] = dot(values, weights[r][:, width:]).astype(BF16)
        raw[r, 0] = dot_nt(values[PAD:], steps[r][...])


def project(normed, state_w, weights, steps):
    n, padded, model = normed.shape
    blocks = len(weights)
    width = weights[0].shape[1] // 2
    length = padded - PAD
    whole = lambda a: pl.BlockSpec(a.shape, lambda s: (0,) * a.ndim)
    return pl.pallas_call(
        functools.partial(project_kernel, blocks),
        grid=(n,),
        in_specs=[pl.BlockSpec((1, padded, model), lambda s: (s, 0, 0)), whole(state_w)]
        + [whole(v) for v in weights]
        + [whole(v) for v in steps],
        out_specs=[
            pl.BlockSpec((blocks, 1, length, width), lambda s: (0, s, 0, 0)),
            pl.BlockSpec((blocks, 1, padded, width), lambda s: (0, s, 0, 0)),
            pl.BlockSpec((blocks, 1, length, LANES), lambda s: (0, s, 0, 0)),
            pl.BlockSpec((1, padded, state_w.shape[1]), lambda s: (s, 0, 0)),
        ],
        out_shape=[
            jax.ShapeDtypeStruct((blocks, n, length, width), BF16),
            jax.ShapeDtypeStruct((blocks, n, padded, width), BF16),
            jax.ShapeDtypeStruct((blocks, n, length, LANES), F32),
            jax.ShapeDtypeStruct((n, padded, state_w.shape[1]), BF16),
        ],
        compiler_params=pltpu.CompilerParams(vmem_limit_bytes=VMEM),
        name="project",
    )(normed, state_w, *weights, *steps)


def conv_state_kernel(rows, ids, taps, acted):
    length = acted.shape[1]

    def store(start, value):
        acted[0, rows_at(start, 16), :] = value

    conv_forward(
        lambda i, c: rows[0, rows_at(i, c), :], lambda i, c: ids[0, rows_at(i, c), :], taps[...], store, length
    )


def conv_state_call(rows, ids, taps):
    n, padded, width = rows.shape
    length = padded - PAD
    return pl.pallas_call(
        conv_state_kernel,
        grid=(n,),
        in_specs=[
            pl.BlockSpec((1, padded, width), lambda s: (s, 0, 0)),
            pl.BlockSpec((1,) + ids.shape[1:], lambda s: (s, 0, 0)),
            pl.BlockSpec(taps.shape, lambda s: (0, 0)),
        ],
        out_specs=pl.BlockSpec((1, length, width), lambda s: (s, 0, 0)),
        out_shape=jax.ShapeDtypeStruct((n, length, width), BF16),
        compiler_params=pltpu.CompilerParams(vmem_limit_bytes=VMEM),
        name="conv_state",
    )(rows, ids, taps)


def state_kernel(rows, bc, ids, steps, log_decay, taps, acted, cum, message):
    length, width = acted.shape[2:]
    heads = head_map(width)

    def store(start, value):
        acted[0, 0, rows_at(start, 16), :] = value

    conv_forward(
        lambda i, c: rows[0, 0, rows_at(i, c), :],
        lambda i, c: ids[0, rows_at(i, c), :],
        taps[0],
        store,
        length,
    )
    ones = triangle(True).astype(F32)
    total = jnp.zeros((1, LANES), F32)
    for c in range(length // CHUNK):
        part = exact_dot(ones, log_decay[0, 0, c * CHUNK : (c + 1) * CHUNK, :]) + total
        cum[0, 0, c * CHUNK : (c + 1) * CHUNK, :] = part
        total = part[CHUNK - 1 : CHUNK]
    last = ids[0, PAD + length - 1 : PAD + length, :]
    before = ids[0, PAD - 1 : PAD, :]
    state = jnp.zeros((LANES, width), F32)
    for c in range(length // CHUNK):
        here = slice(c * CHUNK, (c + 1) * CHUNK)
        same = (ids[0, PAD + c * CHUNK : PAD + (c + 1) * CHUNK, :] == last).astype(F32)
        tail = jnp.exp(total - cum[0, 0, here, :]) * same * steps[0, 0, here, :]
        scaled = (expand(tail, heads) * acted[0, 0, here, :].astype(F32)).astype(BF16)
        state = state + dot_tn(bc[0, here, :LANES], scaled)
    message[0, 0, :LANES, :] = state.astype(BF16)
    survive = jnp.exp(total) * (last == before).astype(F32)
    message[0, 0, LANES:, :] = expand(jnp.broadcast_to(survive, (16, LANES)), heads).astype(BF16)


def state_call(rows, bc, ids, steps, log_decay, taps):
    blocks, n, padded, width = rows.shape
    length = padded - PAD
    four = lambda a, b: pl.BlockSpec((1, 1, a, b), lambda g, s: (g, s, 0, 0))
    return pl.pallas_call(
        state_kernel,
        grid=(blocks, n),
        in_specs=[
            four(padded, width),
            pl.BlockSpec((1,) + bc.shape[1:], lambda g, s: (s, 0, 0)),
            pl.BlockSpec((1,) + ids.shape[1:], lambda g, s: (s, 0, 0)),
            four(length, LANES),
            four(length, LANES),
            pl.BlockSpec((1,) + taps.shape[1:], lambda g, s: (g, 0, 0)),
        ],
        out_specs=[four(length, width), four(length, LANES), four(LANES + 16, width)],
        out_shape=[
            jax.ShapeDtypeStruct((blocks, n, length, width), BF16),
            jax.ShapeDtypeStruct((blocks, n, length, LANES), F32),
            jax.ShapeDtypeStruct((blocks, n, LANES + 16, width), BF16),
        ],
        compiler_params=pltpu.CompilerParams(vmem_limit_bytes=VMEM),
        name="range_state",
    )(rows, bc, ids, steps, log_decay, taps)


def chunk_marks(ids, c):
    first = PAD + c * CHUNK
    return ids[0, first : first + CHUNK, :], ids[0, first + CHUNK - 1 : first + CHUNK, :], ids[0, first - 1 : first, :]


def chunk_decays(ids, cum, c):
    here, last, before = chunk_marks(ids, c)
    value = cum[0, 0, c * CHUNK : (c + 1) * CHUNK, :]
    base = cum[0, 0, c * CHUNK - 1 : c * CHUNK, :] if c else jnp.zeros((1, LANES), F32)
    end = value[CHUNK - 1 : CHUNK]
    entering = jnp.exp(value - base) * (here == before).astype(F32)
    tail = jnp.exp(end - value) * (here == last).astype(F32)
    survive = jnp.exp(end - base) * (last == before).astype(F32)
    return entering, tail, survive


def lane_halves(pair):
    lane = lax.broadcasted_iota(jnp.int32, pair.shape, 1)
    zero = jnp.zeros_like(pair)
    return jnp.concatenate([jnp.where(lane < HEAD_DIM, pair, zero), jnp.where(lane < HEAD_DIM, zero, pair)], axis=0)


def row_of(value, width):
    return jnp.broadcast_to(value, (16, LANES))


def inside_kernel(acted, bc, ids, id_rows, steps, cum, mixed, states, carried):
    length, width = acted.shape[2:]
    heads = head_map(width)
    later = triangle(True)
    for c in range(length // CHUNK):
        here = slice(c * CHUNK, (c + 1) * CHUNK)
        b_part, c_part = bc[0, here, :LANES], bc[0, here, LANES:]
        marks, _, _ = chunk_marks(ids, c)
        same = later & (marks == id_rows[0, 0:1, here])
        scores = jnp.where(same, dot_nt(c_part, b_part), 0.0)
        value = cum[0, 0, here, :]
        value_t = jnp.transpose(value)
        entering, tail, survive = chunk_decays(ids, cum, c)
        scaled = (expand(steps[0, 0, here, :], heads) * acted[0, 0, here, :].astype(F32)).astype(BF16)
        if c:
            held = carried[...]
            held_low = held.astype(BF16)
            states[0, 0, c - 1] = held_low
            outside = dot(c_part, held_low) * expand(entering, heads)
        for pair in range(width // LANES):
            lanes = slice(pair * LANES, (pair + 1) * LANES)
            mixing = []
            for h in (2 * pair, 2 * pair + 1):
                spread = jnp.minimum(value[:, h : h + 1] - value_t[h : h + 1, :], 0.0)
                mixing.append((scores * jnp.exp(spread)).astype(BF16))
            result = dot(jnp.concatenate(mixing, axis=1), lane_halves(scaled[:, lanes]))
            mixed[0, 0, here, lanes] = result + outside[:, lanes] if c else result
        if c + 1 < length // CHUNK:
            fresh = dot_tn(b_part, (expand(tail, heads) * scaled.astype(F32)).astype(BF16))
            if c:
                fresh = fresh + held * expand(jnp.broadcast_to(survive, (16, LANES)), heads)[0:1]
            carried[...] = fresh


def inside_call(acted, bc, ids, id_rows, steps, cum):
    blocks, n, length, width = acted.shape
    chunks = length // CHUNK
    four = lambda a, b: pl.BlockSpec((1, 1, a, b), lambda g, s: (g, s, 0, 0))
    per_seq = lambda a: pl.BlockSpec((1,) + a.shape[1:], lambda g, s: (s, 0, 0))
    return pl.pallas_call(
        inside_kernel,
        grid=(blocks, n),
        in_specs=[four(length, width), per_seq(bc), per_seq(ids), per_seq(id_rows), four(length, LANES), four(length, LANES)],
        out_specs=[
            four(length, width),
            pl.BlockSpec((1, 1, chunks - 1, LANES, width), lambda g, s: (g, s, 0, 0, 0)),
        ],
        out_shape=[
            jax.ShapeDtypeStruct((blocks, n, length, width), F32),
            jax.ShapeDtypeStruct((blocks, n, chunks - 1, LANES, width), BF16),
        ],
        scratch_shapes=[pltpu.VMEM((LANES, width), F32)],
        compiler_params=pltpu.CompilerParams(vmem_limit_bytes=VMEM),
        name="inside",
    )(acted, bc, ids, id_rows, steps, cum)


def relay_kernel(backward, message, carried):
    ranges, rows, width = carried.shape
    state = jnp.zeros((rows, width), F32)
    order = range(ranges - 1, -1, -1) if backward else range(ranges)
    for q in order:
        carried[q] = state.astype(BF16)
        decay = message[q, rows : rows + 1, :].astype(F32)
        state = state * decay + message[q, :rows, :].astype(F32)


def relay(message, backward):
    blocks, n, rows, width = message.shape
    ranges = lax.axis_size("seq")
    cuts = max(1, ranges // (blocks * n))
    own = LANES // cuts
    parts = message.reshape(blocks * n, rows, width)
    if cuts > 1:
        ends = parts[:, LANES:]
        parts = jnp.stack(
            [jnp.concatenate([parts[:, i * own : (i + 1) * own], ends], axis=1) for i in range(cuts)], axis=1
        ).reshape(blocks * n * cuts, own + 16, width)
    arrived = lax.all_to_all(parts, "seq", 0, 0, tiled=True)
    carried = pl.pallas_call(
        functools.partial(relay_kernel, backward),
        out_shape=jax.ShapeDtypeStruct((ranges, own, width), BF16),
        name="relay",
    )(arrived)
    back = lax.all_to_all(carried, "seq", 0, 0, tiled=True)
    return back.reshape(blocks, n, LANES, width)


def middle_kernel(
    blocks, total_width, mixed, gate, acted, cum, entered, bc, ids, ids_before, tokens, cotangent, params, message, *refs
):
    weights, refs = refs[:blocks], refs[blocks:]
    output, normed_out, d_gate, d_summed, pulled, gain_grad, skip_grad = refs[:7]
    summed_s, gated_s, grad_s, first_s, second_s, low_s, row_s, pull_s = refs[7:]
    tile, width = mixed.shape[2:]
    s, t = pl.program_id(0), pl.program_id(1)
    heads = head_map(width)
    before = ids_before[0, PAD - 1 : PAD, :]
    marks = ids[0]
    c_part = bc[0, :, LANES:]
    slabs = tile // 16
    same = (marks == before).astype(F32)
    row_s[...] = jnp.zeros_like(row_s)

    def lanes_sum(value):
        total = value[:, :LANES]
        for i in range(1, width // LANES):
            total = total + value[:, i * LANES : (i + 1) * LANES]
        return total

    @pl.when((s == 0) & (t == 0))
    def _():
        gain_grad[...] = jnp.zeros_like(gain_grad)
        skip_grad[...] = jnp.zeros_like(skip_grad)

    @pl.when(t == 0)
    def _():
        pull_s[...] = jnp.zeros_like(pull_s)

    for r in range(blocks):
        first_s[...] = dot(c_part, entered[r, 0])
        second_s[r] = expand(jnp.exp(cum[r, 0]) * same, heads)
        skip = params[r, 6:7, :]

        def step(i, carry, r=r, skip=skip):
            here = rows_at(i * 16, 16)
            value = mixed[r, 0, here, :] + first_s[here, :] * second_s[r, here, :]
            summed = value + skip * acted[r, 0, here, :].astype(F32)
            g = gate[r, 0, here, :].astype(F32)
            gated = summed * (g * sigmoid(g))
            summed_s[r, here, :] = summed
            gated_s[r, here, :] = gated
            row_s[here, :] = row_s[here, :] + lanes_sum(gated * gated)
            return carry

        lax.fori_loop(0, slabs, step, 0)
    squares = jnp.sum(row_s[...], axis=1, keepdims=True)
    rescale = jnp.broadcast_to(lax.rsqrt(squares / total_width + EPS), (tile, LANES))
    row_s[...] = rescale
    for r in range(blocks):
        gain = params[r, 5:6, :]

        def step(i, carry, r=r, gain=gain):
            here = rows_at(i * 16, 16)
            normed_out[r, 0, here, :] = (gated_s[r, here, :] * widen(row_s[here, :], width) * gain).astype(BF16)
            return carry

        lax.fori_loop(0, slabs, step, 0)
    branch = tokens[0].astype(F32)
    for r in range(blocks):
        branch = branch + dot(normed_out[r, 0], weights[r][...])
    output[0] = branch.astype(BF16)
    first_s[:, :LANES] = jnp.zeros((tile, LANES), F32)
    for r in range(blocks):
        grad_s[r] = dot_nt(cotangent[0], weights[r][...])
        gain = params[r, 5:6, :]

        def step(i, total, r=r, gain=gain):
            here = rows_at(i * 16, 16)
            both = grad_s[r, here, :] * gated_s[r, here, :]
            first_s[here, :LANES] = first_s[here, :LANES] + lanes_sum(both * gain)
            return total + fold8(both * widen(row_s[here, :], width))

        gain_grad[r] = gain_grad[r] + lax.fori_loop(0, slabs, step, jnp.zeros((8, width), F32))
    cross = jnp.sum(first_s[:, :LANES], axis=1, keepdims=True) / total_width
    first_s[:, :LANES] = rescale * rescale * rescale * cross
    for r in range(blocks):
        gain = params[r, 5:6, :]

        def step(i, total, r=r, gain=gain):
            here = rows_at(i * 16, 16)
            g = gate[r, 0, here, :].astype(F32)
            sigma = sigmoid(g)
            d_gated = widen(row_s[here, :], width) * (grad_s[r, here, :] * gain) - gated_s[r, here, :] * widen(
                first_s[here, :LANES], width
            )
            d_sum = d_gated * (g * sigma)
            d_gate[r, 0, here, :] = (d_gated * summed_s[r, here, :] * (sigma * (1.0 + g * (1.0 - sigma)))).astype(BF16)
            low = d_sum.astype(BF16)
            d_summed[r, 0, here, :] = low
            low_s[here, :] = (d_sum * second_s[r, here, :]).astype(BF16)
            return total + fold8(d_sum * acted[r, 0, here, :].astype(F32))

        skip_grad[r] = skip_grad[r] + lax.fori_loop(0, slabs, step, jnp.zeros((8, width), F32))
        pull_s[r] = pull_s[r] + dot_tn(c_part, low_s[...])

    @pl.when(t == pl.num_programs(1) - 1)
    def _():
        for r in range(blocks):
            pulled[r, 0, :LANES, :] = pull_s[r].astype(BF16)
            pulled[r, 0, LANES:, :] = message[r, 0, LANES:, :]


def middle_call(mixed, gate, acted, cum, entered, bc, ids, tokens, cotangent, params, message, weights, total_width):
    blocks, n, length, width = mixed.shape
    model = tokens.shape[2]
    tile = min(256, length)
    wide = lambda w: pl.BlockSpec((blocks, 1, tile, w), lambda s, t: (0, s, t, 0))
    rows = lambda w: pl.BlockSpec((1, tile, w), lambda s, t: (s, t, 0))
    per_seq = lambda a: pl.BlockSpec((a.shape[0], 1) + a.shape[2:], lambda s, t: (0, s, 0, 0))
    whole = lambda a: pl.BlockSpec(a.shape, lambda s, t: (0,) * a.ndim, pipeline_mode=pl.Buffered(1))
    kept = lambda *shape: pl.BlockSpec(shape, lambda s, t: (0,) * len(shape))
    ids_here = ids[:, PAD : PAD + length]
    return pl.pallas_call(
        functools.partial(middle_kernel, blocks, total_width),
        grid=(n, length // tile),
        in_specs=[
            wide(width), wide(width), wide(width), wide(LANES), per_seq(entered), rows(2 * LANES), rows(LANES),
            pl.BlockSpec((1, PAD, LANES), lambda s, t: (s, 0, 0)), rows(model), rows(model), whole(params), per_seq(message),
        ] + [whole(v) for v in weights],
        out_specs=[
            rows(model), wide(width), wide(width), wide(width), per_seq(message),
            kept(blocks, 8, width), kept(blocks, 8, width),
        ],
        out_shape=[
            jax.ShapeDtypeStruct((n, length, model), BF16),
            jax.ShapeDtypeStruct((blocks, n, length, width), BF16),
            jax.ShapeDtypeStruct((blocks, n, length, width), BF16),
            jax.ShapeDtypeStruct((blocks, n, length, width), BF16),
            jax.ShapeDtypeStruct(message.shape, BF16),
            jax.ShapeDtypeStruct((blocks, 8, width), F32),
            jax.ShapeDtypeStruct((blocks, 8, width), F32),
        ],
        scratch_shapes=[
            pltpu.VMEM((blocks, tile, width), F32),
            pltpu.VMEM((blocks, tile, width), F32),
            pltpu.VMEM((blocks, tile, width), F32),
            pltpu.VMEM((tile, width), F32),
            pltpu.VMEM((blocks, tile, width), F32),
            pltpu.VMEM((tile, width), BF16),
            pltpu.VMEM((tile, LANES), F32),
            pltpu.VMEM((blocks, LANES, width), F32),
        ],
        compiler_params=pltpu.CompilerParams(vmem_limit_bytes=VMEM),
        name="middle",
    )(mixed, gate, acted, cum, entered, bc, ids_here, ids[:, :PAD], tokens, cotangent, params, message, *weights)


def inside_back_kernel(
    acted, d_summed, mixed, bc, ids, id_rows, steps, cum, states, entered, d_scaled, d_b, d_c, d_cum, carried
):
    length, width = acted.shape[2:]
    chunks = length // CHUNK
    heads = head_map(width)
    g = pl.program_id(1)
    sooner = triangle(False)
    first_before = ids[0, PAD - 1 : PAD, :]

    @pl.when(g == 0)
    def _():
        d_b[...] = jnp.zeros_like(d_b)
        d_c[...] = jnp.zeros_like(d_c)

    for c in range(chunks - 1, -1, -1):
        here = slice(c * CHUNK, (c + 1) * CHUNK)
        b_part, c_part = bc[0, here, :LANES], bc[0, here, LANES:]
        marks, _, _ = chunk_marks(ids, c)
        same = sooner & (marks == id_rows[0, 0:1, here])
        scores_t = jnp.where(same, dot_nt(b_part, c_part), 0.0)
        value = cum[0, 0, here, :]
        value_t = jnp.transpose(value)
        entering, tail, survive = chunk_decays(ids, cum, c)
        scaled = (expand(steps[0, 0, here, :], heads) * acted[0, 0, here, :].astype(F32)).astype(BF16)
        grad = d_summed[0, 0, here, :]
        grad_wide = grad.astype(F32)
        from_start = jnp.exp(value) * (marks == first_before).astype(F32)
        start_wide = expand(from_start, heads)
        d_c_part = dot_nt((grad_wide * start_wide).astype(BF16), entered[0, 0])
        dots = grad_wide * (mixed[0, 0, here, :] + start_wide * dot(c_part, entered[0, 0]))
        if c < chunks - 1:
            held = carried[...]
            held_low = held.astype(BF16)
            tail_wide = expand(tail, heads)
            later = dot(b_part, held_low) * tail_wide
            d_b_part = dot_nt((tail_wide * scaled.astype(F32)).astype(BF16), held_low)
        if c:
            entering_grad = (expand(entering, heads) * grad_wide).astype(BF16)
            d_c_part = d_c_part + dot_nt(entering_grad, states[0, 0, c - 1])
        d_scores_t = jnp.zeros((CHUNK, CHUNK), F32)
        results = []
        for pair in range(width // LANES):
            lanes = slice(pair * LANES, (pair + 1) * LANES)
            products = dot_nt(lane_halves(scaled[:, lanes]), grad[:, lanes])
            mixing = []
            for half, h in enumerate((2 * pair, 2 * pair + 1)):
                spread = jnp.minimum(value_t[h : h + 1, :] - value[:, h : h + 1], 0.0)
                decay = jnp.exp(spread)
                mixing.append((scores_t * decay).astype(BF16))
                d_scores_t = d_scores_t + products[half * CHUNK : (half + 1) * CHUNK] * decay
            results.append(dot(jnp.concatenate(mixing, axis=1), lane_halves(grad[:, lanes])))
        result = jnp.concatenate(results, axis=1)
        if c < chunks - 1:
            result = result + later
        d_scaled[0, 0, here, :] = result.astype(BF16)
        d_cum[0, 0, here, :] = by_head(dots - scaled.astype(F32) * result, heads)
        d_scores_t = jnp.where(same, d_scores_t, 0.0).astype(BF16)
        d_b_here = dot(d_scores_t, c_part)
        if c < chunks - 1:
            d_b_here = d_b_here + d_b_part
        d_b[0, here, :] = d_b[0, here, :] + d_b_here
        d_c[0, here, :] = d_c[0, here, :] + d_c_part + dot_tn(d_scores_t, b_part)
        if c:
            pulled = dot_tn(c_part, entering_grad)
            if c < chunks - 1:
                pulled = pulled + held * expand(jnp.broadcast_to(survive, (16, LANES)), heads)[0:1]
            carried[...] = pulled


def inside_back_call(acted, d_summed, mixed, bc, ids, id_rows, steps, cum, states, entered):
    blocks, n, length, width = acted.shape
    four = lambda a, b: pl.BlockSpec((1, 1, a, b), lambda s, g: (g, s, 0, 0))
    per_seq = lambda a: pl.BlockSpec((1,) + a.shape[1:], lambda s, g: (s, 0, 0))
    summed = pl.BlockSpec((1, length, LANES), lambda s, g: (s, 0, 0))
    return pl.pallas_call(
        inside_back_kernel,
        grid=(n, blocks),
        in_specs=[
            four(length, width), four(length, width), four(length, width), per_seq(bc), per_seq(ids), per_seq(id_rows),
            four(length, LANES), four(length, LANES),
            pl.BlockSpec((1, 1) + states.shape[2:], lambda s, g: (g, s, 0, 0, 0)), four(LANES, width),
        ],
        out_specs=[four(length, width), summed, summed, four(length, LANES)],
        out_shape=[
            jax.ShapeDtypeStruct((blocks, n, length, width), BF16),
            jax.ShapeDtypeStruct((n, length, LANES), F32),
            jax.ShapeDtypeStruct((n, length, LANES), F32),
            jax.ShapeDtypeStruct((blocks, n, length, LANES), F32),
        ],
        scratch_shapes=[pltpu.VMEM((LANES, width), F32)],
        compiler_params=pltpu.CompilerParams(vmem_limit_bytes=VMEM),
        name="inside_back",
    )(acted, d_summed, mixed, bc, ids, id_rows, steps, cum, states, entered)


def close_kernel(
    rows, acted, d_summed, d_scaled, bc, ids, steps, raw, log_decay, cum, d_cum, leaving, entered, params, small,
    d_rows, d_raw, d_b, taps_grad, small_grad, d_pre, d_acted, d_log,
):
    length, width = acted.shape[2:]
    chunks = length // CHUNK
    heads = head_map(width)
    s, g = pl.program_id(0), pl.program_id(1)
    last = ids[0, PAD + length - 1 : PAD + length, :]
    before = ids[0, PAD - 1 : PAD, :]
    end = cum[0, 0, length - 1 : length, :]
    skip = params[0, 6:7, :]
    held = leaving[0, 0]

    @pl.when(g == 0)
    def _():
        d_b[...] = jnp.zeros_like(d_b)

    boundary = jnp.zeros((1, LANES), F32)
    for c in range(chunks):
        here = slice(c * CHUNK, (c + 1) * CHUNK)
        marks, _, _ = chunk_marks(ids, c)
        tail = jnp.exp(end - cum[0, 0, here, :]) * (marks == last).astype(F32)
        tail_wide = expand(tail, heads)
        steps_wide = expand(steps[0, 0, here, :], heads)
        x = acted[0, 0, here, :].astype(F32)
        scaled = (steps_wide * x).astype(BF16).astype(F32)
        later = dot(bc[0, here, :LANES], held) * tail_wide
        total = d_scaled[0, 0, here, :].astype(F32) + later
        d_acted[here, :] = steps_wide * total + skip * d_summed[0, 0, here, :].astype(F32)
        d_b[0, here, :] = d_b[0, here, :] + dot_nt((tail_wide * scaled).astype(BF16), held)
        from_later = by_head(scaled * later, heads)
        boundary = boundary + jnp.sum(from_later, axis=0, keepdims=True)
        d_log[here, :] = d_cum[0, 0, here, :] - from_later
        d_raw[0, 0, here, :] = by_head(x * total, heads)
    product = held.astype(F32) * entered[0, 0].astype(F32)
    product = jnp.sum(product, axis=0, keepdims=True)
    survive = jnp.exp(end) * (last == before).astype(F32)
    boundary = boundary + survive * by_head(jnp.broadcast_to(product, (16, width)), heads)[0:1]
    rate = jnp.exp(small[0, 1:2, :])
    ones = triangle(False).astype(F32)
    carry = boundary
    decay_sum = jnp.zeros((1, LANES), F32)
    bias_sum = jnp.zeros((1, LANES), F32)
    for c in range(chunks - 1, -1, -1):
        here = slice(c * CHUNK, (c + 1) * CHUNK)
        grads = exact_dot(ones, d_log[here, :]) + carry
        carry = grads[0:1]
        decay_sum = decay_sum + jnp.sum(grads * log_decay[0, 0, here, :], axis=0, keepdims=True)
        value = (d_raw[0, 0, here, :] - grads * rate) * sigmoid(raw[0, 0, here, :] + small[0, 0:1, :])
        bias_sum = bias_sum + jnp.sum(value, axis=0, keepdims=True)
        d_raw[0, 0, here, :] = value
    small_grad[0, 0] = jnp.concatenate([bias_sum, decay_sum, jnp.zeros((6, LANES), F32)], axis=0)

    def store(start, value):
        d_rows[0, 0, rows_at(start, 16), :] = value

    sums = conv_backward(
        lambda i, n: rows[0, 0, rows_at(i, n), :],
        lambda i, n: ids[0, rows_at(i, n), :],
        params[0],
        lambda i: d_acted[rows_at(i, 16), :],
        d_pre,
        store,
        length,
    )
    taps_grad[0, 0] = jnp.concatenate(
        [jnp.sum(v, axis=0, keepdims=True) for v in sums] + [jnp.zeros((3, width), F32)], axis=0
    )


def close_call(
    rows, acted, d_summed, d_scaled, bc, ids, steps, raw, log_decay, cum, d_cum, leaving, entered, params, small
):
    blocks, n, length, width = acted.shape
    four = lambda a, b: pl.BlockSpec((1, 1, a, b), lambda s, g: (g, s, 0, 0))
    per_seq = lambda a: pl.BlockSpec((1,) + a.shape[1:], lambda s, g: (s, 0, 0))
    per_block = lambda a: pl.BlockSpec((1,) + a.shape[1:], lambda s, g: (g, 0, 0))
    lanes = four(length, LANES)
    wide = four(length, width)
    return pl.pallas_call(
        close_kernel,
        grid=(n, blocks),
        in_specs=[
            four(length + PAD, width), wide, wide, wide, per_seq(bc), per_seq(ids), lanes, lanes, lanes, lanes, lanes,
            four(LANES, width), four(LANES, width), per_block(params), per_block(small),
        ],
        out_specs=[
            four(length + PAD, width), lanes, pl.BlockSpec((1, length, LANES), lambda s, g: (s, 0, 0)),
            four(8, width), four(8, LANES),
        ],
        out_shape=[
            jax.ShapeDtypeStruct((blocks, n, length + PAD, width), BF16),
            jax.ShapeDtypeStruct((blocks, n, length, LANES), F32),
            jax.ShapeDtypeStruct((n, length, LANES), F32),
            jax.ShapeDtypeStruct((blocks, n, 8, width), F32),
            jax.ShapeDtypeStruct((blocks, n, 8, LANES), F32),
        ],
        scratch_shapes=[
            pltpu.VMEM((length + 2 * PAD, width), F32),
            pltpu.VMEM((length, width), F32),
            pltpu.VMEM((length, LANES), F32),
        ],
        compiler_params=pltpu.CompilerParams(vmem_limit_bytes=VMEM),
        name="close",
    )(rows, acted, d_summed, d_scaled, bc, ids, steps, raw, log_decay, cum, d_cum, leaving, entered, params, small)


def conv_state_back_kernel(rows, ids, taps, d_b, d_b_more, d_c, d_rows, taps_grad, d_pre, d_acted):
    length = d_b.shape[1]
    d_acted[:, :LANES] = d_b[0] + d_b_more[0]
    d_acted[:, LANES:] = d_c[0]

    def store(start, value):
        d_rows[0, rows_at(start, 16), :] = value

    sums = conv_backward(
        lambda i, n: rows[0, rows_at(i, n), :],
        lambda i, n: ids[0, rows_at(i, n), :],
        taps[...],
        lambda i: d_acted[rows_at(i, 16), :],
        d_pre,
        store,
        length,
    )
    taps_grad[0] = jnp.concatenate(
        [jnp.sum(v, axis=0, keepdims=True) for v in sums] + [jnp.zeros((3, 2 * LANES), F32)], axis=0
    )


def conv_state_back_call(rows, ids, taps, d_b, d_b_more, d_c):
    n, padded, width = rows.shape
    length = padded - PAD
    per_seq = lambda a, b: pl.BlockSpec((1, a, b), lambda s: (s, 0, 0))
    return pl.pallas_call(
        conv_state_back_kernel,
        grid=(n,),
        in_specs=[
            per_seq(padded, width), per_seq(*ids.shape[1:]), pl.BlockSpec(taps.shape, lambda s: (0, 0)),
            per_seq(length, LANES), per_seq(length, LANES), per_seq(length, LANES),
        ],
        out_specs=[per_seq(padded, width), per_seq(8, width)],
        out_shape=[
            jax.ShapeDtypeStruct((n, padded, width), BF16),
            jax.ShapeDtypeStruct((n, 8, width), F32),
        ],
        scratch_shapes=[pltpu.VMEM((length + 2 * PAD, width), F32), pltpu.VMEM((length, width), F32)],
        compiler_params=pltpu.CompilerParams(vmem_limit_bytes=VMEM),
        name="conv_state_back",
    )(rows, ids, taps, d_b, d_b_more, d_c)


def input_kernel(blocks, d_gate, d_rows, d_raw, d_state, tokens, cotangent, gain, state_w, *refs):
    weights, refs = refs[:blocks], refs[blocks:]
    steps, refs = refs[:blocks], refs[blocks:]
    input_grad, edge, halo, gain_grad, main_s, halo_s = refs
    length, width = d_gate.shape[2:]
    model = tokens.shape[2]
    total = dot_nt(d_state[0], state_w[...])
    main_s[...] = total[PAD:]
    halo_s[...] = total[:PAD]
    for r in range(blocks):
        part = dot_nt(d_rows[r, 0], weights[r][:, width:])
        halo_s[...] = halo_s[...] + part[:PAD]
        main_s[...] = main_s[...] + (
            part[PAD:] + dot_nt(d_gate[r, 0], weights[r][:, :width]) + dot(d_raw[r, 0].astype(BF16), steps[r][...])
        )

    def norm_back(value, token):
        scale = lax.rsqrt(jnp.mean(token * token, axis=1, keepdims=True) + EPS)
        unit = value * gain[...]
        inner = jnp.mean(unit * token, axis=1, keepdims=True)
        return scale * unit - token * (scale * scale * scale * inner), fold8(value * token * scale)

    grad, sums = norm_back(halo_s[...], tokens[0, :PAD, :].astype(F32))
    halo[0] = grad.astype(BF16)

    def step(i, carry):
        here = rows_at(i * 16, 16)
        grad, more = norm_back(main_s[here, :], tokens[0, rows_at(PAD + i * 16, 16), :].astype(F32))
        value = grad + cotangent[0, here, :].astype(F32)
        edge[0] = value
        input_grad[0, here, :] = value.astype(BF16)
        return carry + more

    gain_grad[0] = lax.fori_loop(0, length // 16, step, sums)


def input_call(d_gate, d_rows, d_raw, d_state, tokens, cotangent, gain, state_w, weights, steps):
    blocks, n, length, width = d_gate.shape
    padded, model = tokens.shape[1:]
    wide = lambda a, b: pl.BlockSpec((blocks, 1, a, b), lambda s: (0, s, 0, 0))
    per_seq = lambda a, b: pl.BlockSpec((1, a, b), lambda s: (s, 0, 0))
    whole = lambda a: pl.BlockSpec(a.shape, lambda s: (0,) * a.ndim, pipeline_mode=pl.Buffered(1))
    return pl.pallas_call(
        functools.partial(input_kernel, blocks),
        grid=(n,),
        in_specs=[
            wide(length, width), wide(padded, width), wide(length, LANES), per_seq(padded, state_w.shape[1]),
            per_seq(padded, model), per_seq(length, model), whole(gain), whole(state_w),
        ] + [whole(v) for v in weights] + [whole(v) for v in steps],
        out_specs=[per_seq(length, model), per_seq(PAD, model), per_seq(PAD, model), per_seq(8, model)],
        out_shape=[
            jax.ShapeDtypeStruct((n, length, model), BF16),
            jax.ShapeDtypeStruct((n, PAD, model), F32),
            jax.ShapeDtypeStruct((n, PAD, model), BF16),
            jax.ShapeDtypeStruct((n, 8, model), F32),
        ],
        scratch_shapes=[pltpu.VMEM((length, model), F32), pltpu.VMEM((PAD, model), F32)],
        compiler_params=pltpu.CompilerParams(vmem_limit_bytes=VMEM),
        name="input_gradient",
    )(d_gate, d_rows, d_raw, d_state, tokens, cotangent, gain, state_w, *weights, *steps)


def swapped(value, axis, step):
    return lax.ppermute(value, axis, [(i, i ^ step) for i in range(lax.axis_size(axis))])


def gathered(value):
    parts = [value]
    for r in range(1, lax.axis_size("head")):
        parts.append(swapped(parts[r - 1], "head", 1) if r % 2 else swapped(value, "head", r))
    return parts


def scattered(parts):
    parts = list(parts)
    bit = 1
    while bit < lax.axis_size("head"):
        for r in range(0, lax.axis_size("head"), 2 * bit):
            arrived = swapped(parts[r + bit], "head", bit)
            parts[r] = (parts[r].astype(F32) + arrived.astype(F32)).astype(parts[r].dtype)
        bit *= 2
    return parts[0]


def summed_over(value, axis):
    bit = 1
    while bit < lax.axis_size(axis):
        value = value + swapped(value, axis, bit)
        bit *= 2
    return value


def ranges_sum(value):
    ranges = lax.axis_size("seq")
    arrived = lax.all_to_all(value, "seq", 0, 0, tiled=True)
    return jnp.sum(arrived.reshape((ranges, value.shape[0] // ranges) + value.shape[1:]).astype(F32), axis=0)


def assembled(value):
    n = value.shape[0]
    me = lax.axis_index("head")
    whole = jnp.zeros((n * lax.axis_size("head"),) + value.shape[1:], value.dtype)
    for r, part in enumerate(gathered(value)):
        whole = lax.dynamic_update_slice(whole, part, ((me ^ r) * n, 0, 0))
    return whole


def padded_lanes(value, size):
    return jnp.pad(value, ((0, 0), (0, size - value.shape[1])))


def shards(
    tokens,
    doc_ids,
    norm_gain,
    head_input_weight,
    state_input_weight,
    timestep_input_weight,
    conv_x,
    conv_state,
    head_params,
    gated_gain,
    output_weight,
    cotangent,
):
    seqs, length, model = tokens.shape
    blocks = lax.axis_size("head")
    ranges = lax.axis_size("seq")
    n = seqs // blocks
    width = gated_gain.shape[0]
    heads = head_params.shape[1]
    me = lax.axis_index("head")
    tokens = lax.dynamic_slice_in_dim(tokens, me * n, n, 0)
    cotangent = lax.dynamic_slice_in_dim(cotangent, me * n, n, 0)
    before = lax.ppermute(tokens[:, length - PAD :], "seq", [(i, i + 1) for i in range(ranges - 1)])
    padded = jnp.concatenate([before, tokens], axis=1)

    start = lax.axis_index("seq") * length
    lead = jnp.concatenate(
        [jnp.full((seqs, PAD), -1, jnp.int32), doc_ids, jnp.full((seqs, PAD), -2, jnp.int32)], axis=1
    )
    ids = lax.dynamic_slice(lead, (me * n, start), (n, length + 2 * PAD)).astype(F32)
    id_rows = jnp.broadcast_to(ids[:, None, PAD : PAD + length], (n, 8, length))
    ids = jnp.broadcast_to(ids[:, :, None], (n, length + 2 * PAD, LANES))

    pack = jnp.concatenate(
        [
            conv_x,
            gated_gain[None],
            padded_lanes(head_params, width),
            jnp.transpose(timestep_input_weight).astype(F32).reshape(heads * model // width, width),
        ],
        axis=0,
    )
    packs = gathered(pack)
    in_weights = gathered(head_input_weight.reshape(model, 2 * width))
    out_weights = gathered(output_weight)
    small = jnp.stack([jnp.pad(v[6:9, :heads], ((0, 5), (0, LANES - heads))) for v in packs])
    step_weights = [jnp.pad(v[9:].reshape(heads, model).astype(BF16), ((0, LANES - heads), (0, 0))) for v in packs]
    skips = [jnp.repeat(v[8, :heads], HEAD_DIM)[None] for v in packs]
    params = jnp.stack(
        [jnp.concatenate([v[:6], skip, jnp.zeros((1, width), F32)], axis=0) for v, skip in zip(packs, skips)]
    )
    state_taps = jnp.pad(conv_state, ((0, 3), (0, 0)))

    tok_float = padded.astype(F32)
    scale = lax.rsqrt(jnp.mean(tok_float * tok_float, axis=-1, keepdims=True) + EPS)
    normed = (tok_float * scale * norm_gain).astype(BF16)
    gate, rows, raw, state_rows = project(normed, state_input_weight, in_weights, step_weights)
    lane = lax.broadcasted_iota(jnp.int32, (1, 1, 1, LANES), 3) < heads
    step_in = raw + small[:, None, 0:1]
    steps = jnp.where(lane, jax.nn.softplus(step_in), 0.0)
    log_decay = -steps * jnp.exp(small[:, None, 1:2])
    bc = conv_state_call(state_rows, ids, state_taps)
    acted, cum, message = state_call(rows, bc, ids, steps, log_decay, params)
    mixed, states = inside_call(acted, bc, ids, id_rows, steps, cum)
    entered = relay(message, False)
    output, normed_out, d_gate, d_summed, pulled, gain_parts, skip_parts = middle_call(
        mixed, gate, acted, cum, entered, bc, ids, tokens, cotangent, params, message, out_weights, width * blocks
    )
    whole_output = assembled(output)
    leaving = relay(pulled, True)
    d_scaled, d_b, d_c, d_cum = inside_back_call(
        acted, d_summed, mixed, bc, ids, id_rows, steps, cum, states, entered
    )
    d_rows, d_raw, d_b_more, taps_grad, small_grad = close_call(
        rows, acted, d_summed, d_scaled, bc, ids, steps, raw, log_decay, cum, d_cum, leaving, entered, params, small
    )
    d_state, state_taps_grad = conv_state_back_call(state_rows, ids, state_taps, d_b, d_b_more, d_c)
    input_grad, edge, halo, norm_parts = input_call(
        d_gate, d_rows, d_raw, d_state, padded, cotangent, norm_gain[None], state_input_weight, in_weights, step_weights
    )
    halo = lax.ppermute(halo, "seq", [(i + 1, i) for i in range(ranges - 1)])
    edge = (edge + halo.astype(F32)).astype(BF16)
    input_grad = lax.dynamic_update_slice(input_grad, edge, (0, length - PAD, 0))
    whole_input = assembled(input_grad)

    def over_tokens(a, b):
        return jnp.einsum("std,stc->dc", a, b, preferred_element_type=F32)

    plain = normed[:, PAD:]
    out_total = scattered([over_tokens(cotangent, normed_out[r]).astype(BF16) for r in range(blocks)])
    gate_total = scattered([over_tokens(plain, d_gate[r]).astype(BF16) for r in range(blocks)])
    rows_total = scattered([over_tokens(normed, d_rows[r]).astype(BF16) for r in range(blocks)])
    out_grad = jnp.transpose(ranges_sum(out_total))
    heads_grad = jnp.stack([ranges_sum(gate_total), ranges_sum(rows_total)], axis=1)
    state_grad = summed_over(ranges_sum(over_tokens(normed, d_state).astype(BF16)), "head")

    d_raw = d_raw.astype(BF16)
    step_grads = [
        jnp.einsum("sth,std->hd", d_raw[r, :, :, :heads], plain, preferred_element_type=F32) for r in range(blocks)
    ]
    smalls = []
    for r in range(blocks):
        taps = jnp.sum(taps_grad[r], axis=0)[:5]
        gain = jnp.sum(gain_parts[r], axis=0)[None]
        skip = jnp.sum(jnp.sum(skip_parts[r], axis=0).reshape(heads, HEAD_DIM), axis=1)
        rest = jnp.sum(small_grad[r], axis=0)[:2, :heads]
        head_rows = padded_lanes(jnp.concatenate([rest, skip[None]], axis=0), width)
        smalls.append(jnp.concatenate([taps, gain, head_rows, step_grads[r].reshape(-1, width)], axis=0))
    own = summed_over(scattered(smalls), "seq")
    shared = jnp.concatenate(
        [jnp.sum(norm_parts, axis=(0, 1)).reshape(-1, 2 * LANES), jnp.sum(state_taps_grad, axis=0)[:5]], axis=0
    )
    shared = summed_over(summed_over(shared, "head"), "seq")
    count = model // (2 * LANES)
    return (
        whole_output,
        whole_input,
        shared[:count].reshape(model),
        heads_grad,
        state_grad,
        jnp.transpose(own[9:].reshape(heads, model)),
        own[:5],
        shared[count:],
        own[6:9, :heads],
        own[5],
        out_grad,
    )


def solution(mesh):
    return jax.shard_map(
        shards,
        mesh=mesh,
        in_specs=(
            P(None, "seq", None),
            P(),
            P(),
            P(None, None, "head"),
            P(),
            P(None, "head"),
            P(None, "head"),
            P(),
            P(None, "head"),
            P("head"),
            P("head", None),
            P(None, "seq", None),
        ),
        out_specs=(
            P(None, "seq", None),
            P(None, "seq", None),
            P(),
            P("seq", None, "head"),
            P("seq", None),
            P(None, "head"),
            P(None, "head"),
            P(),
            P(None, "head"),
            P("head"),
            P("head", "seq"),
        ),
        check_vma=False,
    )
```

time: 2530 us -> 661 us (0.26)
  waiting for transfers between devices: 1290 us -> 177 us
  other arithmetic: 488 us -> 37.9 us
  matrix products: 376 us -> 44.7 us
  Pallas kernels: 0 us -> 252 us
  local copies, waits for them, and re-layouts: 241 us -> 60 us
  blocking collectives: 59 us -> 0 us
  starting transfers between devices: 49.1 us -> 78 us
    psum x2 -> x0, waiting for transfers between devices: 598 us -> none  [the longest x1 532 us: shards(): branch_path = lax.psum(partial_value, 'head')]
    ppermute x16 -> x39, waiting for transfers between devices: 625 us -> 135 us  [the longest x37 135 us: swapped(): lax.ppermute(value, axis, [(i, i ^ step) for i in range(lax.axis_size(axi...]
    dot_general x37 -> x17, matrix products: 368 us -> 44.7 us  [the longest x13 43.1 us: over_tokens(): return jnp.einsum('std,stc->dc', a, b, preferred_element_type=F32)]
    pallas_call x0 -> x11, Pallas kernels: none -> 252 us  [the longest x1 56.3 us: close_call(): pl.pallas_call(close_kernel, grid=(n, blocks), in_specs=[four(length + PA...]
    another operation x28 -> x4, other arithmetic: 111 us -> 0.75 us  [the longest x2 0.7 us: shards(): jnp.stack([jnp.concatenate([v[:6], skip, jnp.zeros((1, width), F32)], axi...]
    reduce_sum x16 -> x14, other arithmetic: 120 us -> 10.7 us  [the longest x4 4.75 us: ranges_sum(): jnp.sum(arrived.reshape((ranges, value.shape[0] // ranges) + value.shape[...]
    dynamic_update_slice x18 -> x1, other arithmetic: 75 us -> 0.64 us  [shards(): lax.dynamic_update_slice(input_grad, edge, (0, length - PAD, 0))]
    another operation x47 -> x10, local copies, waits for them, and re-layouts: 82 us -> 9.28 us
  transfers between devices with their start and end apart: 21 -> 47, of which waited for: 18 -> 11; matrix products, arithmetic and copies ran while one was open for 9% -> 19% of each run, Pallas kernels for 0% -> 23%
where the time goes in v1:
time: 661 us; the launch traced here: 652 us
  Pallas kernels  252 us (38%)
  waiting for transfers between devices  177 us (27%)
  starting transfers between devices  78 us (12%)
  local copies, waits for them, and re-layouts  60 us (9%)
  matrix products  44.7 us (7%)
  other arithmetic  37.9 us (6%)
    ppermute x37, waiting for transfers between devices, swapped(): lax.ppermute(value, axis, [(i, i ^ step) for i in range(lax.axis_size(axi...  135 us
    pallas_call x1, Pallas kernels, close_call(): pl.pallas_call(close_kernel, grid=(n, blocks), in_specs=[four(length + PA...  56.3 us
    pallas_call x1, Pallas kernels, middle_call(): pl.pallas_call(functools.partial(middle_kernel, blocks, total_width), gri...  51.1 us
    dot_general x13, matrix products, over_tokens(): return jnp.einsum('std,stc->dc', a, b, preferred_element_type=F32)  43.1 us
    pallas_call x1, Pallas kernels, inside_back_call(): pl.pallas_call(inside_back_kernel, grid=(n, blocks), in_specs=[four(lengt...  34 us
    pallas_call x1, Pallas kernels, state_call(): pl.pallas_call(state_kernel, grid=(blocks, n), in_specs=[four(padded, wid...  29.9 us
    ppermute x37, starting transfers between devices, swapped(): lax.ppermute(value, axis, [(i, i ^ step) for i in range(lax.axis_size(axi...  29.2 us
    all_to_all x2, waiting for transfers between devices, relay(): arrived = lax.all_to_all(parts, 'seq', 0, 0, tiled=True)  27.8 us
  transfers between devices with their start and end apart: 47, of which 11 were waited for; matrix products, arithmetic and copies ran while one was open for 19% of the time, Pallas kernels for 23%

profile of v1, /device:TPU:0, one launch (start us, length us, event | category | flops | bytes accessed | tf_op | source)
XLA Modules:
  0.0 651.7 jit_solution(18335654681202851016)
XLA Ops:
  0.7 3.5 copy.88
  4.2 2.9 collective-permute-start.2
  8.7 3.9 collective-permute-start
  16.4 37.4 %collective-permute-done.2.refs_2_ = bf16[1024,1024]{1,0:T(8,128)(2,1)} collective-permute-done((bf16[1024,1024]{1,0:T(8,128)(2,1)}, bf16[1024,1024]{1,0:T(8,128)(2,1)}, u32[]{:S(2)}, u32[]{:S(2)}) %collective-permute-start.2) | collective-permute-done | bytes 2097184 | tf_op jit(solution)/shard_map/ppermute | solution.py:842
  60.5 18.7 %project.1 = (bf16[4,2,512,512]{3,2,1,0:T(8,128)(2,1)}, bf16[4,2,528,512]{3,2,1,0:T(8,128)(2,1)}, f32[4,2,512,128]{3,2,1,0:T(8,128)}, bf16[2,528,256]{2,1,0:T(8,128)(2,1)}) custom-call(bf16[2,528,1024]{2,1,0:T(8,128)(2,1)} %fusion.2.normed, bf16[1024,256]{1,0:T(8,128)(2,1)} %state_w.3, bf16[1024,1024]{1,0:T(8,128)(2,1)} %bitcast.73.refs_0_, ...), custom_call_target="tpu_custom_call" | custom-call | tf_op jit(solution)/shard_map/project/pallas_call | solution.py:155
  80.2 4.5 conv_state.1.bc
  84.8 5.0 negate_multiply_fusion
  89.7 29.9 %range_state.1 = (bf16[4,2,512,512]{3,2,1,0:T(8,128)(2,1)}, f32[4,2,512,128]{3,2,1,0:T(8,128)}, bf16[4,2,144,512]{3,2,1,0:T(8,128)(2,1)}) custom-call(bf16[4,2,528,512]{3,2,1,0:T(8,128)(2,1)} %get-tuple-element.42.rows, bf16[2,512,256]{2,1,0:T(8,128)(2,1)} %conv_state.1.bc, f32[2,544,128]{2,1,0:T(8,128)} %broadcast_in_dim.81.ids, ...), custom_call_target="tpu_custom_call" | custom-call | tf_op jit(solution)/shard_map/range_state/pallas_call | solution.py:245
  119.6 6.1 all-to-all-start
  127.2 27.8 %all-to-all-done.message = bf16[8,144,512]{2,1,0:T(8,128)(2,1)S(1)} async-done(((bf16[8,144,512]{2,1,0:T(8,128)(2,1)}), bf16[8,144,512]{2,1,0:T(8,128)(2,1)S(1)}, u32[]{:S(2)}, u32[]{:S(2)}) %all-to-all-start) | async-done | bytes 1179680 | tf_op jit(solution)/shard_map/all_to_all | solution.py:371
  158.4 4.1 all-to-all-start.1
  163.2 3.1 constant_dynamic-slice_fusion.1.cotangent
  168.5 19.2 %inside.1 = (f32[4,2,512,512]{3,2,1,0:T(8,128)}, bf16[4,2,3,128,512]{4,3,2,1,0:T(8,128)(2,1)}) custom-call(bf16[4,2,512,512]{3,2,1,0:T(8,128)(2,1)} %get-tuple-element.45.acted, bf16[2,512,256]{2,1,0:T(8,128)(2,1)} %conv_state.1.bc, f32[2,544,128]{2,1,0:T(8,128)} %broadcast_in_dim.81.ids, f32[2,8,512]{2,1,0:T(8,128)} %broadcast_in_dim.87.id_rows, ...), custom_call_target="tpu_custom_call" | custom-call | tf_op jit(solution)/shard_map/inside/pallas_call | solution.py:332
  190.3 51.1 %middle.1 = (bf16[2,512,1024]{2,1,0:T(8,128)(2,1)}, bf16[4,2,512,512]{3,2,1,0:T(8,128)(2,1)}, bf16[4,2,512,512]{3,2,1,0:T(8,128)(2,1)}, bf16[4,2,512,512]{3,2,1,...) custom-call(f32[4,2,512,512]{3,2,1,0:T(8,128)} %get-tuple-element.47.mixed, ...), custom_call_target="tpu_custom_call" | custom-call | tf_op jit(solution)/shard_map/middle/pallas_call | solution.py:496
  241.4 3.5 bitcast_convert_fusion
  244.9 5.5 all-to-all-start.2
  250.4 4.3 bitcast_convert_fusion.2
  265.1 34.0 %inside_back.1 = (bf16[4,2,512,512]{3,2,1,0:T(8,128)(2,1)}, f32[2,512,128]{2,1,0:T(8,128)}, f32[2,512,128]{2,1,0:T(8,128)}, f32[4,2,512,128]{3,2,1,0:T(8,128)}) custom-call(bf16[4,2,512,512]{3,2,1,0:T(8,128)(2,1)} %get-tuple-element.45.acted, bf16[4,2,512,512]{3,2,1,0:T(8,128)(2,1)} %get-tuple-element.52.d_summed, ...), custom_call_target="tpu_custom_call" | custom-call | tf_op jit(solution)/shard_map/inside_back/pallas_call | solution.py:606
  299.1 4.5 broadcast.55.clone
  303.6 3.1 constant_dynamic-update-slice_fusion.7
  306.7 3.7 bitcast_convert_fusion.10
  310.6 3.8 add_convert_fusion.1
  318.0 6.0 all-to-all-start.3
  333.3 16.9 %collective-permute-done.38 = bf16[1024,512]{1,0:T(8,128)(2,1)S(1)} collective-permute-done((bf16[1024,512]{1,0:T(8,128)(2,1)}, bf16[1024,512]{1,0:T(8,128)(2,1)S(1)}, u32[]{:S(2)}, u32[]{:S(2)}) %collective-permute-start.38) | collective-permute-done | bytes 1048608 | tf_op jit(solution)/shard_map/ppermute | solution.py:842
  351.6 20.1 %collective-permute-done.24 = bf16[1024,512]{1,0:T(8,128)(2,1)S(1)} collective-permute-done((bf16[1024,512]{1,0:T(8,128)(2,1)S(1)}, bf16[1024,512]{1,0:T(8,128)(2,1)S(1)}, u32[]{:S(2)}, u32[]{:S(2)}) %collective-permute-start.24) | collective-permute-done | bytes 1048608 | tf_op jit(solution)/shard_map/ppermute | solution.py:842
  374.4 3.1 constant_dynamic-update-slice_fusion.6
  377.5 3.1 constant_dynamic-update-slice_fusion.5
  380.6 5.9 all-to-all-start.7
  386.6 56.3 %close.1 = (bf16[4,2,528,512]{3,2,1,0:T(8,128)(2,1)}, f32[4,2,512,128]{3,2,1,0:T(8,128)}, f32[2,512,128]{2,1,0:T(8,128)}, f32[4,2,8,512]{3,2,1,0:T(8,128)}, f32[4,2,8,128]{3,2,1,0:T(8,128)}) custom-call(bf16[4,2,528,512]{3,2,1,0:T(8,128)(2,1)} %get-tuple-element.42.rows, bf16[4,2,512,512]{3,2,1,0:T(8,128)(2,1)} %get-tuple-element.45.acted, ...), custom_call_target="tpu_custom_call" | custom-call | tf_op jit(solution)/shard_map/close/pallas_call | solution.py:707
  447.4 3.8 bitcast_convert_fusion.4
  451.4 3.8 bitcast_convert_fusion.6
  455.5 6.9 %conv_state_back.1 = (bf16[2,528,256]{2,1,0:T(8,128)(2,1)}, f32[2,8,256]{2,1,0:T(8,128)}) custom-call(bf16[2,528,256]{2,1,0:T(8,128)(2,1)} %get-tuple-element.43.rows, f32[2,544,128]{2,1,0:T(8,128)} %broadcast_in_dim.81.ids, f32[8,256]{1,0:T(8,128)} %pad.51.taps, f32[2,512,128]{2,1,0:T(8,128)} %get-tuple-element.59.d_b, ...), custom_call_target="tpu_custom_call" | custom-call | tf_op jit(solution)/shard_map/conv_state_back/pallas_call | solution.py:761
  462.4 26.5 %input_gradient.1 = (bf16[2,512,1024]{2,1,0:T(8,128)(2,1)}, f32[2,16,1024]{2,1,0:T(8,128)}, bf16[2,16,1024]{2,1,0:T(8,128)(2,1)}, f32[2,8,1024]{2,1,0:T(8,128)}) custom-call(bf16[4,2,512,512]{3,2,1,0:T(8,128)(2,1)} %get-tuple-element.51.d_gate, bf16[4,2,528,512]{3,2,1,0:T(8,128)(2,1)} %get-tuple-element.57.d_rows, ...), custom_call_target="tpu_custom_call" | custom-call | tf_op jit(solution)/shard_map/input_gradient/pallas_call | solution.py:821
  491.8 3.8 bitcast_convert_fusion.5
  495.6 7.3 %all-to-all-start.4 = ((bf16[8,128,512]{2,1,0:T(8,128)(2,1)}), bf16[8,128,512]{2,1,0:T(8,128)(2,1)}, u32[]{:S(2)}, u32[]{:S(2)}) async-start(bf16[8,128,512]{2,1,0:T(8,128)(2,1)} %bitcast.165), calls=%async_computation.4 | async-start | bytes 2097152 | tf_op jit(solution)/shard_map/all_to_all | solution.py:873
  512.0 3.8 bitcast_convert_fusion.7
  515.8 13.3 %all-to-all-done.4 = bf16[8,128,512]{2,1,0:T(8,128)(2,1)} async-done(((bf16[8,128,512]{2,1,0:T(8,128)(2,1)}), bf16[8,128,512]{2,1,0:T(8,128)(2,1)}, u32[]{:S(2)}, u32[]{:S(2)}) %all-to-all-start.4) | async-done | bytes 1048608 | tf_op jit(solution)/shard_map/all_to_all | solution.py:873
  529.1 4.1 all-to-all-start.6
  536.5 41.1 %collective-permute-done.18 = f32[9,256]{1,0:T(8,128)S(1)} collective-permute-done((f32[9,256]{1,0:T(8,128)S(1)}, f32[9,256]{1,0:T(8,128)S(1)}, u32[]{:S(2)}, u32[]{:S(2)}) %collective-permute-start.18) | collective-permute-done | bytes 9248 | tf_op jit(solution)/shard_map/ppermute | solution.py:842
  580.3 2.9 add_convert_fusion.3
  583.3 4.6 all-to-all-start.5
  590.3 14.9 %collective-permute-done.20 = f32[9,256]{1,0:T(8,128)S(1)} collective-permute-done((f32[9,256]{1,0:T(8,128)S(1)}, f32[9,256]{1,0:T(8,128)S(1)}, u32[]{:S(2)}, u32[]{:S(2)}) %collective-permute-start.20) | collective-permute-done | bytes 9248 | tf_op jit(solution)/shard_map/ppermute | solution.py:842
  607.1 4.7 collective-permute-start.21
  625.6 4.5 broadcast.55.clone.1
  630.0 3.1 constant_dynamic-update-slice_fusion.3
  636.8 3.1 constant_dynamic-update-slice_fusion.4
  642.2 3.1 constant_dynamic-update-slice_fusion.2
  645.3 3.1 constant_dynamic-update-slice_fusion.1
  (279 shorter events, 100.8 us)
Async XLA Ops:
  4.2 49.6 %collective-permute-start.2 = (bf16[1024,1024]{1,0:T(8,128)(2,1)}, bf16[1024,1024]{1,0:T(8,128)(2,1)}, u32[]{:S(2)}, u32[]{:S(2)}) collective-permute-start(bf16[1024,1024]{1,0:T(8,128)(2,1)} %bitcast.73.refs_0_), channel_id=1, source_target_pairs={{0,2},{1,3},{2,0},{3,1},{4,6},{5,7},{6,4},{7,5},{8,10},{9,11},{10,... | collective-permute-start | bytes 6291464 | tf_op jit(solution)/shard_map/ppermute | solution.py:842
  7.2 47.2 %collective-permute-start.5 = (f32[25,512]{1,0:T(8,128)S(1)}, f32[25,512]{1,0:T(8,128)S(1)}, u32[]{:S(2)}, u32[]{:S(2)}) collective-permute-start(f32[25,512]{1,0:T(8,128)S(1)} %fusion.38), channel_id=1, source_target_pairs={{0,2},{1,3},{2,0},{3,1},{4,6},{5,7},{6,4},{7,5},{8,10},{9,11},{10,... | collective-permute-start | bytes 153608 | tf_op jit(solution)/shard_map/ppermute | solution.py:842
  7.3 47.1 %collective-permute-start.4 = (f32[25,512]{1,0:T(8,128)S(1)}, f32[25,512]{1,0:T(8,128)S(1)}, u32[]{:S(2)}, u32[]{:S(2)}) collective-permute-start(f32[25,512]{1,0:T(8,128)S(1)} %fusion.38), channel_id=1, source_target_pairs={{0,1},{1,0},{2,3},{3,2},{4,5},{5,4},{6,7},{7,6},{8,9},{9,8},{10,11... | collective-permute-start | bytes 153608 | tf_op jit(solution)/shard_map/ppermute | solution.py:842
  7.4 53.1 %collective-permute-start.1 = (bf16[1024,1024]{1,0:T(8,128)(2,1)}, bf16[1024,1024]{1,0:T(8,128)(2,1)}, u32[]{:S(2)}, u32[]{:S(2)}) collective-permute-start(bf16[1024,1024]{1,0:T(8,128)(2,1)} %bitcast.73.refs_0_), channel_id=1, source_target_pairs={{0,1},{1,0},{2,3},{3,2},{4,5},{5,4},{6,7},{7,6},{8,9},{9,8},{10,11... | collective-permute-start | bytes 6291464 | tf_op jit(solution)/shard_map/ppermute | solution.py:842
  8.7 47.6 %collective-permute-start = (bf16[2,16,1024]{2,1,0:T(8,128)(2,1)S(1)}, bf16[2,16,1024]{2,1,0:T(8,128)(2,1)S(1)}, u32[]{:S(2)}, u32[]{:S(2)}) collective-permute-start(bf16[2,16,1024]{2,1,0:T(8,128)(2,1)S(1)} %constant_dynamic-slice_fusion), channel_id=1, source_target_pairs={{0,4},{4,8},{8,12},{12,16},{16,20},{20,24},{24,28},{1,5},{5,9},{9,... | collective-permute-start | bytes 196616 | tf_op jit(solution)/shard_map/ppermute | solution.py:913
  14.6 151.7 %copy-start.1 = (bf16[2,512,1024]{2,1,0:T(8,128)(2,1)}, bf16[2,512,1024]{2,1,0:T(8,128)(2,1)S(1)}, u32[]{:S(2)}) copy-start(bf16[2,512,1024]{2,1,0:T(8,128)(2,1)S(1)} %constant_dynamic-slice_fusion.2.tokens) | copy-start | bytes 6291460
  53.8 6.7 %collective-permute-start.3 = (bf16[1024,1024]{1,0:T(8,128)(2,1)}, bf16[1024,1024]{1,0:T(8,128)(2,1)}, u32[]{:S(2)}, u32[]{:S(2)}) collective-permute-start(bf16[1024,1024]{1,0:T(8,128)(2,1)} %collective-permute-done.2.refs_2_), channel_id=1, source_target_pairs={{0,1},{1,0},{2,3},{3,2},{4,5},{5,4},{6,7},{7,6},{8,9},{9,8},{10,11... | collective-permute-start | bytes 6291464 | tf_op jit(solution)/shard_map/ppermute | solution.py:842
  56.2 2.6 collective-permute-start.6
  119.6 35.3 %all-to-all-start = ((bf16[8,144,512]{2,1,0:T(8,128)(2,1)}), bf16[8,144,512]{2,1,0:T(8,128)(2,1)S(1)}, u32[]{:S(2)}, u32[]{:S(2)}) async-start(bf16[8,144,512]{2,1,0:T(8,128)(2,1)} %bitcast.163), calls=%async_computation | async-start | bytes 2359296 | tf_op jit(solution)/shard_map/all_to_all | solution.py:371
  125.7 36.9 %collective-permute-start.8 = (bf16[512,1024]{1,0:T(8,128)(2,1)}, bf16[512,1024]{1,0:T(8,128)(2,1)}, u32[]{:S(2)}, u32[]{:S(2)}) collective-permute-start(bf16[512,1024]{1,0:T(8,128)(2,1)} %refs_0_.1), channel_id=1, source_target_pairs={{0,2},{1,3},{2,0},{3,1},{4,6},{5,7},{6,4},{7,5},{8,10},{9,11},{10,... | collective-permute-start | bytes 3145736 | tf_op jit(solution)/shard_map/ppermute | solution.py:842
  158.4 30.1 %all-to-all-start.1 = ((bf16[8,128,512]{2,1,0:T(8,128)(2,1)}), bf16[8,128,512]{2,1,0:T(8,128)(2,1)S(1)}, u32[]{:S(2)}, u32[]{:S(2)}) async-start(bf16[8,128,512]{2,1,0:T(8,128)(2,1)} %relay.2), calls=%async_computation.1 | async-start | bytes 2097152 | tf_op jit(solution)/shard_map/all_to_all | solution.py:377
  162.5 25.2 %collective-permute-start.7 = (bf16[512,1024]{1,0:T(8,128)(2,1)}, bf16[512,1024]{1,0:T(8,128)(2,1)}, u32[]{:S(2)}, u32[]{:S(2)}) collective-permute-start(bf16[512,1024]{1,0:T(8,128)(2,1)} %refs_0_.1), channel_id=1, source_target_pairs={{0,1},{1,0},{2,3},{3,2},{4,5},{5,4},{6,7},{7,6},{8,9},{9,8},{10,11... | collective-permute-start | bytes 3145736 | tf_op jit(solution)/shard_map/ppermute | solution.py:842
  162.6 25.1 %collective-permute-start.9 = (bf16[512,1024]{1,0:T(8,128)(2,1)}, bf16[512,1024]{1,0:T(8,128)(2,1)}, u32[]{:S(2)}, u32[]{:S(2)}) collective-permute-start(bf16[512,1024]{1,0:T(8,128)(2,1)} %collective-permute-done.8.refs_2_), channel_id=1, source_target_pairs={{0,1},{1,0},{2,3},{3,2},{4,5},{5,4},{6,7},{7,6},{8,9},{9,8},{10,11... | collective-permute-start | bytes 3145736 | tf_op jit(solution)/shard_map/ppermute | solution.py:842
  244.9 69.5 %all-to-all-start.2 = ((bf16[8,144,512]{2,1,0:T(8,128)(2,1)}), bf16[8,144,512]{2,1,0:T(8,128)(2,1)S(1)}, u32[]{:S(2)}, u32[]{:S(2)}) async-start(bf16[8,144,512]{2,1,0:T(8,128)(2,1)} %bitcast.167), calls=%async_computation.2 | async-start | bytes 2359296 | tf_op jit(solution)/shard_map/all_to_all | solution.py:371
  254.7 119.7 %collective-permute-start.10 = (bf16[2,512,1024]{2,1,0:T(8,128)(2,1)}, bf16[2,512,1024]{2,1,0:T(8,128)(2,1)}, u32[]{:S(2)}, u32[]{:S(2)}) collective-permute-start(bf16[2,512,1024]{2,1,0:T(8,128)(2,1)} %get-tuple-element.50), channel_id=1, source_target_pairs={{0,1},{1,0},{2,3},{3,2},{4,5},{5,4},{6,7},{7,6},{8,9},{9,8},{10,11... | collective-permute-start | bytes 6291464 | tf_op jit(solution)/shard_map/ppermute | solution.py:842
  254.7 119.7 %collective-permute-start.11 = (bf16[2,512,1024]{2,1,0:T(8,128)(2,1)}, bf16[2,512,1024]{2,1,0:T(8,128)(2,1)}, u32[]{:S(2)}, u32[]{:S(2)}) collective-permute-start(bf16[2,512,1024]{2,1,0:T(8,128)(2,1)} %get-tuple-element.50), channel_id=1, source_target_pairs={{0,2},{1,3},{2,0},{3,1},{4,6},{5,7},{6,4},{7,5},{8,10},{9,11},{10,... | collective-permute-start | bytes 6291464 | tf_op jit(solution)/shard_map/ppermute | solution.py:842
  256.2 54.2 %collective-permute-start.37 = (bf16[1024,512]{1,0:T(8,128)(2,1)}, bf16[1024,512]{1,0:T(8,128)(2,1)}, u32[]{:S(2)}, u32[]{:S(2)}) collective-permute-start(bf16[1024,512]{1,0:T(8,128)(2,1)} %bitcast_convert_fusion), channel_id=1, source_target_pairs={{0,1},{1,0},{2,3},{3,2},{4,5},{5,4},{6,7},{7,6},{8,9},{9,8},{10,11... | collective-permute-start | bytes 3145736 | tf_op jit(solution)/shard_map/ppermute | solution.py:842
  256.4 70.0 %collective-permute-start.36 = (bf16[1024,512]{1,0:T(8,128)(2,1)}, bf16[1024,512]{1,0:T(8,128)(2,1)}, u32[]{:S(2)}, u32[]{:S(2)}) collective-permute-start(bf16[1024,512]{1,0:T(8,128)(2,1)} %bitcast_convert_fusion.2), channel_id=1, source_target_pairs={{0,1},{1,0},{2,3},{3,2},{4,5},{5,4},{6,7},{7,6},{8,9},{9,8},{10,11... | collective-permute-start | bytes 3145736 | tf_op jit(solution)/shard_map/ppermute | solution.py:842
  259.0 64.9 %collective-permute-start.23 = (bf16[1024,512]{1,0:T(8,128)(2,1)}, bf16[1024,512]{1,0:T(8,128)(2,1)}, u32[]{:S(2)}, u32[]{:S(2)}) collective-permute-start(bf16[1024,512]{1,0:T(8,128)(2,1)} %bitcast_convert_fusion.8), channel_id=1, source_target_pairs={{0,1},{1,0},{2,3},{3,2},{4,5},{5,4},{6,7},{7,6},{8,9},{9,8},{10,11... | collective-permute-start | bytes 3145736 | tf_op jit(solution)/shard_map/ppermute | solution.py:842
  310.3 41.2 %collective-permute-start.22 = (bf16[1024,512]{1,0:T(8,128)(2,1)}, bf16[1024,512]{1,0:T(8,128)(2,1)}, u32[]{:S(2)}, u32[]{:S(2)}) collective-permute-start(bf16[1024,512]{1,0:T(8,128)(2,1)} %bitcast_convert_fusion.10), channel_id=1, source_target_pairs={{0,1},{1,0},{2,3},{3,2},{4,5},{5,4},{6,7},{7,6},{8,9},{9,8},{10,11... | collective-permute-start | bytes 3145736 | tf_op jit(solution)/shard_map/ppermute | solution.py:842
  318.0 62.6 %all-to-all-start.3 = ((bf16[8,128,512]{2,1,0:T(8,128)(2,1)}), bf16[8,128,512]{2,1,0:T(8,128)(2,1)S(1)}, u32[]{:S(2)}, u32[]{:S(2)}) async-start(bf16[8,128,512]{2,1,0:T(8,128)(2,1)} %relay.3), calls=%async_computation.3 | async-start | bytes 2097152 | tf_op jit(solution)/shard_map/all_to_all | solution.py:377
  324.0 26.3 %collective-permute-start.38 = (bf16[1024,512]{1,0:T(8,128)(2,1)}, bf16[1024,512]{1,0:T(8,128)(2,1)S(1)}, u32[]{:S(2)}, u32[]{:S(2)}) collective-permute-start(bf16[1024,512]{1,0:T(8,128)(2,1)} %add_convert_fusion.1), channel_id=1, source_target_pairs={{0,2},{1,3},{2,0},{3,1},{4,6},{5,7},{6,4},{7,5},{8,10},{9,11},{10,... | collective-permute-start | bytes 3145736 | tf_op jit(solution)/shard_map/ppermute | solution.py:842
  326.4 45.3 %collective-permute-start.24 = (bf16[1024,512]{1,0:T(8,128)(2,1)S(1)}, bf16[1024,512]{1,0:T(8,128)(2,1)S(1)}, u32[]{:S(2)}, u32[]{:S(2)}) collective-permute-start(bf16[1024,512]{1,0:T(8,128)(2,1)S(1)} %add_convert_fusion.7), channel_id=1, source_target_pairs={{0,2},{1,3},{2,0},{3,1},{4,6},{5,7},{6,4},{7,5},{8,10},{9,11},{10,... | collective-permute-start | bytes 3145736 | tf_op jit(solution)/shard_map/ppermute | solution.py:842
  374.4 262.4 %collective-permute-start.12 = (bf16[2,512,1024]{2,1,0:T(8,128)(2,1)}, bf16[2,512,1024]{2,1,0:T(8,128)(2,1)}, u32[]{:S(2)}, u32[]{:S(2)}) collective-permute-start(bf16[2,512,1024]{2,1,0:T(8,128)(2,1)} %collective-permute-done.11), channel_id=1, source_target_pairs={{0,1},{1,0},{2,3},{3,2},{4,5},{5,4},{6,7},{7,6},{8,9},{9,8},{10,11... | collective-permute-start | bytes 6291464 | tf_op jit(solution)/shard_map/ppermute | solution.py:842
  380.6 115.0 %all-to-all-start.7 = ((bf16[8,128,512]{2,1,0:T(8,128)(2,1)}), bf16[8,128,512]{2,1,0:T(8,128)(2,1)}, u32[]{:S(2)}, u32[]{:S(2)}) async-start(bf16[8,128,512]{2,1,0:T(8,128)(2,1)} %bitcast.69), calls=%async_computation.7 | async-start | bytes 2097152 | tf_op jit(solution)/shard_map/all_to_all | solution.py:873
  451.2 56.9 %collective-permute-start.26 = (bf16[1024,512]{1,0:T(8,128)(2,1)}, bf16[1024,512]{1,0:T(8,128)(2,1)}, u32[]{:S(2)}, u32[]{:S(2)}) collective-permute-start(bf16[1024,512]{1,0:T(8,128)(2,1)} %bitcast_convert_fusion.4), channel_id=1, source_target_pairs={{0,1},{1,0},{2,3},{3,2},{4,5},{5,4},{6,7},{7,6},{8,9},{9,8},{10,11... | collective-permute-start | bytes 3145736 | tf_op jit(solution)/shard_map/ppermute | solution.py:842
  455.1 122.8 %collective-permute-start.25 = (bf16[1024,512]{1,0:T(8,128)(2,1)}, bf16[1024,512]{1,0:T(8,128)(2,1)}, u32[]{:S(2)}, u32[]{:S(2)}) collective-permute-start(bf16[1024,512]{1,0:T(8,128)(2,1)} %bitcast_convert_fusion.6), channel_id=1, source_target_pairs={{0,1},{1,0},{2,3},{3,2},{4,5},{5,4},{6,7},{7,6},{8,9},{9,8},{10,11... | collective-permute-start | bytes 3145736 | tf_op jit(solution)/shard_map/ppermute | solution.py:842
  489.8 44.7 %collective-permute-start.17 = (f32[9,256]{1,0:T(8,128)S(1)}, f32[9,256]{1,0:T(8,128)S(1)}, u32[]{:S(2)}, u32[]{:S(2)}) collective-permute-start(f32[9,256]{1,0:T(8,128)S(1)} %pad_maximum_fusion.6), channel_id=1, source_target_pairs={{0,1},{1,0},{2,3},{3,2},{4,5},{5,4},{6,7},{7,6},{8,9},{9,8},{10,11... | collective-permute-start | bytes 27656 | tf_op jit(solution)/shard_map/ppermute | solution.py:842
  490.1 16.4 %collective-permute-start.13 = (bf16[2,16,1024]{2,1,0:T(8,128)(2,1)}, bf16[2,16,1024]{2,1,0:T(8,128)(2,1)S(1)}, u32[]{:S(2)}, u32[]{:S(2)}) collective-permute-start(bf16[2,16,1024]{2,1,0:T(8,128)(2,1)} %get-tuple-element.65), channel_id=1, source_target_pairs={{4,0},{8,4},{12,8},{16,12},{20,16},{24,20},{28,24},{5,1},{9,5},{13... | collective-permute-start | bytes 196616 | tf_op jit(solution)/shard_map/ppermute | solution.py:971
  495.6 33.5 %all-to-all-start.4 = ((bf16[8,128,512]{2,1,0:T(8,128)(2,1)}), bf16[8,128,512]{2,1,0:T(8,128)(2,1)}, u32[]{:S(2)}, u32[]{:S(2)}) async-start(bf16[8,128,512]{2,1,0:T(8,128)(2,1)} %bitcast.165), calls=%async_computation.4 | async-start | bytes 2097152 | tf_op jit(solution)/shard_map/all_to_all | solution.py:873
  507.1 83.0 %collective-permute-start.15 = (bf16[2,512,1024]{2,1,0:T(8,128)(2,1)}, bf16[2,512,1024]{2,1,0:T(8,128)(2,1)}, u32[]{:S(2)}, u32[]{:S(2)}) collective-permute-start(bf16[2,512,1024]{2,1,0:T(8,128)(2,1)} %fusion.37), channel_id=1, source_target_pairs={{0,2},{1,3},{2,0},{3,1},{4,6},{5,7},{6,4},{7,5},{8,10},{9,11},{10,... | collective-permute-start | bytes 6291464 | tf_op jit(solution)/shard_map/ppermute | solution.py:842
  510.6 68.0 %collective-permute-start.27 = (bf16[1024,512]{1,0:T(8,128)(2,1)}, bf16[1024,512]{1,0:T(8,128)(2,1)}, u32[]{:S(2)}, u32[]{:S(2)}) collective-permute-start(bf16[1024,512]{1,0:T(8,128)(2,1)} %add_convert_fusion.4), channel_id=1, source_target_pairs={{0,2},{1,3},{2,0},{3,1},{4,6},{5,7},{6,4},{7,5},{8,10},{9,11},{10,... | collective-permute-start | bytes 3145736 | tf_op jit(solution)/shard_map/ppermute | solution.py:842
  529.1 54.2 %all-to-all-start.6 = ((bf16[8,128,256]{2,1,0:T(8,128)(2,1)}), bf16[8,128,256]{2,1,0:T(8,128)(2,1)}, u32[]{:S(2)}, u32[]{:S(2)}) async-start(bf16[8,128,256]{2,1,0:T(8,128)(2,1)} %bitcast.171), calls=%async_computation.6 | async-start | bytes 1048576 | tf_op jit(solution)/shard_map/all_to_all | solution.py:873
  534.6 43.0 %collective-permute-start.18 = (f32[9,256]{1,0:T(8,128)S(1)}, f32[9,256]{1,0:T(8,128)S(1)}, u32[]{:S(2)}, u32[]{:S(2)}) collective-permute-start(f32[9,256]{1,0:T(8,128)S(1)} %fusion.41), channel_id=1, source_target_pairs={{0,2},{1,3},{2,0},{3,1},{4,6},{5,7},{6,4},{7,5},{8,10},{9,11},{10,... | collective-permute-start | bytes 27656 | tf_op jit(solution)/shard_map/ppermute | solution.py:842
  577.6 64.6 %collective-permute-start.14 = (bf16[2,512,1024]{2,1,0:T(8,128)(2,1)}, bf16[2,512,1024]{2,1,0:T(8,128)(2,1)}, u32[]{:S(2)}, u32[]{:S(2)}) collective-permute-start(bf16[2,512,1024]{2,1,0:T(8,128)(2,1)} %fusion.37), channel_id=1, source_target_pairs={{0,1},{1,0},{2,3},{3,2},{4,5},{5,4},{6,7},{7,6},{8,9},{9,8},{10,11... | collective-permute-start | bytes 6291464 | tf_op jit(solution)/shard_map/ppermute | solution.py:842
  578.0 10.0 %collective-permute-start.31 = (f32[25,512]{1,0:T(8,128)}, f32[25,512]{1,0:T(8,128)S(1)}, u32[]{:S(2)}, u32[]{:S(2)}) collective-permute-start(f32[25,512]{1,0:T(8,128)} %pad_maximum_fusion.4), channel_id=1, source_target_pairs={{0,1},{1,0},{2,3},{3,2},{4,5},{5,4},{6,7},{7,6},{8,9},{9,8},{10,11... | collective-permute-start | bytes 153608 | tf_op jit(solution)/shard_map/ppermute | solution.py:842
  578.6 9.3 %collective-permute-start.19 = (f32[9,256]{1,0:T(8,128)S(1)}, f32[9,256]{1,0:T(8,128)S(1)}, u32[]{:S(2)}, u32[]{:S(2)}) collective-permute-start(f32[9,256]{1,0:T(8,128)S(1)} %add.157), channel_id=1, source_target_pairs={{0,4},{4,0},{8,12},{12,8},{16,20},{20,16},{24,28},{28,24},{1,5},{5... | collective-permute-start | bytes 27656 | tf_op jit(solution)/shard_map/ppermute | solution.py:842
  583.3 65.1 %all-to-all-start.5 = ((bf16[8,128,512]{2,1,0:T(8,128)(2,1)}), bf16[8,128,512]{2,1,0:T(8,128)(2,1)S(1)}, u32[]{:S(2)}, u32[]{:S(2)}) async-start(bf16[8,128,512]{2,1,0:T(8,128)(2,1)} %bitcast.39), calls=%async_computation.5 | async-start | bytes 2097152 | tf_op jit(solution)/shard_map/all_to_all | solution.py:873
  587.9 19.3 %collective-permute-start.30 = (f32[25,512]{1,0:T(8,128)}, f32[25,512]{1,0:T(8,128)S(1)}, u32[]{:S(2)}, u32[]{:S(2)}) collective-permute-start(f32[25,512]{1,0:T(8,128)} %pad_maximum_fusion.3), channel_id=1, source_target_pairs={{0,1},{1,0},{2,3},{3,2},{4,5},{5,4},{6,7},{7,6},{8,9},{9,8},{10,11... | collective-permute-start | bytes 153608 | tf_op jit(solution)/shard_map/ppermute | solution.py:842
  588.0 17.2 %collective-permute-start.20 = (f32[9,256]{1,0:T(8,128)S(1)}, f32[9,256]{1,0:T(8,128)S(1)}, u32[]{:S(2)}, u32[]{:S(2)}) collective-permute-start(f32[9,256]{1,0:T(8,128)S(1)} %add.158), channel_id=1, source_target_pairs={{0,8},{4,12},{8,0},{12,4},{16,24},{20,28},{24,16},{28,20},{1,9},{5... | collective-permute-start | bytes 27656 | tf_op jit(solution)/shard_map/ppermute | solution.py:842
  590.1 59.7 %collective-permute-start.16 = (bf16[2,512,1024]{2,1,0:T(8,128)(2,1)}, bf16[2,512,1024]{2,1,0:T(8,128)(2,1)S(1)}, u32[]{:S(2)}, u32[]{:S(2)}) collective-permute-start(bf16[2,512,1024]{2,1,0:T(8,128)(2,1)} %collective-permute-done.15), channel_id=1, source_target_pairs={{0,1},{1,0},{2,3},{3,2},{4,5},{5,4},{6,7},{7,6},{8,9},{9,8},{10,11... | collective-permute-start | bytes 6291464 | tf_op jit(solution)/shard_map/ppermute | solution.py:842
  605.1 6.7 %collective-permute-start.32 = (f32[25,512]{1,0:T(8,128)S(1)}, f32[25,512]{1,0:T(8,128)S(1)}, u32[]{:S(2)}, u32[]{:S(2)}) collective-permute-start(f32[25,512]{1,0:T(8,128)S(1)} %maximum_add_fusion.1), channel_id=1, source_target_pairs={{0,2},{1,3},{2,0},{3,1},{4,6},{5,7},{6,4},{7,5},{8,10},{9,11},{10,... | collective-permute-start | bytes 153608 | tf_op jit(solution)/shard_map/ppermute | solution.py:842
  607.1 9.9 %collective-permute-start.21 = (f32[9,256]{1,0:T(8,128)S(1)}, f32[9,256]{1,0:T(8,128)}, u32[]{:S(2)}, u32[]{:S(2)}) collective-permute-start(f32[9,256]{1,0:T(8,128)S(1)} %add.159), channel_id=1, source_target_pairs={{0,16},{4,20},{8,24},{12,28},{16,0},{20,4},{24,8},{28,12},{1,17},{... | collective-permute-start | bytes 27656 | tf_op jit(solution)/shard_map/ppermute | solution.py:842
  612.6 5.2 collective-permute-start.33
  617.7 4.3 collective-permute-start.34
  622.1 11.0 %collective-permute-start.35 = (f32[25,512]{1,0:T(8,128)S(1)}, f32[25,512]{1,0:T(8,128)S(1)}, u32[]{:S(2)}, u32[]{:S(2)}) collective-permute-start(f32[25,512]{1,0:T(8,128)S(1)} %add.173), channel_id=1, source_target_pairs={{0,16},{4,20},{8,24},{12,28},{16,0},{20,4},{24,8},{28,12},{1,17},{... | collective-permute-start | bytes 153608 | tf_op jit(solution)/shard_map/ppermute | solution.py:842
  625.5 10.1 %collective-permute-start.28 = (f32[128,256]{1,0:T(8,128)S(1)}, f32[128,256]{1,0:T(8,128)S(1)}, u32[]{:S(2)}, u32[]{:S(2)}) collective-permute-start(f32[128,256]{1,0:T(8,128)S(1)} %convert_reduce_fusion.3), channel_id=1, source_target_pairs={{0,1},{1,0},{2,3},{3,2},{4,5},{5,4},{6,7},{7,6},{8,9},{9,8},{10,11... | collective-permute-start | bytes 393224 | tf_op jit(solution)/shard_map/ppermute | solution.py:842
  635.6 6.0 collective-permute-start.29
  (35 other events, 536.2 us)

commit v2 on v1

v2 whole, which is shorter than its diff:
```python
import functools

import jax
import jax.numpy as jnp
from jax import lax
from jax.experimental import pallas as pl
from jax.experimental.pallas import tpu as pltpu
from jax.sharding import PartitionSpec as P

F32 = jnp.float32
BF16 = jnp.bfloat16
EPS = 1e-5
CHUNK = 128
PAD = 16
LANES = 128
HEAD_DIM = 64
VMEM = 60 * 1024 * 1024


def dot(a, b):
    return lax.dot_general(a, b, (((1,), (0,)), ((), ())), preferred_element_type=F32)


def dot_nt(a, b):
    return lax.dot_general(a, b, (((1,), (1,)), ((), ())), preferred_element_type=F32)


def dot_tn(a, b):
    return lax.dot_general(a, b, (((0,), (0,)), ((), ())), preferred_element_type=F32)


def split(value):
    high = value.astype(BF16)
    return high, (value - high.astype(F32)).astype(BF16)


def head_map(width, offset):
    lane = lax.broadcasted_iota(jnp.int32, (LANES, width), 1)
    row = lax.broadcasted_iota(jnp.int32, (LANES, width), 0)
    return (lax.shift_right_logical(lane, 6) + offset == row).astype(F32).astype(BF16)


def expand(value, width, offset):
    lane = lax.shift_right_logical(lax.broadcasted_iota(jnp.int32, value.shape, 1), 6) + offset
    return jnp.concatenate(
        [jnp.take_along_axis(value, lane + 2 * p, axis=1) for p in range(width // LANES)], axis=1
    )


def expand_row(value, width, offset):
    return expand(jnp.broadcast_to(value, (8, LANES)), width, offset)


def column(value, index):
    return jnp.take_along_axis(value, jnp.zeros(value.shape, jnp.int32) + index, axis=1)


def by_head(value, heads):
    high, low = split(value)
    return dot_nt(high, heads) + dot_nt(low, heads)


def by_head_low(value, heads):
    return dot_nt(value.astype(BF16), heads)


def widen(value, width):
    return jnp.concatenate([value] * (width // LANES), axis=1)


def fold8(value):
    return value[0:8] + value[8:16]


def sigmoid(value):
    return 0.5 * jnp.tanh(0.5 * value) + 0.5


def triangle(lower):
    row = lax.broadcasted_iota(jnp.int32, (CHUNK, CHUNK), 0)
    column = lax.broadcasted_iota(jnp.int32, (CHUNK, CHUNK), 1)
    return (row >= column if lower else row <= column)


def exact_dot(ones, value):
    return jnp.dot(ones, value, precision=lax.Precision.HIGHEST, preferred_element_type=F32)


def rows_at(start, count):
    return pl.ds(pl.multiple_of(start, 16), count)


def entering_maps(columns, rows, first, count):
    window = count + PAD
    token = lax.broadcasted_iota(jnp.int32, (count, window), 0)
    entry = lax.broadcasted_iota(jnp.int32, (count, window), 1)
    same = wide_marks(columns[0, first : first + count, :], window) == rows[0, 0:1, first - PAD : first + count]
    distance = entry - token
    return jnp.concatenate(
        [jnp.where(same & (distance == PAD - 3 + k), 1.0, 0.0).astype(BF16) for k in range(3)], axis=0
    )


def leaving_maps(columns, rows, first, count):
    window = count + PAD
    row = lax.broadcasted_iota(jnp.int32, (count, window), 0)
    token = lax.broadcasted_iota(jnp.int32, (count, window), 1)
    same = wide_marks(columns[0, first : first + count, :], window) == rows[0, 0:1, first : first + window]
    distance = token - row
    return jnp.concatenate(
        [jnp.where(same & (distance == 3 - k), 1.0, 0.0).astype(BF16) for k in range(3)], axis=0
    )


def wide_marks(columns, window):
    whole = jnp.concatenate([columns] * -(-window // LANES), axis=1)
    return whole[:, :window]


def conv_sum(rows, maps, taps, first, lanes):
    moved = dot(maps, rows[first - PAD : first + CHUNK, lanes])
    entering = [moved[k * CHUNK : (k + 1) * CHUNK] for k in range(3)]
    entering.append(rows[first : first + CHUNK, lanes].astype(F32))
    total = taps[4:5, lanes]
    for k in range(4):
        total = total + taps[k : k + 1, lanes] * entering[k]
    return total, entering


def lane_groups(width):
    step = min(width, 2 * LANES)
    return [slice(i, i + step) for i in range(0, width, step)]


def conv_forward(rows, ids, id_rows, taps, store, length):
    for c in range(length // CHUNK):
        first = PAD + c * CHUNK
        maps = entering_maps(ids, id_rows, first, CHUNK)
        for lanes in lane_groups(rows.shape[1]):
            total, _ = conv_sum(rows, maps, taps, first, lanes)
            store(slice(c * CHUNK, (c + 1) * CHUNK), lanes, (total * sigmoid(total)).astype(BF16))


def conv_backward(rows, ids, id_rows, taps, d_acted, d_pre, d_rows, length):
    width = d_pre.shape[1]
    zero = jnp.zeros((16, width), BF16)
    d_pre[0:16, :] = zero
    d_pre[length + PAD : length + PAD + 16, :] = zero
    groups = lane_groups(width)
    sums = [[jnp.zeros((8, g.stop - g.start), F32) for _ in range(5)] for g in groups]
    for c in range(length // CHUNK - 1, -1, -1):
        first = PAD + c * CHUNK
        here = slice(first, first + CHUNK)
        maps = entering_maps(ids, id_rows, first, CHUNK)
        back = leaving_maps(ids, id_rows, first, CHUNK)
        for i, lanes in enumerate(groups):
            total, entering = conv_sum(rows, maps, taps, first, lanes)
            sigma = sigmoid(total)
            grad = d_acted(c, lanes) * (sigma * (1.0 + total * (1.0 - sigma)))
            d_pre[here, lanes] = grad.astype(BF16)
            for k in range(5):
                product = grad * entering[k] if k < 4 else grad
                sums[i][k] = sums[i][k] + jnp.sum(product.reshape(CHUNK // 8, 8, -1), axis=0)
            moved = dot(back, d_pre[first : first + CHUNK + PAD, lanes])
            result = taps[3:4, lanes] * grad
            for k in range(3):
                result = result + taps[k : k + 1, lanes] * moved[k * CHUNK : (k + 1) * CHUNK]
            d_rows(here, lanes, result.astype(BF16))
    back = leaving_maps(ids, id_rows, 0, PAD)
    for lanes in groups:
        moved = dot(back, d_pre[0 : 2 * PAD, lanes])
        result = taps[0:1, lanes] * moved[0:PAD]
        for k in range(1, 3):
            result = result + taps[k : k + 1, lanes] * moved[k * PAD : (k + 1) * PAD]
        d_rows(slice(0, PAD), lanes, result.astype(BF16))
    return [
        jnp.concatenate([jnp.sum(part[k], axis=0, keepdims=True) for part in sums], axis=1) for k in range(5)
    ]


def softplus(value):
    return jnp.maximum(value, 0.0) + jnp.log1p(jnp.exp(-jnp.abs(value)))


def project_rows(values, weights, rows):
    for r, weight in enumerate(weights):
        rows[r, 0] = dot(values, weight[...]).astype(BF16)


def project_first_kernel(blocks, heads, normed, state_w, step_w, small, ids, id_rows, taps, *refs):
    weights, refs = refs[:blocks], refs[blocks:]
    rows, raw, steps, log_decay, cum, state_rows, bc = refs
    length = bc.shape[1]
    values = normed[0]
    state_rows[0] = dot(values, state_w[...]).astype(BF16)
    part = dot_nt(values[PAD:], step_w[...])
    raw[0] = part
    lane = lax.broadcasted_iota(jnp.int32, (length, LANES), 1)
    size = jnp.where(lane < heads, softplus(part + small[0:1, :]), 0.0)
    steps[0] = size
    log_decay[0] = -size * jnp.exp(small[1:2, :])
    ones = triangle(True).astype(F32)
    total = jnp.zeros((1, LANES), F32)
    for c in range(length // CHUNK):
        here = slice(c * CHUNK, (c + 1) * CHUNK)
        value = exact_dot(ones, log_decay[0, here, :]) + total
        cum[0, here, :] = value
        total = value[CHUNK - 1 : CHUNK]

    def store(here, lanes, value):
        bc[0, here, lanes] = value

    conv_forward(state_rows.at[0], ids, id_rows, taps[...], store, length)
    project_rows(values, weights, rows)


def project_more_kernel(blocks, normed, held, *refs):
    project_rows(normed[0], refs[:blocks], refs[blocks])


def project_first(normed, state_w, step_w, small, ids, id_rows, taps, weights, blocks, heads):
    n, padded, model = normed.shape
    width = weights[0].shape[1]
    length = padded - PAD
    whole = lambda a: pl.BlockSpec(a.shape, lambda s: (0,) * a.ndim, pipeline_mode=pl.Buffered(1))
    per_seq = lambda a, b: pl.BlockSpec((1, a, b), lambda s: (s, 0, 0))
    lanes = jax.ShapeDtypeStruct((n, length, LANES), F32)
    return pl.pallas_call(
        functools.partial(project_first_kernel, len(weights), heads),
        grid=(n,),
        in_specs=[
            per_seq(padded, model), whole(state_w), whole(step_w), whole(small), per_seq(*ids.shape[1:]),
            per_seq(*id_rows.shape[1:]), whole(taps),
        ] + [whole(v) for v in weights],
        out_specs=[pl.BlockSpec((len(weights), 1, padded, width), lambda s: (0, s, 0, 0))]
        + [per_seq(length, LANES)] * 4
        + [per_seq(padded, 2 * LANES), per_seq(length, 2 * LANES)],
        out_shape=[
            jax.ShapeDtypeStruct((blocks, n, padded, width), BF16), lanes, lanes, lanes, lanes,
            jax.ShapeDtypeStruct((n, padded, 2 * LANES), BF16),
            jax.ShapeDtypeStruct((n, length, 2 * LANES), BF16),
        ],
        compiler_params=pltpu.CompilerParams(vmem_limit_bytes=VMEM),
        name="project_first",
    )(normed, state_w, step_w, small, ids, id_rows, taps, *weights)


def project_more(normed, rows, weights, first):
    n, padded, model = normed.shape
    width = weights[0].shape[1]
    count = len(weights)
    return pl.pallas_call(
        functools.partial(project_more_kernel, count),
        grid=(n,),
        in_specs=[pl.BlockSpec((1, padded, model), lambda s: (s, 0, 0)), pl.BlockSpec(memory_space=pl.ANY)]
        + [pl.BlockSpec(v.shape, lambda s: (0, 0), pipeline_mode=pl.Buffered(1)) for v in weights],
        out_specs=pl.BlockSpec((count, 1, padded, width), lambda s: (first // count, s, 0, 0)),
        out_shape=jax.ShapeDtypeStruct(rows.shape, BF16),
        input_output_aliases={1: 0},
        compiler_params=pltpu.CompilerParams(vmem_limit_bytes=VMEM),
        name="project_more",
    )(normed, rows, *weights)


def project_gate_kernel(blocks, normed, *refs):
    for r in range(blocks):
        refs[blocks][r, 0] = dot(normed[0, PAD:, :], refs[r][...]).astype(BF16)


def project_gate(normed, weights):
    n, padded, model = normed.shape
    width = weights[0].shape[1]
    count = len(weights)
    return pl.pallas_call(
        functools.partial(project_gate_kernel, count),
        grid=(n,),
        in_specs=[pl.BlockSpec((1, padded, model), lambda s: (s, 0, 0))]
        + [pl.BlockSpec(v.shape, lambda s: (0, 0), pipeline_mode=pl.Buffered(1)) for v in weights],
        out_specs=pl.BlockSpec((count, 1, padded - PAD, width), lambda s: (0, s, 0, 0)),
        out_shape=jax.ShapeDtypeStruct((count, n, padded - PAD, width), BF16),
        compiler_params=pltpu.CompilerParams(vmem_limit_bytes=VMEM),
        name="project_gate",
    )(normed, *weights)


def write_message(message, state, survive):
    cuts, rows, width = message.shape
    own = rows - 16
    survive = jnp.concatenate([survive, survive], axis=0).astype(BF16)
    for i in range(cuts):
        message[i, :own, :] = state[i * own : (i + 1) * own].astype(BF16)
        message[i, own:, :] = survive


def state_kernel(first, per_block, rows, bc, ids, id_rows, steps, cum, taps, *refs):
    acted, message = refs[-2:]
    length, width = acted.shape[2:]
    offset = (pl.program_id(0) + first) * per_block

    def store(here, lanes, value):
        acted[0, 0, here, lanes] = value

    conv_forward(rows.at[0, 0], ids, id_rows, taps[0], store, length)
    total = cum[0, length - 1 : length, :]
    last = ids[0, PAD + length - 1 : PAD + length, :]
    before = ids[0, PAD - 1 : PAD, :]
    state = jnp.zeros((LANES, width), F32)
    for c in range(length // CHUNK):
        here = slice(c * CHUNK, (c + 1) * CHUNK)
        same = (ids[0, PAD + c * CHUNK : PAD + (c + 1) * CHUNK, :] == last).astype(F32)
        tail = jnp.exp(total - cum[0, here, :]) * same * steps[0, here, :]
        scaled = (expand(tail, width, offset) * acted[0, 0, here, :].astype(F32)).astype(BF16)
        state = state + dot_tn(bc[0, here, :LANES], scaled)
    survive = jnp.exp(total) * (last == before).astype(F32)
    write_message(message.at[0, 0], state, expand_row(survive, width, offset))


def state_call(rows, bc, ids, id_rows, steps, cum, taps, held, first, count, per_block, cuts):
    blocks, n, padded, width = rows.shape
    length = padded - PAD
    four = lambda a, b: pl.BlockSpec((1, 1, a, b), lambda g, s: (g + first, s, 0, 0))
    per_seq = lambda a: pl.BlockSpec((1,) + a.shape[1:], lambda g, s: (s, 0, 0))
    piece = LANES // cuts + 16
    return pl.pallas_call(
        functools.partial(state_kernel, first, per_block),
        grid=(count, n),
        in_specs=[
            four(padded, width), per_seq(bc), per_seq(ids), per_seq(id_rows), per_seq(steps), per_seq(cum),
            pl.BlockSpec((1,) + taps.shape[1:], lambda g, s: (g + first, 0, 0)),
        ] + [pl.BlockSpec(memory_space=pl.ANY) for _ in held],
        out_specs=[
            four(length, width),
            pl.BlockSpec((1, 1, cuts, piece, width), lambda g, s: (g + first, s, 0, 0, 0)),
        ],
        out_shape=[
            jax.ShapeDtypeStruct((blocks, n, length, width), BF16),
            jax.ShapeDtypeStruct((blocks, n, cuts, piece, width), BF16),
        ],
        input_output_aliases={7: 0, 8: 1} if held else {},
        compiler_params=pltpu.CompilerParams(vmem_limit_bytes=VMEM),
        name="range_state",
    )(rows, bc, ids, id_rows, steps, cum, taps, *held)


def chunk_marks(ids, c):
    first = PAD + c * CHUNK
    return ids[0, first : first + CHUNK, :], ids[0, first + CHUNK - 1 : first + CHUNK, :], ids[0, first - 1 : first, :]


def chunk_decays(ids, cum, c):
    here, last, before = chunk_marks(ids, c)
    value = cum[0, c * CHUNK : (c + 1) * CHUNK, :]
    base = cum[0, c * CHUNK - 1 : c * CHUNK, :] if c else jnp.zeros((1, LANES), F32)
    end = value[CHUNK - 1 : CHUNK]
    entering = jnp.exp(value - base) * (here == before).astype(F32)
    tail = jnp.exp(end - value) * (here == last).astype(F32)
    survive = jnp.exp(end - base) * (last == before).astype(F32)
    return entering, tail, survive


def lane_halves(pair):
    lane = lax.broadcasted_iota(jnp.int32, pair.shape, 1)
    zero = jnp.zeros_like(pair)
    return jnp.concatenate([jnp.where(lane < HEAD_DIM, pair, zero), jnp.where(lane < HEAD_DIM, zero, pair)], axis=0)


def inside_kernel(per_block, acted, bc, ids, id_rows, steps, cum, mixed, states, carried, turned):
    length, width = acted.shape[2:]
    offset = pl.program_id(1) * per_block
    later = triangle(True)
    for c in range(length // CHUNK):
        here = slice(c * CHUNK, (c + 1) * CHUNK)
        b_part, c_part = bc[0, here, :LANES], bc[0, here, LANES:]
        marks, _, _ = chunk_marks(ids, c)
        same = later & (marks == id_rows[0, 0:1, PAD + c * CHUNK : PAD + (c + 1) * CHUNK])
        scores = jnp.where(same, dot_nt(c_part, b_part), 0.0)
        value = cum[0, here, :]
        turned[...] = jnp.transpose(value)
        entering, tail, survive = chunk_decays(ids, cum, c)
        scaled = (expand(steps[0, here, :], width, offset) * acted[0, 0, here, :].astype(F32)).astype(BF16)
        if c:
            held = carried[...]
            held_low = held.astype(BF16)
            states[0, 0, c - 1] = held_low
            outside = dot(c_part, held_low) * expand(entering, width, offset)
        for pair in range(width // LANES):
            lanes = slice(pair * LANES, (pair + 1) * LANES)
            mixing = []
            for h in (2 * pair, 2 * pair + 1):
                spread = jnp.minimum(column(value, offset + h) - turned[pl.ds(offset + h, 1), :], 0.0)
                mixing.append((scores * jnp.exp(spread)).astype(BF16))
            result = dot(jnp.concatenate(mixing, axis=1), lane_halves(scaled[:, lanes]))
            mixed[0, 0, here, lanes] = result + outside[:, lanes] if c else result
        if c + 1 < length // CHUNK:
            fresh = dot_tn(b_part, (expand(tail, width, offset) * scaled.astype(F32)).astype(BF16))
            if c:
                fresh = fresh + held * expand_row(survive, width, offset)[0:1]
            carried[...] = fresh


def inside_call(acted, bc, ids, id_rows, steps, cum, per_block):
    blocks, n, length, width = acted.shape
    chunks = length // CHUNK
    four = lambda a, b: pl.BlockSpec((1, 1, a, b), lambda s, g: (g, s, 0, 0))
    per_seq = lambda a: pl.BlockSpec((1,) + a.shape[1:], lambda s, g: (s, 0, 0))
    return pl.pallas_call(
        functools.partial(inside_kernel, per_block),
        grid=(n, blocks),
        in_specs=[four(length, width), per_seq(bc), per_seq(ids), per_seq(id_rows), per_seq(steps), per_seq(cum)],
        out_specs=[
            four(length, width),
            pl.BlockSpec((1, 1, chunks - 1, LANES, width), lambda s, g: (g, s, 0, 0, 0)),
        ],
        out_shape=[
            jax.ShapeDtypeStruct((blocks, n, length, width), F32),
            jax.ShapeDtypeStruct((blocks, n, chunks - 1, LANES, width), BF16),
        ],
        scratch_shapes=[pltpu.VMEM((LANES, width), F32), pltpu.VMEM((LANES, LANES), F32)],
        compiler_params=pltpu.CompilerParams(vmem_limit_bytes=VMEM),
        name="inside",
    )(acted, bc, ids, id_rows, steps, cum)


def relay_kernel(backward, message, carried):
    ranges, rows, width = carried.shape
    state = jnp.zeros((rows, width), F32)
    order = range(ranges - 1, -1, -1) if backward else range(ranges)
    for q in order:
        carried[q] = state.astype(BF16)
        decay = message[q, rows : rows + 1, :].astype(F32)
        state = state * decay + message[q, :rows, :].astype(F32)


def after(value, *others):
    return lax.optimization_barrier((value,) + others)[0]


def relay_out(message, backward, meanwhile):
    blocks, n, cuts, rows, width = message.shape
    ranges = lax.axis_size("seq")
    arrived = lax.all_to_all(message.reshape(ranges, rows, width), "seq", 0, 0, tiled=True)
    return pl.pallas_call(
        functools.partial(relay_kernel, backward),
        out_shape=jax.ShapeDtypeStruct((ranges, rows - 16, width), BF16),
        compiler_params=pltpu.CompilerParams(vmem_limit_bytes=VMEM),
        name="relay",
    )(after(arrived, *meanwhile))


def relay_back(carried, message):
    blocks, n, _, _, width = message.shape
    return lax.all_to_all(carried, "seq", 0, 0, tiled=True).reshape(blocks, n, LANES, width)


def middle_kernel(
    blocks, per_block, total_width, mixed, gate, acted, cum, cum_end, bc, ids, ids_before, ids_after, tokens, cotangent,
    params, entered, *refs
):
    weights, refs = refs[:blocks], refs[blocks:]
    output, normed_out, d_gate, d_summed, pulled, gain_grad, skip_grad = refs[:7]
    summed_s, gated_s, grad_s, first_s, second_s, low_s, row_s, pull_s = refs[7:]
    tile, width = mixed.shape[2:]
    t = pl.program_id(0)
    before = ids_before[0, PAD - 1 : PAD, :]
    marks = ids[0]
    c_part = bc[0, :, LANES:]
    slabs = tile // 16
    same = (marks == before).astype(F32)
    decay = jnp.exp(cum[0]) * same
    row_s[...] = jnp.zeros_like(row_s)

    def lanes_sum(value):
        total = value[:, :LANES]
        for i in range(1, width // LANES):
            total = total + value[:, i * LANES : (i + 1) * LANES]
        return total

    @pl.when(t == 0)
    def _():
        gain_grad[...] = jnp.zeros_like(gain_grad)
        skip_grad[...] = jnp.zeros_like(skip_grad)
        pull_s[...] = jnp.zeros_like(pull_s)

    for r in range(blocks):
        first_s[...] = dot(c_part, entered[r, 0])
        second_s[r] = expand(decay, width, r * per_block)
        skip = params[r, 6:7, :]

        def step(i, carry, r=r, skip=skip):
            here = rows_at(i * 16, 16)
            value = mixed[r, 0, here, :] + first_s[here, :] * second_s[r, here, :]
            summed = value + skip * acted[r, 0, here, :].astype(F32)
            g = gate[r, 0, here, :].astype(F32)
            gated = summed * (g * sigmoid(g))
            summed_s[r, here, :] = summed
            gated_s[r, here, :] = gated
            row_s[here, :] = row_s[here, :] + lanes_sum(gated * gated)
            return carry

        lax.fori_loop(0, slabs, step, 0, unroll=4)
    squares = jnp.sum(row_s[...], axis=1, keepdims=True)
    rescale = jnp.broadcast_to(lax.rsqrt(squares / total_width + EPS), (tile, LANES))
    row_s[...] = rescale
    for r in range(blocks):
        gain = params[r, 5:6, :]

        def step(i, carry, r=r, gain=gain):
            here = rows_at(i * 16, 16)
            normed_out[r, 0, here, :] = (gated_s[r, here, :] * widen(row_s[here, :], width) * gain).astype(BF16)
            return carry

        lax.fori_loop(0, slabs, step, 0, unroll=4)
    branch = tokens[0].astype(F32)
    for r in range(blocks):
        branch = branch + dot(normed_out[r, 0], weights[r][...])
    output[0] = branch.astype(BF16)
    first_s[:, :LANES] = jnp.zeros((tile, LANES), F32)
    for r in range(blocks):
        grad_s[r] = dot_nt(cotangent[0], weights[r][...])
        gain = params[r, 5:6, :]

        def step(i, total, r=r, gain=gain):
            here = rows_at(i * 16, 16)
            both = grad_s[r, here, :] * gated_s[r, here, :]
            first_s[here, :LANES] = first_s[here, :LANES] + lanes_sum(both * gain)
            return total + fold8(both * widen(row_s[here, :], width))

        gain_grad[r] = gain_grad[r] + lax.fori_loop(0, slabs, step, jnp.zeros((8, width), F32), unroll=4)
    cross = jnp.sum(first_s[:, :LANES], axis=1, keepdims=True) / total_width
    first_s[:, :LANES] = rescale * rescale * rescale * cross
    for r in range(blocks):
        gain = params[r, 5:6, :]

        def step(i, total, r=r, gain=gain):
            here = rows_at(i * 16, 16)
            g = gate[r, 0, here, :].astype(F32)
            sigma = sigmoid(g)
            d_gated = widen(row_s[here, :], width) * (grad_s[r, here, :] * gain) - gated_s[r, here, :] * widen(
                first_s[here, :LANES], width
            )
            d_sum = d_gated * (g * sigma)
            d_gate[r, 0, here, :] = (d_gated * summed_s[r, here, :] * (sigma * (1.0 + g * (1.0 - sigma)))).astype(BF16)
            low = d_sum.astype(BF16)
            d_summed[r, 0, here, :] = low
            low_s[here, :] = (d_sum * second_s[r, here, :]).astype(BF16)
            return total + fold8(d_sum * acted[r, 0, here, :].astype(F32))

        skip_grad[r] = skip_grad[r] + lax.fori_loop(0, slabs, step, jnp.zeros((8, width), F32), unroll=4)
        pull_s[r] = pull_s[r] + dot_tn(c_part, low_s[...])

    @pl.when(t == pl.num_programs(0) - 1)
    def _():
        survive = jnp.exp(cum_end[0, 7:8, :]) * (ids_after[0, PAD - 1 : PAD, :] == before).astype(F32)
        for r in range(blocks):
            write_message(pulled.at[r, 0], pull_s[r], expand_row(survive, width, r * per_block))


def middle_call(s, mixed, gate, acted, cum, entered, bc, ids, tokens, cotangent, params, weights, per_block, cuts):
    blocks, n, length, width = mixed.shape
    model = tokens.shape[2]
    tile = min(256, length)
    wide = lambda w: pl.BlockSpec((blocks, 1, tile, w), lambda t: (0, s, t, 0))
    wide_out = lambda w: pl.BlockSpec((blocks, 1, tile, w), lambda t: (0, 0, t, 0))
    rows = lambda w: pl.BlockSpec((1, tile, w), lambda t: (s, t, 0))
    one = lambda a: pl.BlockSpec((a.shape[0], 1) + a.shape[2:], lambda t: (0, s, 0, 0), pipeline_mode=pl.Buffered(1))
    whole = lambda a: pl.BlockSpec(a.shape, lambda t: (0,) * a.ndim, pipeline_mode=pl.Buffered(1))
    kept = lambda *shape: pl.BlockSpec(shape, lambda t: (0,) * len(shape))
    piece = LANES // cuts + 16
    edge = lambda a: pl.BlockSpec((1, PAD, LANES), lambda t: (s, a, 0))
    ids_here = ids[:, PAD : PAD + length]
    wide_shape = jax.ShapeDtypeStruct((blocks, 1, length, width), BF16)
    return pl.pallas_call(
        functools.partial(middle_kernel, blocks, per_block, width * blocks),
        grid=(length // tile,),
        in_specs=[
            wide(width), wide(width), wide(width), rows(LANES),
            pl.BlockSpec((1, 8, LANES), lambda t: (s, length // 8 - 1, 0)), rows(2 * LANES), rows(LANES),
            edge(0), edge(length // PAD), rows(model), rows(model), whole(params),
            one(entered),
        ] + [whole(v) for v in weights],
        out_specs=[
            pl.BlockSpec((1, tile, model), lambda t: (0, t, 0)), wide_out(width), wide_out(width), wide_out(width),
            kept(blocks, 1, cuts, piece, width), kept(blocks, 8, width), kept(blocks, 8, width),
        ],
        out_shape=[
            jax.ShapeDtypeStruct((1, length, model), BF16),
            wide_shape, wide_shape, wide_shape,
            jax.ShapeDtypeStruct((blocks, 1, cuts, piece, width), BF16),
            jax.ShapeDtypeStruct((blocks, 8, width), F32),
            jax.ShapeDtypeStruct((blocks, 8, width), F32),
        ],
        scratch_shapes=[
            pltpu.VMEM((blocks, tile, width), F32),
            pltpu.VMEM((blocks, tile, width), F32),
            pltpu.VMEM((blocks, tile, width), F32),
            pltpu.VMEM((tile, width), F32),
            pltpu.VMEM((blocks, tile, width), F32),
            pltpu.VMEM((tile, width), BF16),
            pltpu.VMEM((tile, LANES), F32),
            pltpu.VMEM((blocks, LANES, width), F32),
        ],
        compiler_params=pltpu.CompilerParams(vmem_limit_bytes=VMEM),
        name="middle",
    )(mixed, gate, acted, cum, cum, bc, ids_here, ids, ids, tokens, cotangent, params, entered, *weights)


def inside_back_kernel(
    per_block, acted, d_summed, mixed, bc, ids, id_rows, steps, cum, states, entered, d_scaled, d_b, d_c, d_cum,
    carried, turned,
):
    length, width = acted.shape[2:]
    chunks = length // CHUNK
    g = pl.program_id(0)
    offset = g * per_block
    heads = head_map(width, offset)
    sooner = triangle(False)
    first_before = ids[0, PAD - 1 : PAD, :]
    came = entered[0, 0]

    @pl.when(g == 0)
    def _():
        d_b[...] = jnp.zeros_like(d_b)
        d_c[...] = jnp.zeros_like(d_c)
        d_cum[...] = jnp.zeros_like(d_cum)

    for c in range(chunks - 1, -1, -1):
        here = slice(c * CHUNK, (c + 1) * CHUNK)
        b_part, c_part = bc[0, here, :LANES], bc[0, here, LANES:]
        marks, _, _ = chunk_marks(ids, c)
        same = sooner & (marks == id_rows[0, 0:1, PAD + c * CHUNK : PAD + (c + 1) * CHUNK])
        scores_t = jnp.where(same, dot_nt(b_part, c_part), 0.0)
        value = cum[0, here, :]
        turned[...] = jnp.transpose(value)
        entering, tail, survive = chunk_decays(ids, cum, c)
        scaled = (expand(steps[0, here, :], width, offset) * acted[0, 0, here, :].astype(F32)).astype(BF16)
        grad = d_summed[0, 0, here, :]
        grad_wide = grad.astype(F32)
        from_start = jnp.exp(value) * (marks == first_before).astype(F32)
        start_wide = expand(from_start, width, offset)
        d_c_part = dot_nt((grad_wide * start_wide).astype(BF16), came)
        dots = grad_wide * (mixed[0, 0, here, :] + start_wide * dot(c_part, came))
        if c < chunks - 1:
            held = carried[...]
            held_low = held.astype(BF16)
            tail_wide = expand(tail, width, offset)
            later = dot(b_part, held_low) * tail_wide
            d_b_part = dot_nt((tail_wide * scaled.astype(F32)).astype(BF16), held_low)
        if c:
            entering_grad = (expand(entering, width, offset) * grad_wide).astype(BF16)
            d_c_part = d_c_part + dot_nt(entering_grad, states[0, 0, c - 1])
        d_scores_t = jnp.zeros((CHUNK, CHUNK), F32)
        results = []
        for pair in range(width // LANES):
            lanes = slice(pair * LANES, (pair + 1) * LANES)
            products = dot_nt(lane_halves(scaled[:, lanes]), grad[:, lanes])
            mixing = []
            for half, h in enumerate((2 * pair, 2 * pair + 1)):
                spread = jnp.minimum(turned[pl.ds(offset + h, 1), :] - column(value, offset + h), 0.0)
                decay = jnp.exp(spread)
                mixing.append((scores_t * decay).astype(BF16))
                d_scores_t = d_scores_t + products[half * CHUNK : (half + 1) * CHUNK] * decay
            results.append(dot(jnp.concatenate(mixing, axis=1), lane_halves(grad[:, lanes])))
        result = jnp.concatenate(results, axis=1)
        if c < chunks - 1:
            result = result + later
        d_scaled[0, 0, here, :] = result.astype(BF16)
        d_cum[0, here, :] = d_cum[0, here, :] + by_head(dots - scaled.astype(F32) * result, heads)
        d_scores_t = jnp.where(same, d_scores_t, 0.0).astype(BF16)
        d_b_here = dot(d_scores_t, c_part)
        if c < chunks - 1:
            d_b_here = d_b_here + d_b_part
        d_b[0, here, :] = d_b[0, here, :] + d_b_here
        d_c[0, here, :] = d_c[0, here, :] + d_c_part + dot_tn(d_scores_t, b_part)
        if c:
            pulled = dot_tn(c_part, entering_grad)
            if c < chunks - 1:
                pulled = pulled + held * expand_row(survive, width, offset)[0:1]
            carried[...] = pulled


def inside_back_call(s, acted, d_summed, mixed, bc, ids, id_rows, steps, cum, states, entered, per_block):
    blocks, n, length, width = acted.shape
    four = lambda a, b: pl.BlockSpec((1, 1, a, b), lambda g: (g, s, 0, 0))
    own = lambda a, b: pl.BlockSpec((1, 1, a, b), lambda g: (g, 0, 0, 0))
    per_seq = lambda a: pl.BlockSpec((1,) + a.shape[1:], lambda g: (s, 0, 0))
    summed = pl.BlockSpec((1, length, LANES), lambda g: (0, 0, 0))
    lanes = jax.ShapeDtypeStruct((1, length, LANES), F32)
    return pl.pallas_call(
        functools.partial(inside_back_kernel, per_block),
        grid=(blocks,),
        in_specs=[
            four(length, width), own(length, width), four(length, width), per_seq(bc), per_seq(ids), per_seq(id_rows),
            per_seq(steps), per_seq(cum),
            pl.BlockSpec((1, 1) + states.shape[2:], lambda g: (g, s, 0, 0, 0)),
            four(LANES, width),
        ],
        out_specs=[own(length, width), summed, summed, summed],
        out_shape=[jax.ShapeDtypeStruct((blocks, 1, length, width), BF16), lanes, lanes, lanes],
        scratch_shapes=[pltpu.VMEM((LANES, width), F32), pltpu.VMEM((LANES, LANES), F32)],
        compiler_params=pltpu.CompilerParams(vmem_limit_bytes=VMEM),
        name="inside_back",
    )(acted, d_summed, mixed, bc, ids, id_rows, steps, cum, states, entered)


def close_kernel(
    per_block, rows, acted, d_summed, d_scaled, bc, ids, id_rows, steps, raw, log_decay, cum, d_cum, leaving, entered,
    params, small, state_rows, state_taps, d_b, d_c,
    d_rows, d_raw, d_state, taps_grad, state_taps_grad, small_grad, d_pre, d_acted, d_log, d_step, ends, d_bc, d_pre_bc,
):
    length, width = acted.shape[2:]
    chunks = length // CHUNK
    g = pl.program_id(0)
    offset = g * per_block
    heads = head_map(width, offset)
    last = ids[0, PAD + length - 1 : PAD + length, :]
    before = ids[0, PAD - 1 : PAD, :]
    end = cum[0, length - 1 : length, :]
    skip = params[0, 6:7, :]
    held = leaving[0, 0]
    came = entered[0, 0]

    @pl.when(g == 0)
    def _():
        d_bc[:, :LANES] = d_b[0]
        d_bc[:, LANES:] = d_c[0]
        d_log[...] = d_cum[0]
        d_step[...] = jnp.zeros_like(d_step)
        ends[...] = jnp.zeros_like(ends)

    boundary = jnp.zeros((1, LANES), F32)
    for c in range(chunks):
        here = slice(c * CHUNK, (c + 1) * CHUNK)
        marks, _, _ = chunk_marks(ids, c)
        tail = jnp.exp(end - cum[0, here, :]) * (marks == last).astype(F32)
        tail_wide = expand(tail, width, offset)
        steps_wide = expand(steps[0, here, :], width, offset)
        x = acted[0, 0, here, :].astype(F32)
        scaled = (steps_wide * x).astype(BF16).astype(F32)
        later = dot(bc[0, here, :LANES], held) * tail_wide
        total = d_scaled[0, 0, here, :].astype(F32) + later
        d_acted[here, :] = steps_wide * total + skip * d_summed[0, 0, here, :].astype(F32)
        d_bc[here, :LANES] = d_bc[here, :LANES] + dot_nt((tail_wide * scaled).astype(BF16), held)
        from_later = by_head_low(scaled * later, heads)
        boundary = boundary + jnp.sum(from_later, axis=0, keepdims=True)
        d_log[here, :] = d_log[here, :] - from_later
        d_step[here, :] = d_step[here, :] + by_head_low(x * total, heads)
    product = held.astype(F32) * came.astype(F32)
    product = jnp.sum(product.reshape(LANES // 8, 8, width), axis=0)
    survive = jnp.exp(end) * (last == before).astype(F32)
    boundary = boundary + survive * jnp.sum(by_head(jnp.concatenate([product, product * 0.0], axis=0), heads), axis=0, keepdims=True)
    ends[0:1, :] = ends[0:1, :] + boundary

    def store(here, lanes, value):
        d_rows[0, 0, here, lanes] = value

    sums = conv_backward(
        rows.at[0, 0],
        ids,
        id_rows,
        params[0],
        lambda c, lanes: d_acted[c * CHUNK : (c + 1) * CHUNK, lanes],
        d_pre,
        store,
        length,
    )
    taps_grad[0] = jnp.concatenate(sums + [jnp.zeros((3, width), F32)], axis=0)

    @pl.when(g == pl.num_programs(0) - 1)
    def _():
        rate = jnp.exp(small[1:2, :])
        ones = triangle(False).astype(F32)
        carry = ends[0:1, :]
        decay_sum = jnp.zeros((1, LANES), F32)
        bias_sum = jnp.zeros((1, LANES), F32)
        for c in range(chunks - 1, -1, -1):
            here = slice(c * CHUNK, (c + 1) * CHUNK)
            grads = exact_dot(ones, d_log[here, :]) + carry
            carry = grads[0:1]
            decay_sum = decay_sum + jnp.sum(grads * log_decay[0, here, :], axis=0, keepdims=True)
            value = (d_step[here, :] - grads * rate) * sigmoid(raw[0, here, :] + small[0:1, :])
            bias_sum = bias_sum + jnp.sum(value, axis=0, keepdims=True)
            d_raw[0, here, :] = value.astype(BF16)
        small_grad[...] = jnp.concatenate([bias_sum, decay_sum, jnp.zeros((6, LANES), F32)], axis=0)

        def store_state(here, lanes, value):
            d_state[0, here, lanes] = value

        sums = conv_backward(
            state_rows.at[0],
            ids,
            id_rows,
            state_taps[...],
            lambda c, lanes: d_bc[c * CHUNK : (c + 1) * CHUNK, lanes],
            d_pre_bc,
            store_state,
            length,
        )
        state_taps_grad[...] = jnp.concatenate(sums + [jnp.zeros((3, 2 * LANES), F32)], axis=0)


def close_call(
    s, rows, acted, d_summed, d_scaled, bc, ids, id_rows, steps, raw, log_decay, cum, d_cum, leaving, entered, params,
    small, state_rows, state_taps, d_b, d_c, per_block,
):
    blocks, n, length, width = acted.shape
    four = lambda a, b: pl.BlockSpec((1, 1, a, b), lambda g: (g, s, 0, 0))
    own = lambda a, b: pl.BlockSpec((1, 1, a, b), lambda g: (g, 0, 0, 0))
    per_seq = lambda a: pl.BlockSpec((1,) + a.shape[1:], lambda g: (s, 0, 0))
    kept = lambda *shape: pl.BlockSpec(shape, lambda g: (0,) * len(shape))
    whole = lambda a: kept(*a.shape)
    wide = own(length, width)
    return pl.pallas_call(
        functools.partial(close_kernel, per_block),
        grid=(blocks,),
        in_specs=[
            four(length + PAD, width), four(length, width), wide, wide, per_seq(bc), per_seq(ids), per_seq(id_rows),
            per_seq(steps), per_seq(raw), per_seq(log_decay), per_seq(cum), kept(1, length, LANES), own(LANES, width),
            four(LANES, width),
            pl.BlockSpec((1,) + params.shape[1:], lambda g: (g, 0, 0)), whole(small), per_seq(state_rows),
            whole(state_taps), whole(d_b), whole(d_c),
        ],
        out_specs=[
            own(length + PAD, width), kept(1, length, LANES), kept(1, length + PAD, 2 * LANES),
            pl.BlockSpec((1, 8, width), lambda g: (g, 0, 0)), kept(8, 2 * LANES), kept(8, LANES),
        ],
        out_shape=[
            jax.ShapeDtypeStruct((blocks, 1, length + PAD, width), BF16),
            jax.ShapeDtypeStruct((1, length, LANES), BF16),
            jax.ShapeDtypeStruct((1, length + PAD, 2 * LANES), BF16),
            jax.ShapeDtypeStruct((blocks, 8, width), F32),
            jax.ShapeDtypeStruct((8, 2 * LANES), F32),
            jax.ShapeDtypeStruct((8, LANES), F32),
        ],
        scratch_shapes=[
            pltpu.VMEM((length + 2 * PAD, width), BF16),
            pltpu.VMEM((length, width), F32),
            pltpu.VMEM((length, LANES), F32),
            pltpu.VMEM((length, LANES), F32),
            pltpu.VMEM((8, LANES), F32),
            pltpu.VMEM((length, 2 * LANES), F32),
            pltpu.VMEM((length + 2 * PAD, 2 * LANES), BF16),
        ],
        compiler_params=pltpu.CompilerParams(vmem_limit_bytes=VMEM),
        name="close",
    )(
        rows, acted, d_summed, d_scaled, bc, ids, id_rows, steps, raw, log_decay, cum, d_cum, leaving, entered, params,
        small, state_rows, state_taps, d_b, d_c,
    )


def input_kernel(blocks, d_gate, d_rows, d_raw, d_state, tokens, cotangent, gain, state_w, step_w, *refs):
    row_weights, refs = refs[:blocks], refs[blocks:]
    gate_weights, refs = refs[:blocks], refs[blocks:]
    input_grad, edge, halo, gain_grad, main_s, halo_s = refs
    length = d_gate.shape[2]
    total = dot_nt(d_state[0], state_w[...])
    halo_s[...] = total[:PAD]
    main_s[...] = total[PAD:] + dot(d_raw[0], step_w[...])
    for r in range(blocks):
        halo_s[...] = halo_s[...] + dot_nt(d_rows[r, 0, :PAD, :], row_weights[r][...])
        main_s[...] = main_s[...] + (
            dot_nt(d_rows[r, 0, PAD:, :], row_weights[r][...]) + dot_nt(d_gate[r, 0], gate_weights[r][...])
        )

    def norm_back(value, token):
        scale = lax.rsqrt(jnp.mean(token * token, axis=1, keepdims=True) + EPS)
        unit = value * gain[...]
        inner = jnp.mean(unit * token, axis=1, keepdims=True)
        return scale * unit - token * (scale * scale * scale * inner), fold8(value * token * scale)

    grad, sums = norm_back(halo_s[...], tokens[0, :PAD, :].astype(F32))
    halo[0] = grad.astype(BF16)

    def step(i, carry):
        here = rows_at(i * 16, 16)
        grad, more = norm_back(main_s[here, :], tokens[0, rows_at(PAD + i * 16, 16), :].astype(F32))
        value = grad + cotangent[0, here, :].astype(F32)
        edge[0] = value
        input_grad[0, here, :] = value.astype(BF16)
        return carry + more

    gain_grad[...] = lax.fori_loop(0, length // 16, step, sums, unroll=4)


def input_call(s, d_gate, d_rows, d_raw, d_state, tokens, cotangent, gain, state_w, step_w, row_weights, gate_weights):
    blocks, _, length, width = d_gate.shape
    padded, model = tokens.shape[1:]
    whole = lambda a: pl.BlockSpec(a.shape, lambda t: (0,) * a.ndim, pipeline_mode=pl.Buffered(1))
    one = lambda a, b: pl.BlockSpec((1, a, b), lambda t: (s, 0, 0), pipeline_mode=pl.Buffered(1))
    kept = lambda *shape: pl.BlockSpec(shape, lambda t: (0,) * len(shape), pipeline_mode=pl.Buffered(1))
    return pl.pallas_call(
        functools.partial(input_kernel, blocks),
        grid=(1,),
        in_specs=[
            whole(d_gate), whole(d_rows), whole(d_raw), whole(d_state), one(padded, model), one(length, model),
            whole(gain), whole(state_w), whole(step_w),
        ] + [whole(v) for v in row_weights] + [whole(v) for v in gate_weights],
        out_specs=[kept(1, length, model), kept(1, PAD, model), kept(1, PAD, model), kept(8, model)],
        out_shape=[
            jax.ShapeDtypeStruct((1, length, model), BF16),
            jax.ShapeDtypeStruct((1, PAD, model), F32),
            jax.ShapeDtypeStruct((1, PAD, model), BF16),
            jax.ShapeDtypeStruct((8, model), F32),
        ],
        scratch_shapes=[pltpu.VMEM((length, model), F32), pltpu.VMEM((PAD, model), F32)],
        compiler_params=pltpu.CompilerParams(vmem_limit_bytes=VMEM),
        name="input_gradient",
    )(d_gate, d_rows, d_raw, d_state, tokens, cotangent, gain, state_w, step_w, *row_weights, *gate_weights)


def assemble_kernel(count, places, *refs):
    parts, refs = refs[:count], refs[count:]
    edges, refs = (refs[:count], refs[count:]) if len(refs) > 2 * count else ((), refs)
    whole, buffers, (in_sem, out_sem) = refs[0], refs[1:-2], refs[-2:]
    length = parts[0].shape[1]
    reads = [pltpu.make_async_copy(p.at[0], b, in_sem.at[i]) for i, (p, b) in enumerate(zip(parts, buffers))]
    writes = [pltpu.make_async_copy(b, whole.at[places[i]], out_sem.at[i]) for i, b in enumerate(buffers)]
    for read in reads:
        read.start()
    for i, (read, write) in enumerate(zip(reads, writes)):
        read.wait()
        if edges:
            buffers[i][length - PAD :, :] = edges[i][0]
        write.start()
    for write in writes:
        write.wait()


def assemble(parts, edges, places):
    count = len(parts)
    _, length, model = parts[0].shape
    return pl.pallas_call(
        functools.partial(assemble_kernel, count),
        grid_spec=pltpu.PrefetchScalarGridSpec(
            num_scalar_prefetch=1,
            grid=(1,),
            in_specs=[pl.BlockSpec(memory_space=pl.ANY) for _ in parts]
            + [pl.BlockSpec((1, PAD, model), lambda t, i: (0, 0, 0)) for _ in edges],
            out_specs=pl.BlockSpec(memory_space=pl.ANY),
            scratch_shapes=[pltpu.VMEM((length, model), BF16) for _ in parts]
            + [pltpu.SemaphoreType.DMA((count,)), pltpu.SemaphoreType.DMA((count,))],
        ),
        out_shape=jax.ShapeDtypeStruct((count, length, model), BF16),
        compiler_params=pltpu.CompilerParams(vmem_limit_bytes=VMEM),
        name="assemble",
    )(jnp.stack(places).astype(jnp.int32), *parts, *edges)


def weight_grad_kernel(n, halo, *refs):
    turned, refs = refs[:n], refs[n:]
    grads, refs = refs[:n], refs[n:]
    total = None
    if halo:
        before, refs = refs[0], refs[1:]
    (out,) = refs
    for s in range(n):
        part = dot(turned[s][...], grads[s][0, 0, PAD if halo else 0 :, :])
        if halo:
            part = part + dot_tn(before[s], grads[s][0, 0, :PAD, :])
        total = part if total is None else total + part
    out[0] = total.astype(BF16)


def weight_grad(turned, grads, before=None):
    n = len(turned)
    model, length = turned[0].shape
    blocks, _, tokens, width = grads[0].shape
    halo = [] if before is None else [before]
    return pl.pallas_call(
        functools.partial(weight_grad_kernel, n, len(halo)),
        grid=(blocks,),
        in_specs=[pl.BlockSpec(v.shape, lambda g: (0, 0), pipeline_mode=pl.Buffered(1)) for v in turned]
        + [pl.BlockSpec((1, 1, tokens, width), lambda g: (g, 0, 0, 0)) for _ in grads]
        + [pl.BlockSpec(v.shape, lambda g: (0, 0, 0), pipeline_mode=pl.Buffered(1)) for v in halo],
        out_specs=pl.BlockSpec((1, model, width), lambda g: (g, 0, 0)),
        out_shape=jax.ShapeDtypeStruct((blocks, model, width), BF16),
        compiler_params=pltpu.CompilerParams(vmem_limit_bytes=VMEM),
        name="weight_gradient",
    )(*turned, *grads, *halo)


def small_grad_kernel(n, *refs):
    turned, refs = refs[:n], refs[n:]
    plain, refs = refs[:n], refs[n:]
    states, refs = refs[:n], refs[n:]
    steps, (before, state_out, step_out) = refs[:n], refs[n:]
    state, step = None, None
    for s in range(n):
        part = dot(turned[s][...], states[s][0, PAD:, :]) + dot_tn(before[s], states[s][0, :PAD, :])
        state = part if state is None else state + part
        part = dot_tn(steps[s][0], plain[s][...])
        step = part if step is None else step + part
    state_out[...] = state.astype(BF16)
    step_out[...] = step


def small_grad(turned, plain, states, steps, before):
    n = len(turned)
    model = turned[0].shape[0]
    return pl.pallas_call(
        functools.partial(small_grad_kernel, n),
        out_shape=[
            jax.ShapeDtypeStruct((model, 2 * LANES), BF16),
            jax.ShapeDtypeStruct((LANES, model), F32),
        ],
        compiler_params=pltpu.CompilerParams(vmem_limit_bytes=VMEM),
        name="small_weight_gradient",
    )(*turned, *plain, *states, *steps, before)


def swapped(value, axis, step):
    return lax.ppermute(value, axis, [(i, i ^ step) for i in range(lax.axis_size(axis))])


def gathered(value):
    parts = [value]
    for r in range(1, lax.axis_size("head")):
        parts.append(swapped(parts[r - 1], "head", 1) if r % 2 else swapped(value, "head", r))
    return parts


def scattered(parts, bits, shared=None):
    parts = list(parts)
    for bit in bits:
        kept = [r for r in range(len(parts)) if parts[r] is not None and not r & bit]
        send = [parts[r + bit] for r in kept] + ([] if shared is None else [shared])
        arrived = swapped(jnp.concatenate(send, axis=0), "head", bit)
        rows = parts[0].shape[0]
        for i, r in enumerate(kept):
            parts[r] = (parts[r].astype(F32) + arrived[i * rows : (i + 1) * rows].astype(F32)).astype(parts[r].dtype)
            parts[r + bit] = None
        if shared is not None:
            shared = shared + arrived[len(kept) * rows :]
    return parts, shared


def head_bits():
    return [1 << i for i in range((lax.axis_size("head") - 1).bit_length())]


def summed_weights(blocks_grads, ranges_first):
    bits = head_bits()
    parts, _ = scattered([blocks_grads[r] for r in range(blocks_grads.shape[0])], bits[:1])
    if ranges_first and len(bits) > 1:
        left = [r for r, part in enumerate(parts) if part is not None]
        width = blocks_grads.shape[2]
        total = ranges_sum(jnp.concatenate([parts[r] for r in left], axis=1))
        for i, r in enumerate(left):
            parts[r] = total[:, i * width : (i + 1) * width]
        return scattered(parts, bits[1:])[0][0]
    return ranges_sum(scattered(parts, bits[1:])[0][0])


def summed_over(value, axis):
    bit = 1
    while bit < lax.axis_size(axis):
        value = value + swapped(value, axis, bit)
        bit *= 2
    return value


def ranges_sum(value):
    ranges = lax.axis_size("seq")
    me = lax.axis_index("seq")
    rest = value.shape[1:]
    bit = 1
    while bit < ranges:
        mine = (me // bit) % 2
        halves = value.reshape((ranges // bit // 2, 2, -1) + rest)
        send = lax.dynamic_index_in_dim(halves, 1 - mine, 1, keepdims=False)
        keep = lax.dynamic_index_in_dim(halves, mine, 1, keepdims=False)
        total = keep.astype(F32) + swapped(send, "seq", bit).astype(F32)
        bit *= 2
        value = total.reshape((-1,) + rest).astype(value.dtype if bit < ranges else F32)
    return value


def assembled(parts, edges=None):
    n = len(parts)
    me = lax.axis_index("head")
    pieces, places, last_rows = [], [], []
    around = None if edges is None else gathered(jnp.concatenate(edges, axis=0))
    for s, value in enumerate(parts):
        for r, part in enumerate(gathered(value)):
            pieces.append(part)
            places.append((me ^ r) * n + s)
            if edges is not None:
                last_rows.append(around[r][s : s + 1])
    return assemble(pieces, last_rows, places)


def padded_lanes(value, size):
    return jnp.pad(value, ((0, 0), (0, size - value.shape[1])))


def shards(
    tokens,
    doc_ids,
    norm_gain,
    head_input_weight,
    state_input_weight,
    timestep_input_weight,
    conv_x,
    conv_state,
    head_params,
    gated_gain,
    output_weight,
    cotangent,
):
    seqs, length, model = tokens.shape
    blocks = lax.axis_size("head")
    ranges = lax.axis_size("seq")
    n = seqs // blocks
    width = gated_gain.shape[0]
    heads = head_params.shape[1]
    me = lax.axis_index("head")
    tokens = lax.dynamic_slice_in_dim(tokens, me * n, n, 0)
    cotangent = lax.dynamic_slice_in_dim(cotangent, me * n, n, 0)
    before = lax.ppermute(tokens[:, length - PAD :], "seq", [(i, i + 1) for i in range(ranges - 1)])
    padded = jnp.concatenate([before, tokens], axis=1)

    start = lax.axis_index("seq") * length
    lead = jnp.concatenate(
        [jnp.full((seqs, PAD), -1, jnp.int32), doc_ids, jnp.full((seqs, PAD), -2, jnp.int32)], axis=1
    )
    ids = lax.dynamic_slice(lead, (me * n, start), (n, length + 2 * PAD)).astype(F32)
    id_rows = jnp.broadcast_to(ids[:, None], (n, 8, length + 2 * PAD))
    ids = jnp.broadcast_to(ids[:, :, None], (n, length + 2 * PAD, LANES))

    pack = jnp.concatenate(
        [
            conv_x,
            gated_gain[None],
            padded_lanes(head_params, width),
            jnp.transpose(timestep_input_weight).astype(F32).reshape(heads * model // width, width),
        ],
        axis=0,
    )
    half = blocks // 2
    packs = gathered(pack)
    row_weights = gathered(head_input_weight[:, 1])
    gate_own = after(head_input_weight[:, 0], row_weights[half])
    out_own = after(output_weight, row_weights[half])
    packed = lambda rows: jnp.pad(jnp.concatenate(rows, axis=1), ((0, 0), (0, LANES - heads * blocks)))
    small = jnp.pad(packed([v[6:9, :heads] for v in packs]), ((0, 5), (0, 0)))
    step_weights = jnp.pad(
        jnp.concatenate([v[9:].reshape(heads, model) for v in packs]).astype(BF16), ((0, LANES - heads * blocks), (0, 0))
    )
    params = jnp.stack(
        [
            jnp.concatenate([v[:6], jnp.repeat(v[8, :heads], HEAD_DIM)[None], jnp.zeros((1, width), F32)], axis=0)
            for v in packs
        ]
    )
    state_taps = jnp.pad(conv_state, ((0, 3), (0, 0)))

    tok_float = padded.astype(F32)
    scale = lax.rsqrt(jnp.mean(tok_float * tok_float, axis=-1, keepdims=True) + EPS)
    normed = (tok_float * scale * norm_gain).astype(BF16)
    turned = [jnp.transpose(normed[s, PAD:]) for s in range(n)]
    turned_cotangent = [jnp.transpose(cotangent[s]) for s in range(n)]
    rows, raw, steps, log_decay, cum, state_rows, bc = project_first(
        normed, state_input_weight, step_weights, small, ids, id_rows, state_taps, row_weights[:half], blocks,
        heads * blocks,
    )
    cuts = ranges // (blocks * n)
    held = state_call(rows, bc, ids, id_rows, steps, cum, params, (), 0, half, heads, cuts)
    rows = project_more(normed, rows, row_weights[half:], half)
    acted, message = state_call(rows, bc, ids, id_rows, steps, cum, params, held, half, half, heads, cuts)
    mixed, states = inside_call(acted, bc, ids, id_rows, steps, cum, heads)
    entered = relay_back(relay_out(message, False, [mixed]), message)
    gate_weights = gathered(gate_own)
    out_weights = gathered(out_own)
    gate = project_gate(normed, gate_weights)
    entered = after(entered, gate)

    cuts = ranges // blocks
    middles, insides, closes, leaving = [], [], [], []
    ready = entered
    for s in range(n):
        middles.append(
            middle_call(s, mixed, gate, acted, cum, ready, bc, ids, tokens, cotangent, params, out_weights, heads, cuts)
        )
        ready = after(entered, middles[-1][4])
    whole_output = assembled([m[0] for m in middles])

    def inside_back(s, *others):
        d_summed = after(middles[s][3], *others)
        return inside_back_call(s, acted, d_summed, mixed, bc, ids, id_rows, steps, cum, states, entered, heads)

    def close(s, *others):
        d_scaled, d_b, d_c, d_cum = insides[s]
        return close_call(
            s, rows, acted, middles[s][3], d_scaled, bc, ids, id_rows, steps, raw, log_decay, cum, d_cum,
            after(leaving[s], *others), entered, params, small, state_rows, state_taps, d_b, d_c, heads,
        )

    for s, m in enumerate(middles):
        message = after(m[4], *leaving[-1:])
        meanwhile = [v[4] for v in middles[1:]]
        if s:
            insides.append(inside_back(s, leaving[-1]))
            meanwhile = [insides[s][3]]
        if s == n - 1:
            gate_grads = weight_grad([after(turned[0], message)] + turned[1:], [v[2] for v in middles])
            meanwhile.append(gate_grads)
        carried = relay_out(message, True, meanwhile)
        if s:
            closes.append(close(s - 1, carried))
            meanwhile = [closes[-1][0]]
        else:
            insides.append(inside_back(0, carried))
            out_grads = weight_grad(
                [after(turned_cotangent[0], carried)] + turned_cotangent[1:], [v[1] for v in middles]
            )
            meanwhile = [insides[0][3], out_grads]
        if s == n - 1:
            meanwhile.append(whole_output)
        leaving.append(after(relay_back(carried, message), *meanwhile))
    closes.append(close(n - 1))
    before = normed[:, :PAD]
    rows_grads = weight_grad(turned, [c[0] for c in closes], before)

    input_parts, edges, norm_parts = [], [], []
    gain = after(norm_gain[None], rows_grads)
    for s, (m, (d_rows, d_raw, d_state, *_)) in enumerate(zip(middles, closes)):
        input_grad, edge, halo, gain_part = input_call(
            s, m[2], d_rows, d_raw, d_state, padded, cotangent, gain, state_input_weight, step_weights,
            row_weights, gate_weights,
        )
        halo = lax.ppermute(halo, "seq", [(i + 1, i) for i in range(ranges - 1)])
        edges.append((edge + halo.astype(F32)).astype(BF16))
        input_parts.append(input_grad)
        norm_parts.append(gain_part)
    whole_input = assembled(input_parts, edges)

    plain = [normed[s, PAD:] for s in range(n)]
    out_grad = jnp.transpose(summed_weights(out_grads, False))
    heads_grad = jnp.stack([summed_weights(gate_grads, False), summed_weights(rows_grads, True)], axis=1)
    state_total, step_grads = small_grad(turned, plain, [c[2] for c in closes], [c[1] for c in closes], before)
    state_grad = summed_over(ranges_sum(state_total), "head")

    taps = sum(c[3] for c in closes)
    state_taps_grad = sum(c[4] for c in closes)
    rest = sum(c[5] for c in closes)
    gains = jnp.sum(sum(m[5] for m in middles), axis=1)
    skip_grads = jnp.sum(jnp.sum(sum(m[6] for m in middles), axis=1).reshape(blocks, heads, HEAD_DIM), axis=2)
    smalls = []
    for r in range(blocks):
        mine = slice(r * heads, (r + 1) * heads)
        head_rows = padded_lanes(jnp.concatenate([rest[:2, mine], skip_grads[r : r + 1]], axis=0), width)
        smalls.append(
            jnp.concatenate([taps[r, :5], gains[r : r + 1], head_rows, step_grads[mine].reshape(-1, width)], axis=0)
        )
    shared = jnp.concatenate([jnp.sum(sum(norm_parts), axis=0), state_taps_grad[:5].reshape(-1)])
    shared = jnp.pad(shared, (0, -shared.shape[0] % width)).reshape(-1, width)
    parts, shared = scattered(smalls, head_bits(), shared)
    own = parts[0]
    count = own.shape[0]
    both = summed_over(jnp.concatenate([own, shared], axis=0), "seq")
    own, shared = both[:count], both[count:].reshape(-1)
    return (
        whole_output,
        whole_input,
        shared[:model],
        heads_grad,
        state_grad,
        jnp.transpose(own[9:].reshape(heads, model)),
        own[:5],
        shared[model : model + 10 * LANES].reshape(5, 2 * LANES),
        own[6:9, :heads],
        own[5],
        out_grad,
    )


def solution(mesh):
    return jax.shard_map(
        shards,
        mesh=mesh,
        in_specs=(
            P(None, "seq", None),
            P(),
            P(),
            P(None, None, "head"),
            P(),
            P(None, "head"),
            P(None, "head"),
            P(),
            P(None, "head"),
            P("head"),
            P("head", None),
            P(None, "seq", None),
        ),
        out_specs=(
            P(None, "seq", None),
            P(None, "seq", None),
            P(),
            P("seq", None, "head"),
            P("seq", None),
            P(None, "head"),
            P(None, "head"),
            P(),
            P(None, "head"),
            P("head"),
            P("head", "seq"),
        ),
        check_vma=False,
    )
```

time: 661 us -> 553 us (0.84)
  waiting for transfers between devices: 177 us -> 122 us
  matrix products: 44.7 us -> 0 us
  other arithmetic: 37.9 us -> 30.2 us
    dot_general x17 -> x0, matrix products: 44.7 us -> none  [the longest x13 43.1 us: over_tokens(): return jnp.einsum('std,stc->dc', a, b, preferred_element_type=F32)]
    ppermute x37 -> x52, waiting for transfers between devices: 135 us -> 104 us  [swapped(): lax.ppermute(value, axis, [(i, i ^ step) for i in range(lax.axis_size(axi...]
    all_to_all x8 -> x6, waiting for transfers between devices: 41.8 us -> 12.6 us  [the longest x3 8.79 us: relay_out(): lax.all_to_all(message.reshape(ranges, rows, width), 'seq', 0, 0, tiled=T...]
    dynamic_update_slice x8 -> x0, local copies, waits for them, and re-layouts: 23.1 us -> none  [assembled(): whole = lax.dynamic_update_slice(whole, part, ((me ^ r) * n, 0, 0))]
    all_to_all x8 -> x6, starting transfers between devices: 43.6 us -> 31.8 us  [the longest x3 16.2 us: relay_back(): lax.all_to_all(carried, 'seq', 0, 0, tiled=True)]
    slice x16 -> x20, local copies, waits for them, and re-layouts: 3.77 us -> 15 us  [the longest x1 6.51 us: shards(): gate_own = after(head_input_weight[:, 0], row_weights[half])]
    ppermute x37 -> x52, starting transfers between devices: 29.2 us -> 40.2 us  [swapped(): lax.ppermute(value, axis, [(i, i ^ step) for i in range(lax.axis_size(axi...]
    squeeze x4 -> x21, local copies, waits for them, and re-layouts: 0.01 us -> 10.5 us  [the longest x3 5.03 us: summed_weights(): blocks_grads[r]]
  transfers between devices with their start and end apart: 47 -> 61, of which waited for: 11 -> 22; matrix products, arithmetic and copies ran while one was open for 19% -> 14% of each run, Pallas kernels for 23% -> 39%
where the time goes in v2:
time: 553 us; the launch traced here: 542 us
  Pallas kernels  252 us (46%)
  waiting for transfers between devices  122 us (22%)
  starting transfers between devices  78.7 us (14%)
  local copies, waits for them, and re-layouts  57.1 us (10%)
  other arithmetic  30.2 us (5%)
    ppermute x52, waiting for transfers between devices, swapped(): lax.ppermute(value, axis, [(i, i ^ step) for i in range(lax.axis_size(axi...  104 us
    pallas_call x2, Pallas kernels, middle_call(): pl.pallas_call(functools.partial(middle_kernel, blocks, per_block, width...  47 us
    ppermute x52, starting transfers between devices, swapped(): lax.ppermute(value, axis, [(i, i ^ step) for i in range(lax.axis_size(axi...  40.2 us
    pallas_call x2, Pallas kernels, close_call(): pl.pallas_call(functools.partial(close_kernel, per_block), grid=(blocks,)...  36.8 us
    pallas_call x2, Pallas kernels, inside_back_call(): pl.pallas_call(functools.partial(inside_back_kernel, per_block), grid=(bl...  31.3 us
    pallas_call x2, Pallas kernels, input_call(): pl.pallas_call(functools.partial(input_kernel, blocks), grid=(1,), in_spe...  28.5 us
    pallas_call x3, Pallas kernels, weight_grad(): pl.pallas_call(functools.partial(weight_grad_kernel, n, len(halo)), grid=...  26.9 us
    pallas_call x1, Pallas kernels, inside_call(): pl.pallas_call(functools.partial(inside_kernel, per_block), grid=(n, bloc...  18.1 us
  transfers between devices with their start and end apart: 61, of which 22 were waited for; matrix products, arithmetic and copies ran while one was open for 14% of the time, Pallas kernels for 39%

profile of v2, /device:TPU:0, one launch (start us, length us, event | category | flops | bytes accessed | tf_op | source)
XLA Modules:
  0.0 541.8 jit_solution(11286986146449824975)
XLA Ops:
  2.1 3.0 collective-permute-start.2
  5.2 6.5 %fusion.27 = (bf16[1024,1,512]{2,1,0:T(2,128)(2,1)}, bf16[1024,1,512]{2,1,0:T(2,128)(2,1)S(1)}) fusion(bf16[1024,2,512]{2,1,0:T(2,128)(2,1)} %param.15), kind=kLoop, calls=%fused_computation.140 | loop fusion | bytes 4194304 | tf_op jit(solution)/shard_map/slice | solution.py:1142
  13.5 3.9 collective-permute-start
  17.5 4.2 constant_dynamic-slice_fusion.5
  29.7 8.1 %collective-permute-done.5.refs_0_.refs_2_ = bf16[1024,512]{1,0:T(8,128)(2,1)} collective-permute-done((bf16[1024,512]{1,0:T(8,128)(2,1)S(1)}, bf16[1024,512]{1,0:T(8,128)(2,1)}, u32[]{:S(2)}, u32[]{:S(2)}) %collective-permute-start.5) | collective-permute-done | bytes 1048608 | tf_op jit(solution)/shard_map/ppermute | solution.py:1012
  43.7 8.8 %project_first.1 = (bf16[4,2,528,512]{3,2,1,0:T(8,128)(2,1)}, f32[2,512,128]{2,1,0:T(8,128)}, f32[2,512,128]{2,1,0:T(8,128)}, f32[2,512,128]{2,1,0:T(8,128)}, f3...) custom-call(bf16[2,528,1024]{2,1,0:T(8,128)(2,1)} %fusion.2.normed, ...), custom_call_target="tpu_custom_call" | custom-call | tf_op jit(solution)/shard_map/project_first/pallas_call | solution.py:228
  52.4 6.9 %range_state.2 = (bf16[4,2,512,512]{3,2,1,0:T(8,128)(2,1)}, bf16[4,2,1,144,512]{4,3,2,1,0:T(8,128)(2,1)}) custom-call(bf16[4,2,528,512]{3,2,1,0:T(8,128)(2,1)} %get-tuple-element.84.held.rows, bf16[2,512,256]{2,1,0:T(8,128)(2,1)} %get-tuple-element.85.bc, f32[2,544,128]{2,1,0:T(8,128)} %broadcast_in_dim.43.ids.ids_before.ids_after, ...), custom_call_target="tpu_custom_call" | custom-call | tf_op jit(solution)/shard_map/range_state/pallas_call | solution.py:324
  59.3 5.5 %project_more.1.rows = bf16[4,2,528,512]{3,2,1,0:T(8,128)(2,1)} custom-call(bf16[2,528,1024]{2,1,0:T(8,128)(2,1)} %fusion.2.normed, bf16[4,2,528,512]{3,2,1,0:T(8,128)(2,1)} %get-tuple-element.84.held.rows, bf16[1024,512]{1,0:T(8,128)(2,1)} %collective-permute-done.5.refs_0_.refs_2_, ...), custom_call_target="tpu_custom_call", output_to_operand_aliasing={{}: (1, {})} | custom-call | tf_op jit(solution)/shard_map/project_more/pallas_call | solution.py:252
  64.9 6.9 %range_state.3 = (bf16[4,2,512,512]{3,2,1,0:T(8,128)(2,1)}, bf16[4,2,1,144,512]{4,3,2,1,0:T(8,128)(2,1)}) custom-call(bf16[4,2,528,512]{3,2,1,0:T(8,128)(2,1)} %project_more.1.rows, bf16[2,512,256]{2,1,0:T(8,128)(2,1)} %get-tuple-element.85.bc, ...), custom_call_target="tpu_custom_call", output_to_operand_aliasing={{0}: (7, {}), {1}: (8, {})} | custom-call | tf_op jit(solution)/shard_map/range_state/pallas_call | solution.py:324
  71.8 6.0 %all-to-all-start = ((bf16[8,144,512]{2,1,0:T(8,128)(2,1)}), bf16[8,144,512]{2,1,0:T(8,128)(2,1)}, u32[]{:S(2)}, u32[]{:S(2)}) async-start(bf16[8,144,512]{2,1,0:T(8,128)(2,1)} %bitcast.200), calls=%async_computation | async-start | bytes 2359296 | tf_op jit(solution)/shard_map/all_to_all | solution.py:441
  80.2 18.1 %inside.1 = (f32[4,2,512,512]{3,2,1,0:T(8,128)}, bf16[4,2,3,128,512]{4,3,2,1,0:T(8,128)(2,1)}) custom-call(bf16[4,2,512,512]{3,2,1,0:T(8,128)(2,1)} %get-tuple-element.90.acted, bf16[2,512,256]{2,1,0:T(8,128)(2,1)} %get-tuple-element.85.bc, f32[2,544,128]{2,1,0:T(8,128)} %broadcast_in_dim.43.ids.ids_before.ids_after, f32[2,8,544]{2,1,0:T(8,128)} %broadcast_in_dim.44.id_rows, ...), custom_call_target="tpu_custom_call" | custom-call | tf_op jit(solution)/shard_map/inside/pallas_call | solution.py:406
  98.3 8.8 %all-to-all-done.message = bf16[8,144,512]{2,1,0:T(8,128)(2,1)} async-done(((bf16[8,144,512]{2,1,0:T(8,128)(2,1)}), bf16[8,144,512]{2,1,0:T(8,128)(2,1)}, u32[]{:S(2)}, u32[]{:S(2)}) %all-to-all-start) | async-done | bytes 1179680 | tf_op jit(solution)/shard_map/all_to_all | solution.py:441
  107.1 2.5 relay.3
  109.6 3.8 all-to-all-start.1
  114.2 11.8 %collective-permute-done.11.refs_2_ = bf16[512,1024]{1,0:T(8,128)(2,1)} collective-permute-done((bf16[512,1024]{1,0:T(8,128)(2,1)}, bf16[512,1024]{1,0:T(8,128)(2,1)}, u32[]{:S(2)}, u32[]{:S(2)}) %collective-permute-start.11) | collective-permute-done | bytes 1048608 | tf_op jit(solution)/shard_map/ppermute | solution.py:1012
  127.1 8.5 %project_gate.1.gate = bf16[4,2,512,512]{3,2,1,0:T(8,128)(2,1)} custom-call(bf16[2,528,1024]{2,1,0:T(8,128)(2,1)} %fusion.2.normed, bf16[1024,512]{1,0:T(8,128)(2,1)} %bitcast.195, bf16[1024,512]{1,0:T(8,128)(2,1)} %copy-done.7, bf16[1024,512]{1,0:T(8,128)(2,1)} %copy-done.6, bf16[1024,512]{1,0:T(8,128)(2,1)} %collective-permute-done.9.refs_3_.refs_7_), custom_call_target="tpu_custom_call" | custom-call | tf_op jit(solution)/shard_map/project_gate/pallas_call | solution.py:274
  135.7 3.8 all-to-all-done.1
  140.7 23.4 %middle.2 = (bf16[1,512,1024]{2,1,0:T(8,128)(2,1)}, bf16[4,1,512,512]{3,2,1,0:T(8,128)(2,1)}, bf16[4,1,512,512]{3,2,1,0:T(8,128)(2,1)}, bf16[4,1,512,512]{3,2,1,...) custom-call(f32[4,2,512,512]{3,2,1,0:T(8,128)} %get-tuple-element.91.mixed, ...), custom_call_target="tpu_custom_call" | custom-call | tf_op jit(solution)/shard_map/middle/pallas_call | solution.py:572
  164.1 3.6 all-to-all-start.2
  167.8 23.6 %middle.3 = (bf16[1,512,1024]{2,1,0:T(8,128)(2,1)}, bf16[4,1,512,512]{3,2,1,0:T(8,128)(2,1)}, bf16[4,1,512,512]{3,2,1,0:T(8,128)(2,1)}, bf16[4,1,512,512]{3,2,1,...) custom-call(f32[4,2,512,512]{3,2,1,0:T(8,128)} %get-tuple-element.91.mixed, ...), custom_call_target="tpu_custom_call" | custom-call | tf_op jit(solution)/shard_map/middle/pallas_call | solution.py:572
  194.2 6.4 %all-to-all-start.3 = ((bf16[8,64,512]{2,1,0:T(8,128)(2,1)}), bf16[8,64,512]{2,1,0:T(8,128)(2,1)S(1)}, u32[]{:S(2)}, u32[]{:S(2)}) async-start(bf16[8,64,512]{2,1,0:T(8,128)(2,1)} %relay.4), calls=%async_computation.3 | async-start | bytes 1048576 | tf_op jit(solution)/shard_map/all_to_all | solution.py:452
  207.0 8.3 %weight_gradient.3 = bf16[4,1024,512]{2,1,0:T(8,128)(2,1)} custom-call(bf16[1024,512]{1,0:T(8,128)(2,1)} %copy.54.refs_0_, bf16[1024,512]{1,0:T(8,128)(2,1)} %copy.55.refs_1_, bf16[4,1,512,512]{3,2,1,0:T(8,128)(2,1)} %get-tuple-element.112.refs_2_, bf16[4,1,512,512]{3,2,1,0:T(8,128)(2,1)} %get-tuple-element.113.refs_3_), custom_call_target="tpu_custom_call" | custom-call | tf_op jit(solution)/shard_map/weight_gradient/pallas_call | solution.py:969
  218.5 15.7 %inside_back.2 = (bf16[4,1,512,512]{3,2,1,0:T(8,128)(2,1)}, f32[1,512,128]{2,1,0:T(8,128)}, f32[1,512,128]{2,1,0:T(8,128)}, f32[1,512,128]{2,1,0:T(8,128)}) custom-call(bf16[4,2,512,512]{3,2,1,0:T(8,128)(2,1)} %get-tuple-element.90.acted, bf16[4,1,512,512]{3,2,1,0:T(8,128)(2,1)} %get-tuple-element.105.d_summed, f32[4,2,512,512]{3,2,1,0:T(8,128)} %get-tuple-element.91.mixed, ...), custom_call_target="tpu_custom_call" | custom-call | tf_op jit(solution)/shard_map/inside_back/pallas_call | solution.py:688
  234.2 6.0 %all-to-all-start.4 = ((bf16[8,80,512]{2,1,0:T(8,128)(2,1)}), bf16[8,80,512]{2,1,0:T(8,128)(2,1)}, u32[]{:S(2)}, u32[]{:S(2)}) async-start(bf16[8,80,512]{2,1,0:T(8,128)(2,1)} %bitcast.28), calls=%async_computation.4 | async-start | bytes 1310720 | tf_op jit(solution)/shard_map/all_to_all | solution.py:441
  243.4 2.4 copy.57.refs_1_
  252.3 15.6 %inside_back.3 = (bf16[4,1,512,512]{3,2,1,0:T(8,128)(2,1)}, f32[1,512,128]{2,1,0:T(8,128)}, f32[1,512,128]{2,1,0:T(8,128)}, f32[1,512,128]{2,1,0:T(8,128)}) custom-call(bf16[4,2,512,512]{3,2,1,0:T(8,128)(2,1)} %get-tuple-element.90.acted, bf16[4,1,512,512]{3,2,1,0:T(8,128)(2,1)} %get-tuple-element.117.d_summed, f32[4,2,512,512]{3,2,1,0:T(8,128)} %get-tuple-element.91.mixed, ...), custom_call_target="tpu_custom_call" | custom-call | tf_op jit(solution)/shard_map/inside_back/pallas_call | solution.py:688
  267.9 8.3 %weight_gradient.4 = bf16[4,1024,512]{2,1,0:T(8,128)(2,1)} custom-call(bf16[1024,512]{1,0:T(8,128)(2,1)} %copy.56.refs_0_, bf16[1024,512]{1,0:T(8,128)(2,1)} %copy.57.refs_1_, bf16[4,1,512,512]{3,2,1,0:T(8,128)(2,1)} %get-tuple-element.101.refs_2_.d_gate, bf16[4,1,512,512]{3,2,1,0:T(8,128)(2,1)} %get-tuple-element.120.refs_3_.d_gate), custom_call_target="tpu_custom_call" | custom-call | tf_op jit(solution)/shard_map/weight_gradient/pallas_call | solution.py:969
  278.2 5.9 %all-to-all-start.5 = ((bf16[8,64,512]{2,1,0:T(8,128)(2,1)}), bf16[8,64,512]{2,1,0:T(8,128)(2,1)S(1)}, u32[]{:S(2)}, u32[]{:S(2)}) async-start(bf16[8,64,512]{2,1,0:T(8,128)(2,1)} %relay.5), calls=%async_computation.5 | async-start | bytes 1048576 | tf_op jit(solution)/shard_map/all_to_all | solution.py:452
  288.2 7.1 %assemble.2 = bf16[8,512,1024]{2,1,0:T(8,128)(2,1)} custom-call(s32[8]{0:T(128)} %stack.65.places, bf16[1,512,1024]{2,1,0:T(8,128)(2,1)} %get-tuple-element.97.refs_0_, bf16[1,512,1024]{2,1,0:T(8,128)(2,1)} %collective-permute-done.13.refs_1_, bf16[1,512,1024]{2,1,0:T(8,128)(2,1)} %collective-permute-done.14.refs_2_, ...), custom_call_target="tpu_custom_call" | custom-call | tf_op jit(solution)/shard_map/assemble/pallas_call | solution.py:932
  295.3 18.4 %close.2 = (bf16[4,1,528,512]{3,2,1,0:T(8,128)(2,1)}, bf16[1,512,128]{2,1,0:T(8,128)(2,1)}, bf16[1,528,256]{2,1,0:T(8,128)(2,1)}, f32[4,8,512]{2,1,0:T(8,128)}, f32[8,256]{1,0:T(8,128)}, /*index=5*/f32[8,128]{1,0:T(8,128)}) custom-call(bf16[4,2,528,512]{3,2,1,0:T(8,128)(2,1)} %project_more.1.rows, bf16[4,2,512,512]{3,2,1,0:T(8,128)(2,1)} %get-tuple-element.90.acted, ...), custom_call_target="tpu_custom_call" | custom-call | tf_op jit(solution)/shard_map/close/pallas_call | solution.py:812
  313.7 2.8 fusion.3
  317.8 18.5 %close.3 = (bf16[4,1,528,512]{3,2,1,0:T(8,128)(2,1)}, bf16[1,512,128]{2,1,0:T(8,128)(2,1)}, bf16[1,528,256]{2,1,0:T(8,128)(2,1)}, f32[4,8,512]{2,1,0:T(8,128)}, f32[8,256]{1,0:T(8,128)}, /*index=5*/f32[8,128]{1,0:T(8,128)}) custom-call(bf16[4,2,528,512]{3,2,1,0:T(8,128)(2,1)} %project_more.1.rows, bf16[4,2,512,512]{3,2,1,0:T(8,128)(2,1)} %get-tuple-element.90.acted, ...), custom_call_target="tpu_custom_call" | custom-call | tf_op jit(solution)/shard_map/close/pallas_call | solution.py:812
  336.3 4.6 small_weight_gradient.1
  343.9 10.4 %weight_gradient.5 = bf16[4,1024,512]{2,1,0:T(8,128)(2,1)} custom-call(bf16[1024,512]{1,0:T(8,128)(2,1)} %copy.58.refs_0_, bf16[1024,512]{1,0:T(8,128)(2,1)} %copy.57.refs_1_, bf16[4,1,528,512]{3,2,1,0:T(8,128)(2,1)} %get-tuple-element.126.refs_2_.d_rows, bf16[4,1,528,512]{3,2,1,0:T(8,128)(2,1)} %get-tuple-element.133.refs_3_.d_rows, ...), custom_call_target="tpu_custom_call" | custom-call | tf_op jit(solution)/shard_map/weight_gradient/pallas_call | solution.py:969
  357.6 14.2 %input_gradient.3 = (bf16[1,512,1024]{2,1,0:T(8,128)(2,1)}, f32[1,16,1024]{2,1,0:T(8,128)}, bf16[1,16,1024]{2,1,0:T(8,128)(2,1)}, f32[8,1024]{1,0:T(8,128)}) custom-call(bf16[4,1,512,512]{3,2,1,0:T(8,128)(2,1)} %get-tuple-element.120.refs_3_.d_gate, bf16[4,1,528,512]{3,2,1,0:T(8,128)(2,1)} %get-tuple-element.133.refs_3_.d_rows, ...), custom_call_target="tpu_custom_call" | custom-call | tf_op jit(solution)/shard_map/input_gradient/pallas_call | solution.py:891
  373.3 14.2 %input_gradient.2 = (bf16[1,512,1024]{2,1,0:T(8,128)(2,1)}, f32[1,16,1024]{2,1,0:T(8,128)}, bf16[1,16,1024]{2,1,0:T(8,128)(2,1)}, f32[8,1024]{1,0:T(8,128)}) custom-call(bf16[4,1,512,512]{3,2,1,0:T(8,128)(2,1)} %get-tuple-element.101.refs_2_.d_gate, bf16[4,1,528,512]{3,2,1,0:T(8,128)(2,1)} %get-tuple-element.126.refs_2_.d_rows, ...), custom_call_target="tpu_custom_call" | custom-call | tf_op jit(solution)/shard_map/input_gradient/pallas_call | solution.py:891
  391.4 5.1 collective-permute-done.25
  398.9 2.9 fusion.8
  406.5 22.2 %collective-permute-done.31 = f32[30,512]{1,0:T(8,128)S(1)} collective-permute-done((f32[30,512]{1,0:T(8,128)S(1)}, f32[30,512]{1,0:T(8,128)S(1)}, u32[]{:S(2)}, u32[]{:S(2)}) %collective-permute-start.31) | collective-permute-done | bytes 61472 | tf_op jit(solution)/shard_map/ppermute | solution.py:1012
  430.0 2.9 collective-permute-start.32
  460.2 3.3 collective-permute-done.49
  469.2 12.9 %collective-permute-done.41 = bf16[4,128,1024]{2,1,0:T(8,128)(2,1)S(1)} collective-permute-done((bf16[4,128,1024]{2,1,0:T(8,128)(2,1)S(1)}, bf16[4,128,1024]{2,1,0:T(8,128)(2,1)S(1)}, u32[]{:S(2)}, u32[]{:S(2)}) %collective-permute-start.41) | collective-permute-done | bytes 1048608 | tf_op jit(solution)/shard_map/ppermute | solution.py:1012
  484.8 10.8 %collective-permute-done.37 = bf16[4,128,512]{2,1,0:T(8,128)(2,1)S(1)} collective-permute-done((bf16[4,128,512]{2,1,0:T(8,128)(2,1)S(1)}, bf16[4,128,512]{2,1,0:T(8,128)(2,1)S(1)}, u32[]{:S(2)}, u32[]{:S(2)}) %collective-permute-start.37) | collective-permute-done | bytes 524320 | tf_op jit(solution)/shard_map/ppermute | solution.py:1012
  500.0 3.7 collective-permute-done.54
  503.7 3.1 collective-permute-done.38
  507.9 12.3 %collective-permute-done.43 = bf16[1,128,1024]{2,1,0:T(8,128)(2,1)S(1)} collective-permute-done((bf16[1,128,1024]{2,1,0:T(8,128)(2,1)S(1)}, bf16[1,128,1024]{2,1,0:T(8,128)(2,1)S(1)}, u32[]{:S(2)}, u32[]{:S(2)}) %collective-permute-start.43) | collective-permute-done | bytes 262176 | tf_op jit(solution)/shard_map/ppermute | solution.py:1012
  521.0 7.3 %collective-permute-done.39 = bf16[1,128,512]{2,1,0:T(8,128)(2,1)S(1)} collective-permute-done((bf16[1,128,512]{2,1,0:T(8,128)(2,1)S(1)}, bf16[1,128,512]{2,1,0:T(8,128)(2,1)S(1)}, u32[]{:S(2)}, u32[]{:S(2)}) %collective-permute-start.39) | collective-permute-done | bytes 131104 | tf_op jit(solution)/shard_map/ppermute | solution.py:1012
  531.2 8.0 %assemble.3 = bf16[8,512,1024]{2,1,0:T(8,128)(2,1)} custom-call(s32[8]{0:T(128)} %stack.65.places, bf16[1,512,1024]{2,1,0:T(8,128)(2,1)} %get-tuple-element.135.refs_0_, bf16[1,512,1024]{2,1,0:T(8,128)(2,1)} %collective-permute-done.19.refs_1_, bf16[1,512,1024]{2,1,0:T(8,128)(2,1)} %collective-permute-done.20.refs_2_, ...), custom_call_target="tpu_custom_call" | custom-call | tf_op jit(solution)/shard_map/assemble/pallas_call | solution.py:932
  (323 shorter events, 118.2 us)
Async XLA Ops:
  2.1 20.8 %collective-permute-start.2 = (f32[25,512]{1,0:T(8,128)S(1)}, f32[25,512]{1,0:T(8,128)}, u32[]{:S(2)}, u32[]{:S(2)}) collective-permute-start(f32[25,512]{1,0:T(8,128)S(1)} %fusion.25), channel_id=1, source_target_pairs={{0,2},{1,3},{2,0},{3,1},{4,6},{5,7},{6,4},{7,5},{8,10},{9,11},{10,... | collective-permute-start | bytes 153608 | tf_op jit(solution)/shard_map/ppermute | solution.py:1012
  5.2 18.5 %collective-permute-start.1 = (f32[25,512]{1,0:T(8,128)S(1)}, f32[25,512]{1,0:T(8,128)}, u32[]{:S(2)}, u32[]{:S(2)}) collective-permute-start(f32[25,512]{1,0:T(8,128)S(1)} %fusion.25), channel_id=1, source_target_pairs={{0,1},{1,0},{2,3},{3,2},{4,5},{5,4},{6,7},{7,6},{8,9},{9,8},{10,11... | collective-permute-start | bytes 153608 | tf_op jit(solution)/shard_map/ppermute | solution.py:1012
  12.0 30.0 %collective-permute-start.4 = (bf16[1024,512]{1,0:T(8,128)(2,1)S(1)}, bf16[1024,512]{1,0:T(8,128)(2,1)}, u32[]{:S(2)}, u32[]{:S(2)}) collective-permute-start(bf16[1024,512]{1,0:T(8,128)(2,1)S(1)} %bitcast.188), channel_id=1, source_target_pairs={{0,1},{1,0},{2,3},{3,2},{4,5},{5,4},{6,7},{7,6},{8,9},{9,8},{10,11... | collective-permute-start | bytes 3145736 | tf_op jit(solution)/shard_map/ppermute | solution.py:1012
  12.5 25.2 %collective-permute-start.5 = (bf16[1024,512]{1,0:T(8,128)(2,1)S(1)}, bf16[1024,512]{1,0:T(8,128)(2,1)}, u32[]{:S(2)}, u32[]{:S(2)}) collective-permute-start(bf16[1024,512]{1,0:T(8,128)(2,1)S(1)} %bitcast.189), channel_id=1, source_target_pairs={{0,2},{1,3},{2,0},{3,1},{4,6},{5,7},{6,4},{7,5},{8,10},{9,11},{10,... | collective-permute-start | bytes 3145736 | tf_op jit(solution)/shard_map/ppermute | solution.py:1012
  13.5 15.6 %collective-permute-start = (bf16[2,16,1024]{2,1,0:T(8,128)(2,1)S(1)}, bf16[2,16,1024]{2,1,0:T(8,128)(2,1)S(1)}, u32[]{:S(2)}, u32[]{:S(2)}) collective-permute-start(bf16[2,16,1024]{2,1,0:T(8,128)(2,1)S(1)} %constant_dynamic-slice_fusion), channel_id=1, source_target_pairs={{0,4},{4,8},{8,12},{12,16},{16,20},{20,24},{24,28},{1,5},{5,9},{9,... | collective-permute-start | bytes 196616 | tf_op jit(solution)/shard_map/ppermute | solution.py:1119
  26.3 13.4 %collective-permute-start.3 = (f32[25,512]{1,0:T(8,128)}, f32[25,512]{1,0:T(8,128)S(1)}, u32[]{:S(2)}, u32[]{:S(2)}) collective-permute-start(f32[25,512]{1,0:T(8,128)} %collective-permute-done.2), channel_id=1, source_target_pairs={{0,1},{1,0},{2,3},{3,2},{4,5},{5,4},{6,7},{7,6},{8,9},{9,8},{10,11... | collective-permute-start | bytes 153608 | tf_op jit(solution)/shard_map/ppermute | solution.py:1012
  37.8 21.6 %collective-permute-start.6 = (bf16[1024,512]{1,0:T(8,128)(2,1)}, bf16[1024,512]{1,0:T(8,128)(2,1)}, u32[]{:S(2)}, u32[]{:S(2)}) collective-permute-start(bf16[1024,512]{1,0:T(8,128)(2,1)} %collective-permute-done.5.refs_0_.refs_2_), channel_id=1, source_target_pairs={{0,1},{1,0},{2,3},{3,2},{4,5},{5,4},{6,7},{7,6},{8,9},{9,8},{10,11... | collective-permute-start | bytes 3145736 | tf_op jit(solution)/shard_map/ppermute | solution.py:1012
  71.8 35.3 %all-to-all-start = ((bf16[8,144,512]{2,1,0:T(8,128)(2,1)}), bf16[8,144,512]{2,1,0:T(8,128)(2,1)}, u32[]{:S(2)}, u32[]{:S(2)}) async-start(bf16[8,144,512]{2,1,0:T(8,128)(2,1)} %bitcast.200), calls=%async_computation | async-start | bytes 2359296 | tf_op jit(solution)/shard_map/all_to_all | solution.py:441
  78.1 35.5 %collective-permute-start.8 = (bf16[1024,512]{1,0:T(8,128)(2,1)S(1)}, bf16[1024,512]{1,0:T(8,128)(2,1)S(1)}, u32[]{:S(2)}, u32[]{:S(2)}) collective-permute-start(bf16[1024,512]{1,0:T(8,128)(2,1)S(1)} %bitcast.193), channel_id=1, source_target_pairs={{0,2},{1,3},{2,0},{3,1},{4,6},{5,7},{6,4},{7,5},{8,10},{9,11},{10,... | collective-permute-start | bytes 3145736 | tf_op jit(solution)/shard_map/ppermute | solution.py:1012
  78.7 47.3 %collective-permute-start.11 = (bf16[512,1024]{1,0:T(8,128)(2,1)}, bf16[512,1024]{1,0:T(8,128)(2,1)}, u32[]{:S(2)}, u32[]{:S(2)}) collective-permute-start(bf16[512,1024]{1,0:T(8,128)(2,1)} %refs_0_.1), channel_id=1, source_target_pairs={{0,2},{1,3},{2,0},{3,1},{4,6},{5,7},{6,4},{7,5},{8,10},{9,11},{10,... | collective-permute-start | bytes 3145736 | tf_op jit(solution)/shard_map/ppermute | solution.py:1012
  109.6 29.8 %all-to-all-start.1 = ((bf16[8,128,512]{2,1,0:T(8,128)(2,1)}), bf16[8,128,512]{2,1,0:T(8,128)(2,1)S(1)}, u32[]{:S(2)}, u32[]{:S(2)}) async-start(bf16[8,128,512]{2,1,0:T(8,128)(2,1)} %relay.3), calls=%async_computation.1 | async-start | bytes 2097152 | tf_op jit(solution)/shard_map/all_to_all | solution.py:452
  113.5 12.6 %collective-permute-start.7 = (bf16[1024,512]{1,0:T(8,128)(2,1)S(1)}, bf16[1024,512]{1,0:T(8,128)(2,1)S(1)}, u32[]{:S(2)}, u32[]{:S(2)}) collective-permute-start(bf16[1024,512]{1,0:T(8,128)(2,1)S(1)} %bitcast.194), channel_id=1, source_target_pairs={{0,1},{1,0},{2,3},{3,2},{4,5},{5,4},{6,7},{7,6},{8,9},{9,8},{10,11... | collective-permute-start | bytes 3145736 | tf_op jit(solution)/shard_map/ppermute | solution.py:1012
  113.6 13.5 %collective-permute-start.9 = (bf16[1024,512]{1,0:T(8,128)(2,1)S(1)}, bf16[1024,512]{1,0:T(8,128)(2,1)}, u32[]{:S(2)}, u32[]{:S(2)}) collective-permute-start(bf16[1024,512]{1,0:T(8,128)(2,1)S(1)} %collective-permute-done.8.refs_2_.refs_6_), channel_id=1, source_target_pairs={{0,1},{1,0},{2,3},{3,2},{4,5},{5,4},{6,7},{7,6},{8,9},{9,8},{10,11... | collective-permute-start | bytes 3145736 | tf_op jit(solution)/shard_map/ppermute | solution.py:1012
  114.1 25.4 %collective-permute-start.10 = (bf16[512,1024]{1,0:T(8,128)(2,1)}, bf16[512,1024]{1,0:T(8,128)(2,1)}, u32[]{:S(2)}, u32[]{:S(2)}) collective-permute-start(bf16[512,1024]{1,0:T(8,128)(2,1)} %refs_0_.1), channel_id=1, source_target_pairs={{0,1},{1,0},{2,3},{3,2},{4,5},{5,4},{6,7},{7,6},{8,9},{9,8},{10,11... | collective-permute-start | bytes 3145736 | tf_op jit(solution)/shard_map/ppermute | solution.py:1012
  126.0 13.5 %collective-permute-start.12 = (bf16[512,1024]{1,0:T(8,128)(2,1)}, bf16[512,1024]{1,0:T(8,128)(2,1)}, u32[]{:S(2)}, u32[]{:S(2)}) collective-permute-start(bf16[512,1024]{1,0:T(8,128)(2,1)} %collective-permute-done.11.refs_2_), channel_id=1, source_target_pairs={{0,1},{1,0},{2,3},{3,2},{4,5},{5,4},{6,7},{7,6},{8,9},{9,8},{10,11... | collective-permute-start | bytes 3145736 | tf_op jit(solution)/shard_map/ppermute | solution.py:1012
  164.1 27.2 %all-to-all-start.2 = ((bf16[8,80,512]{2,1,0:T(8,128)(2,1)}), bf16[8,80,512]{2,1,0:T(8,128)(2,1)S(1)}, u32[]{:S(2)}, u32[]{:S(2)}) async-start(bf16[8,80,512]{2,1,0:T(8,128)(2,1)} %bitcast.215), calls=%async_computation.2 | async-start | bytes 1310720 | tf_op jit(solution)/shard_map/all_to_all | solution.py:441
  194.2 40.0 %all-to-all-start.3 = ((bf16[8,64,512]{2,1,0:T(8,128)(2,1)}), bf16[8,64,512]{2,1,0:T(8,128)(2,1)S(1)}, u32[]{:S(2)}, u32[]{:S(2)}) async-start(bf16[8,64,512]{2,1,0:T(8,128)(2,1)} %relay.4), calls=%async_computation.3 | async-start | bytes 1048576 | tf_op jit(solution)/shard_map/all_to_all | solution.py:452
  203.7 45.5 %collective-permute-start.17 = (bf16[1,512,1024]{2,1,0:T(8,128)(2,1)}, bf16[1,512,1024]{2,1,0:T(8,128)(2,1)}, u32[]{:S(2)}, u32[]{:S(2)}) collective-permute-start(bf16[1,512,1024]{2,1,0:T(8,128)(2,1)} %get-tuple-element.100.refs_4_), channel_id=1, source_target_pairs={{0,2},{1,3},{2,0},{3,1},{4,6},{5,7},{6,4},{7,5},{8,10},{9,11},{10,... | collective-permute-start | bytes 3145736 | tf_op jit(solution)/shard_map/ppermute | solution.py:1012
  204.3 46.5 %collective-permute-start.14 = (bf16[1,512,1024]{2,1,0:T(8,128)(2,1)}, bf16[1,512,1024]{2,1,0:T(8,128)(2,1)}, u32[]{:S(2)}, u32[]{:S(2)}) collective-permute-start(bf16[1,512,1024]{2,1,0:T(8,128)(2,1)} %get-tuple-element.97.refs_0_), channel_id=1, source_target_pairs={{0,2},{1,3},{2,0},{3,1},{4,6},{5,7},{6,4},{7,5},{8,10},{9,11},{10,... | collective-permute-start | bytes 3145736 | tf_op jit(solution)/shard_map/ppermute | solution.py:1012
  218.5 95.2 %collective-permute-start.50 = (bf16[2048,512]{1,0:T(8,128)(2,1)}, bf16[2048,512]{1,0:T(8,128)(2,1)}, u32[]{:S(2)}, u32[]{:S(2)}) collective-permute-start(bf16[2048,512]{1,0:T(8,128)(2,1)} %pad_maximum_fusion.4), channel_id=1, source_target_pairs={{0,1},{1,0},{2,3},{3,2},{4,5},{5,4},{6,7},{7,6},{8,9},{9,8},{10,11... | collective-permute-start | bytes 6291464 | tf_op jit(solution)/shard_map/ppermute | solution.py:1012
  234.2 41.9 %all-to-all-start.4 = ((bf16[8,80,512]{2,1,0:T(8,128)(2,1)}), bf16[8,80,512]{2,1,0:T(8,128)(2,1)}, u32[]{:S(2)}, u32[]{:S(2)}) async-start(bf16[8,80,512]{2,1,0:T(8,128)(2,1)} %bitcast.28), calls=%async_computation.4 | async-start | bytes 1310720 | tf_op jit(solution)/shard_map/all_to_all | solution.py:441
  248.6 38.6 %collective-permute-start.16 = (bf16[1,512,1024]{2,1,0:T(8,128)(2,1)}, bf16[1,512,1024]{2,1,0:T(8,128)(2,1)S(1)}, u32[]{:S(2)}, u32[]{:S(2)}) collective-permute-start(bf16[1,512,1024]{2,1,0:T(8,128)(2,1)} %get-tuple-element.100.refs_4_), channel_id=1, source_target_pairs={{0,1},{1,0},{2,3},{3,2},{4,5},{5,4},{6,7},{7,6},{8,9},{9,8},{10,11... | collective-permute-start | bytes 3145736 | tf_op jit(solution)/shard_map/ppermute | solution.py:1012
  248.9 38.6 %collective-permute-start.13 = (bf16[1,512,1024]{2,1,0:T(8,128)(2,1)}, bf16[1,512,1024]{2,1,0:T(8,128)(2,1)}, u32[]{:S(2)}, u32[]{:S(2)}) collective-permute-start(bf16[1,512,1024]{2,1,0:T(8,128)(2,1)} %get-tuple-element.97.refs_0_), channel_id=1, source_target_pairs={{0,1},{1,0},{2,3},{3,2},{4,5},{5,4},{6,7},{7,6},{8,9},{9,8},{10,11... | collective-permute-start | bytes 3145736 | tf_op jit(solution)/shard_map/ppermute | solution.py:1012
  249.2 38.2 %collective-permute-start.18 = (bf16[1,512,1024]{2,1,0:T(8,128)(2,1)}, bf16[1,512,1024]{2,1,0:T(8,128)(2,1)}, u32[]{:S(2)}, u32[]{:S(2)}) collective-permute-start(bf16[1,512,1024]{2,1,0:T(8,128)(2,1)} %collective-permute-done.17.refs_6_), channel_id=1, source_target_pairs={{0,1},{1,0},{2,3},{3,2},{4,5},{5,4},{6,7},{7,6},{8,9},{9,8},{10,11... | collective-permute-start | bytes 3145736 | tf_op jit(solution)/shard_map/ppermute | solution.py:1012
  250.7 36.7 %collective-permute-start.15 = (bf16[1,512,1024]{2,1,0:T(8,128)(2,1)}, bf16[1,512,1024]{2,1,0:T(8,128)(2,1)}, u32[]{:S(2)}, u32[]{:S(2)}) collective-permute-start(bf16[1,512,1024]{2,1,0:T(8,128)(2,1)} %collective-permute-done.14.refs_2_), channel_id=1, source_target_pairs={{0,1},{1,0},{2,3},{3,2},{4,5},{5,4},{6,7},{7,6},{8,9},{9,8},{10,11... | collective-permute-start | bytes 3145736 | tf_op jit(solution)/shard_map/ppermute | solution.py:1012
  278.2 38.9 %all-to-all-start.5 = ((bf16[8,64,512]{2,1,0:T(8,128)(2,1)}), bf16[8,64,512]{2,1,0:T(8,128)(2,1)S(1)}, u32[]{:S(2)}, u32[]{:S(2)}) async-start(bf16[8,64,512]{2,1,0:T(8,128)(2,1)} %relay.5), calls=%async_computation.5 | async-start | bytes 1048576 | tf_op jit(solution)/shard_map/all_to_all | solution.py:452
  287.2 110.2 %collective-permute-start.35 = (bf16[2048,512]{1,0:T(8,128)(2,1)}, bf16[2048,512]{1,0:T(8,128)(2,1)}, u32[]{:S(2)}, u32[]{:S(2)}) collective-permute-start(bf16[2048,512]{1,0:T(8,128)(2,1)} %pad_maximum_fusion.1), channel_id=1, source_target_pairs={{0,1},{1,0},{2,3},{3,2},{4,5},{5,4},{6,7},{7,6},{8,9},{9,8},{10,11... | collective-permute-start | bytes 6291464 | tf_op jit(solution)/shard_map/ppermute | solution.py:1012
  316.5 121.6 %collective-permute-start.51 = (bf16[1024,512]{1,0:T(8,128)(2,1)}, bf16[1024,512]{1,0:T(8,128)(2,1)}, u32[]{:S(2)}, u32[]{:S(2)}) collective-permute-start(bf16[1024,512]{1,0:T(8,128)(2,1)} %fusion.3), channel_id=1, source_target_pairs={{0,2},{1,3},{2,0},{3,1},{4,6},{5,7},{6,4},{7,5},{8,10},{9,11},{10,... | collective-permute-start | bytes 3145736 | tf_op jit(solution)/shard_map/ppermute | solution.py:1012
  341.9 94.6 %collective-permute-start.45 = (bf16[4,128,256]{2,1,0:T(8,128)(2,1)S(1)}, bf16[4,128,256]{2,1,0:T(8,128)(2,1)S(1)}, u32[]{:S(2)}, u32[]{:S(2)}) collective-permute-start(bf16[4,128,256]{2,1,0:T(8,128)(2,1)S(1)} %dynamic-slice_bitcast_fusion.7), channel_id=1, source_target_pairs={{0,4},{4,0},{8,12},{12,8},{16,20},{20,16},{24,28},{28,24},{1,5},{5... | collective-permute-start | bytes 786440 | tf_op jit(solution)/shard_map/ppermute | solution.py:1012
  357.6 96.3 %collective-permute-start.40 = (bf16[2048,512]{1,0:T(8,128)(2,1)}, bf16[2048,512]{1,0:T(8,128)(2,1)S(1)}, u32[]{:S(2)}, u32[]{:S(2)}) collective-permute-start(bf16[2048,512]{1,0:T(8,128)(2,1)} %pad_maximum_fusion.2), channel_id=1, source_target_pairs={{0,1},{1,0},{2,3},{3,2},{4,5},{5,4},{6,7},{7,6},{8,9},{9,8},{10,11... | collective-permute-start | bytes 6291464 | tf_op jit(solution)/shard_map/ppermute | solution.py:1012
  371.9 18.0 %collective-permute-start.26 = (bf16[1,16,1024]{2,1,0:T(8,128)(2,1)}, bf16[1,16,1024]{2,1,0:T(8,128)(2,1)S(1)}, u32[]{:S(2)}, u32[]{:S(2)}) collective-permute-start(bf16[1,16,1024]{2,1,0:T(8,128)(2,1)} %get-tuple-element.142), channel_id=1, source_target_pairs={{4,0},{8,4},{12,8},{16,12},{20,16},{24,20},{28,24},{5,1},{9,5},{13... | collective-permute-start | bytes 98312 | tf_op jit(solution)/shard_map/ppermute | solution.py:1231
  402.0 97.4 %collective-permute-start.23 = (bf16[1,512,1024]{2,1,0:T(8,128)(2,1)}, bf16[1,512,1024]{2,1,0:T(8,128)(2,1)}, u32[]{:S(2)}, u32[]{:S(2)}) collective-permute-start(bf16[1,512,1024]{2,1,0:T(8,128)(2,1)} %get-tuple-element.138.refs_4_), channel_id=1, source_target_pairs={{0,2},{1,3},{2,0},{3,1},{4,6},{5,7},{6,4},{7,5},{8,10},{9,11},{10,... | collective-permute-start | bytes 3145736 | tf_op jit(solution)/shard_map/ppermute | solution.py:1012
  405.3 23.4 %collective-permute-start.31 = (f32[30,512]{1,0:T(8,128)S(1)}, f32[30,512]{1,0:T(8,128)S(1)}, u32[]{:S(2)}, u32[]{:S(2)}) collective-permute-start(f32[30,512]{1,0:T(8,128)S(1)} %pad_maximum_fusion.8), channel_id=1, source_target_pairs={{0,2},{1,3},{2,0},{3,1},{4,6},{5,7},{6,4},{7,5},{8,10},{9,11},{10,... | collective-permute-start | bytes 184328 | tf_op jit(solution)/shard_map/ppermute | solution.py:1012
  435.3 29.8 %collective-permute-start.36 = (bf16[1024,512]{1,0:T(8,128)(2,1)}, bf16[1024,512]{1,0:T(8,128)(2,1)}, u32[]{:S(2)}, u32[]{:S(2)}) collective-permute-start(bf16[1024,512]{1,0:T(8,128)(2,1)} %fusion.8), channel_id=1, source_target_pairs={{0,2},{1,3},{2,0},{3,1},{4,6},{5,7},{6,4},{7,5},{8,10},{9,11},{10,... | collective-permute-start | bytes 3145736 | tf_op jit(solution)/shard_map/ppermute | solution.py:1012
  438.1 10.3 %collective-permute-start.46 = (bf16[2,128,256]{2,1,0:T(8,128)(2,1)S(1)}, bf16[2,128,256]{2,1,0:T(8,128)(2,1)S(1)}, u32[]{:S(2)}, u32[]{:S(2)}) collective-permute-start(bf16[2,128,256]{2,1,0:T(8,128)(2,1)S(1)} %dynamic-slice_bitcast_fusion.9), channel_id=1, source_target_pairs={{0,8},{4,12},{8,0},{12,4},{16,24},{20,28},{24,16},{28,20},{1,9},{5... | collective-permute-start | bytes 393224 | tf_op jit(solution)/shard_map/ppermute | solution.py:1012
  446.7 11.3 %collective-permute-start.52 = (bf16[4,128,512]{2,1,0:T(8,128)(2,1)}, bf16[4,128,512]{2,1,0:T(8,128)(2,1)}, u32[]{:S(2)}, u32[]{:S(2)}) collective-permute-start(bf16[4,128,512]{2,1,0:T(8,128)(2,1)} %dynamic-slice_bitcast_fusion.3), channel_id=1, source_target_pairs={{0,4},{4,0},{8,12},{12,8},{16,20},{20,16},{24,28},{28,24},{1,5},{5... | collective-permute-start | bytes 1572872 | tf_op jit(solution)/shard_map/ppermute | solution.py:1012
  456.4 25.6 %collective-permute-start.41 = (bf16[4,128,1024]{2,1,0:T(8,128)(2,1)S(1)}, bf16[4,128,1024]{2,1,0:T(8,128)(2,1)S(1)}, u32[]{:S(2)}, u32[]{:S(2)}) collective-permute-start(bf16[4,128,1024]{2,1,0:T(8,128)(2,1)S(1)} %dynamic-slice_bitcast_fusion.2), channel_id=1, source_target_pairs={{0,4},{4,0},{8,12},{12,8},{16,20},{20,16},{24,28},{28,24},{1,5},{5... | collective-permute-start | bytes 3145736 | tf_op jit(solution)/shard_map/ppermute | solution.py:1012
  457.5 72.7 %collective-permute-start.22 = (bf16[1,512,1024]{2,1,0:T(8,128)(2,1)}, bf16[1,512,1024]{2,1,0:T(8,128)(2,1)S(1)}, u32[]{:S(2)}, u32[]{:S(2)}) collective-permute-start(bf16[1,512,1024]{2,1,0:T(8,128)(2,1)} %get-tuple-element.138.refs_4_), channel_id=1, source_target_pairs={{0,1},{1,0},{2,3},{3,2},{4,5},{5,4},{6,7},{7,6},{8,9},{9,8},{10,11... | collective-permute-start | bytes 3145736 | tf_op jit(solution)/shard_map/ppermute | solution.py:1012
  463.5 35.9 %collective-permute-start.20 = (bf16[1,512,1024]{2,1,0:T(8,128)(2,1)S(1)}, bf16[1,512,1024]{2,1,0:T(8,128)(2,1)}, u32[]{:S(2)}, u32[]{:S(2)}) collective-permute-start(bf16[1,512,1024]{2,1,0:T(8,128)(2,1)S(1)} %copy-done.12), channel_id=1, source_target_pairs={{0,2},{1,3},{2,0},{3,1},{4,6},{5,7},{6,4},{7,5},{8,10},{9,11},{10,... | collective-permute-start | bytes 3145736 | tf_op jit(solution)/shard_map/ppermute | solution.py:1012
  465.1 17.8 %collective-permute-start.53 = (bf16[2,128,512]{2,1,0:T(8,128)(2,1)S(1)}, bf16[2,128,512]{2,1,0:T(8,128)(2,1)S(1)}, u32[]{:S(2)}, u32[]{:S(2)}) collective-permute-start(bf16[2,128,512]{2,1,0:T(8,128)(2,1)S(1)} %dynamic-slice_bitcast_fusion.6), channel_id=1, source_target_pairs={{0,8},{4,12},{8,0},{12,4},{16,24},{20,28},{24,16},{28,20},{1,9},{5... | collective-permute-start | bytes 786440 | tf_op jit(solution)/shard_map/ppermute | solution.py:1012
  482.0 13.6 %collective-permute-start.37 = (bf16[4,128,512]{2,1,0:T(8,128)(2,1)S(1)}, bf16[4,128,512]{2,1,0:T(8,128)(2,1)S(1)}, u32[]{:S(2)}, u32[]{:S(2)}) collective-permute-start(bf16[4,128,512]{2,1,0:T(8,128)(2,1)S(1)} %dynamic-slice_bitcast_fusion.5), channel_id=1, source_target_pairs={{0,4},{4,0},{8,12},{12,8},{16,20},{20,16},{24,28},{28,24},{1,5},{5... | collective-permute-start | bytes 1572872 | tf_op jit(solution)/shard_map/ppermute | solution.py:1012
  482.9 15.0 %collective-permute-start.42 = (bf16[2,128,1024]{2,1,0:T(8,128)(2,1)S(1)}, bf16[2,128,1024]{2,1,0:T(8,128)(2,1)S(1)}, u32[]{:S(2)}, u32[]{:S(2)}) collective-permute-start(bf16[2,128,1024]{2,1,0:T(8,128)(2,1)S(1)} %dynamic-slice_bitcast_fusion.4), channel_id=1, source_target_pairs={{0,8},{4,12},{8,0},{12,4},{16,24},{20,28},{24,16},{28,20},{1,9},{5... | collective-permute-start | bytes 1572872 | tf_op jit(solution)/shard_map/ppermute | solution.py:1012
  497.9 9.0 %collective-permute-start.38 = (bf16[2,128,512]{2,1,0:T(8,128)(2,1)S(1)}, bf16[2,128,512]{2,1,0:T(8,128)(2,1)S(1)}, u32[]{:S(2)}, u32[]{:S(2)}) collective-permute-start(bf16[2,128,512]{2,1,0:T(8,128)(2,1)S(1)} %dynamic-slice_bitcast_fusion.8), channel_id=1, source_target_pairs={{0,8},{4,12},{8,0},{12,4},{16,24},{20,28},{24,16},{28,20},{1,9},{5... | collective-permute-start | bytes 786440 | tf_op jit(solution)/shard_map/ppermute | solution.py:1012
  499.4 30.8 %collective-permute-start.19 = (bf16[1,512,1024]{2,1,0:T(8,128)(2,1)S(1)}, bf16[1,512,1024]{2,1,0:T(8,128)(2,1)}, u32[]{:S(2)}, u32[]{:S(2)}) collective-permute-start(bf16[1,512,1024]{2,1,0:T(8,128)(2,1)S(1)} %copy-done.12), channel_id=1, source_target_pairs={{0,1},{1,0},{2,3},{3,2},{4,5},{5,4},{6,7},{7,6},{8,9},{9,8},{10,11... | collective-permute-start | bytes 3145736 | tf_op jit(solution)/shard_map/ppermute | solution.py:1012
  499.5 30.7 %collective-permute-start.24 = (bf16[1,512,1024]{2,1,0:T(8,128)(2,1)}, bf16[1,512,1024]{2,1,0:T(8,128)(2,1)}, u32[]{:S(2)}, u32[]{:S(2)}) collective-permute-start(bf16[1,512,1024]{2,1,0:T(8,128)(2,1)} %collective-permute-done.23.refs_6_), channel_id=1, source_target_pairs={{0,1},{1,0},{2,3},{3,2},{4,5},{5,4},{6,7},{7,6},{8,9},{9,8},{10,11... | collective-permute-start | bytes 3145736 | tf_op jit(solution)/shard_map/ppermute | solution.py:1012
  503.7 26.5 %collective-permute-start.21 = (bf16[1,512,1024]{2,1,0:T(8,128)(2,1)}, bf16[1,512,1024]{2,1,0:T(8,128)(2,1)}, u32[]{:S(2)}, u32[]{:S(2)}) collective-permute-start(bf16[1,512,1024]{2,1,0:T(8,128)(2,1)} %collective-permute-done.20.refs_2_), channel_id=1, source_target_pairs={{0,1},{1,0},{2,3},{3,2},{4,5},{5,4},{6,7},{7,6},{8,9},{9,8},{10,11... | collective-permute-start | bytes 3145736 | tf_op jit(solution)/shard_map/ppermute | solution.py:1012
  506.9 13.4 %collective-permute-start.43 = (bf16[1,128,1024]{2,1,0:T(8,128)(2,1)S(1)}, bf16[1,128,1024]{2,1,0:T(8,128)(2,1)S(1)}, u32[]{:S(2)}, u32[]{:S(2)}) collective-permute-start(bf16[1,128,1024]{2,1,0:T(8,128)(2,1)S(1)} %constant_dynamic-slice_fusion.3), channel_id=1, source_target_pairs={{0,16},{4,20},{8,24},{12,28},{16,0},{20,4},{24,8},{28,12},{1,17},{... | collective-permute-start | bytes 786440 | tf_op jit(solution)/shard_map/ppermute | solution.py:1012
  528.4 10.8 %collective-permute-start.44 = (f32[128,512]{1,0:T(8,128)}, f32[128,512]{1,0:T(8,128)}, u32[]{:S(2)}, u32[]{:S(2)}) collective-permute-start(f32[128,512]{1,0:T(8,128)} %slice.400), channel_id=1, source_target_pairs={{0,2},{1,3},{2,0},{3,1},{4,6},{5,7},{6,4},{7,5},{8,10},{9,11},{10,... | collective-permute-start | bytes 786440 | tf_op jit(solution)/shard_map/ppermute | solution.py:1012
  (50 other events, 480.1 us)
